TPU v7x, 32 devices: a whole 2x2x4 slice. The times are simulated.
32 devices in a mesh: grp: 1, row: 8 (over z, core), col: 4 (over y, x).
Axes of the slice: x: 2, y: 2, z: 4, core: 2. Of those that a mesh axis runs over, the one named last changes fastest.
Arguments:
- ocean_field: bfloat16 [64, 128, 128, 128], P('grp', 'row', 'col'), may hold values from -6 to 6
- spec_first: bfloat16 [2, 32, 64, 64], replicated, may hold values from -0.5 to 0.5
- spec_second: bfloat16 [2, 32, 64, 64], replicated, may hold values from -0.5 to 0.5
- spec_third: bfloat16 [2, 32, 64, 64], replicated, may hold values from -0.5 to 0.5
- ffn_in: bfloat16 [64, 256], replicated, may hold values from -0.75 to 0.75
- ffn_out: bfloat16 [256, 64], replicated, may hold values from -0.375 to 0.375
- bias_in: float32 [256], replicated, may hold values from -3 to 3
- bias_out: float32 [64], replicated, may hold values from -3 to 3
Outputs:
- next_field: bfloat16 [64, 128, 128, 128], P('grp', 'row', 'col')
All inputs are finite; a program needn't handle non-finite values.
Results may differ from a plain program's by a relative error of at most 0.013.
Values may be sent and summed in bfloat16 or wider, within the bound.
No kernel may reach another device: no remote copies, remote signals or barrier semaphores. Data moves between devices by JAX's collectives and lax.ppermute only.
A program may use at most 192 MiB of HBM per device.

v0:
```python
import math

import jax
import jax.numpy as jnp
from jax import lax
from jax.sharding import PartitionSpec as P


def forward_table(length, mode_count):
    grid_pos = jnp.arange(length, dtype=jnp.int32)[:, None]
    mode_location = jnp.arange(mode_count, dtype=jnp.int32)[None, :]
    phase = (grid_pos * mode_location % length).astype(jnp.float32) * (2.0 * math.pi / length)
    return jnp.stack([jnp.cos(phase), -jnp.sin(phase)], axis=1).astype(jnp.bfloat16)


def inverse_table(length, mode_count):
    mode_location = jnp.arange(mode_count, dtype=jnp.int32)[:, None]
    grid_pos = jnp.arange(length, dtype=jnp.int32)[None, :]
    phase = (grid_pos * mode_location % length).astype(jnp.float32) * (2.0 * math.pi / length)
    factor = jnp.where(mode_location == 0, 1.0, 2.0).astype(jnp.float32) / length
    return jnp.stack([factor * jnp.cos(phase), -factor * jnp.sin(phase)], axis=0).astype(
        jnp.bfloat16
    )


def block_weight_tensor(weight_tensor):
    real_part = weight_tensor[0]
    imag_part = weight_tensor[1]
    upper = jnp.concatenate([real_part, imag_part], axis=2)
    lower = jnp.concatenate([-imag_part, real_part], axis=2)
    return jnp.concatenate([upper, lower], axis=1)


def along_axis(values, weight_tensor):
    channels, across, length, columns = values.shape
    mode_count = weight_tensor.shape[1]
    spectral_coefficients = jnp.einsum(
        "canq,nsm->mscaq",
        values,
        forward_table(length, mode_count),
        preferred_element_type=jnp.float32,
    )
    spectral_coefficients = spectral_coefficients.reshape(
        mode_count, 2 * channels, across * columns
    ).astype(jnp.bfloat16)
    mixed_result = jnp.einsum(
        "plf,plk->pkf",
        spectral_coefficients,
        block_weight_tensor(weight_tensor),
        preferred_element_type=jnp.float32,
    )
    mixed_result = mixed_result.astype(jnp.bfloat16).reshape(
        mode_count, 2, channels, across, columns
    )
    result = jnp.einsum(
        "mscaq,smn->canq",
        mixed_result,
        inverse_table(length, mode_count),
        preferred_element_type=jnp.float32,
    )
    return result.astype(jnp.bfloat16)


def final_axis_transform(values, weight_tensor):
    channels, places, length = values.shape
    mode_count = weight_tensor.shape[1]
    spectral_coefficients = jnp.einsum(
        "cpn,nsm->mscp",
        values,
        forward_table(length, mode_count),
        preferred_element_type=jnp.float32,
    )
    spectral_coefficients = spectral_coefficients.reshape(mode_count, 2 * channels, places).astype(
        jnp.bfloat16
    )
    mixed_result = jnp.einsum(
        "plf,plk->pkf",
        spectral_coefficients,
        block_weight_tensor(weight_tensor),
        preferred_element_type=jnp.float32,
    )
    mixed_result = mixed_result.astype(jnp.bfloat16).reshape(mode_count, 2, channels, places)
    result = jnp.einsum(
        "mscp,smn->cpn",
        mixed_result,
        inverse_table(length, mode_count),
        preferred_element_type=jnp.float32,
    )
    return result.astype(jnp.bfloat16)


def feed_forward(summed, initial, ffn_in, ffn_out, bias_in, bias_out):

    def update(position, output):
        row_index = jnp.asarray(position).astype(jnp.int32)
        block = lax.dynamic_index_in_dim(summed, row_index, 1, keepdims=False)
        base = lax.dynamic_index_in_dim(initial, row_index, 1, keepdims=False)
        hidden_pre = (
            jnp.einsum("ch,ck->hk", ffn_in, block, preferred_element_type=jnp.float32)
            + bias_in[:, None]
        )
        hidden = jax.nn.gelu(hidden_pre, approximate=False).astype(jnp.bfloat16)
        result = jnp.einsum("hc,hk->ck", ffn_out, hidden, preferred_element_type=jnp.float32)
        result = result + bias_out[:, None] + base.astype(jnp.float32)
        return lax.dynamic_update_index_in_dim(output, result.astype(jnp.bfloat16), row_index, 1)

    return lax.fori_loop(0, summed.shape[1], update, jnp.zeros_like(initial))


def body(ocean_field, spec_first, spec_second, spec_third, ffn_in, ffn_out, bias_in, bias_out):
    channels, row_cells, col_cells, line_cells = ocean_field.shape
    third_part = final_axis_transform(
        ocean_field.reshape(channels, row_cells * col_cells, line_cells), spec_third
    )
    third_part = third_part.reshape(ocean_field.shape)
    piece = lax.all_to_all(ocean_field, "row", split_axis=2, concat_axis=1, tiled=True)
    depth_a, full_rows, across, items = piece.shape
    lines = along_axis(piece.reshape(depth_a, 1, full_rows, across * items), spec_first)
    lines = lines.reshape(piece.shape)
    first_part = lax.all_to_all(lines, "row", split_axis=1, concat_axis=2, tiled=True)
    lines = along_axis(
        lax.all_to_all(ocean_field, "col", split_axis=1, concat_axis=2, tiled=True), spec_second
    )
    second_part = lax.all_to_all(lines, "col", split_axis=2, concat_axis=1, tiled=True)
    pair = (first_part.astype(jnp.float32) + second_part.astype(jnp.float32)).astype(jnp.bfloat16)
    summed = (pair.astype(jnp.float32) + third_part.astype(jnp.float32)).astype(jnp.bfloat16)
    flat_sum = summed.reshape(channels, row_cells, col_cells * line_cells)
    flat_field = ocean_field.reshape(channels, row_cells, col_cells * line_cells)
    result = feed_forward(flat_sum, flat_field, ffn_in, ffn_out, bias_in, bias_out)
    return result.reshape(ocean_field.shape)


def solution(mesh):
    return jax.shard_map(
        body,
        mesh=mesh,
        in_specs=(P("grp", "row", "col", None), P(), P(), P(), P(), P(), P(), P()),
        out_specs=P("grp", "row", "col", None),
        check_vma=False,
    )
```

profile of v0, /device:TPU:0, one launch (start us, length us, event | category | flops | bytes accessed | tf_op | source)
XLA Modules:
  0.0 852.9 jit_solution(11026743847898403180)
XLA Ops:
  24.5 83.8 %all-to-all-done.2 = bf16[64,16,32,128]{3,2,0,1:T(8,128)(2,1)} async-done(((bf16[64,16,32,128]{3,2,0,1:T(8,128)(2,1)}), bf16[64,16,32,128]{3,2,0,1:T(8,128)(2,1)}, u32[]{:S(2)}, u32[]{:S(2)}) %all-to-all-start.2) | async-done | bytes 8388640 | tf_op jit(solution)/shard_map/all_to_all | solution.py:122
  158.2 18.9 %copy.59 = bf16[64,4,128,128]{3,1,0,2:T(4,128)(2,1)} copy(bf16[64,4,128,128]{3,2,1,0:T(8,128)(2,1)S(1)} %fusion.93) | data formatting | bytes 16777216 | tf_op jit(solution)/shard_map/convert_element_type | solution.py:61
  177.2 120.5 %all-to-all-done = bf16[64,16,32,128]{3,1,0,2:T(8,128)(2,1)} async-done(((bf16[64,16,32,128]{3,1,0,2:T(8,128)(2,1)}), bf16[64,16,32,128]{3,1,0,2:T(8,128)(2,1)}, u32[]{:S(2)}, u32[]{:S(2)}) %all-to-all-start) | async-done | bytes 8388640 | tf_op jit(solution)/shard_map/all_to_all | solution.py:116
  304.0 18.0 %copy.101 = bf16[64,16,8,4,128]{4,3,1,2,0:T(4,128)(2,1)} copy(bf16[64,16,8,4,128]{4,1,0,3,2:T(8,128)(2,1)} %bitcast.11) | data formatting | bytes 16777216 | tf_op jit(solution)/shard_map/all_to_all | solution.py:116
  322.0 13.1 %reshape.266 = bf16[64,128,512,1]{2,1,0,3:T(8,128)(2,1)} reshape(bf16[64,8,16,4,128]{4,3,2,1,0:T(4,128)(2,1)} %bitcast.214) | data formatting | bytes 16777216 | tf_op jit(solution)/shard_map/reshape.1
  355.2 12.5 %reshape.253 = bf16[64,128,4,128]{3,2,1,0:T(4,128)(2,1)} reshape(bf16[64,1,128,512]{3,2,0,1:T(8,128)(2,1)} %fusion.92) | data formatting | bytes 16777216 | tf_op jit(solution)/shard_map/reshape | solution.py:119
  376.3 19.5 %all-to-all-done.3 = bf16[64,4,128,128]{3,1,0,2:T(4,128)(2,1)} async-done(((bf16[64,4,128,128]{3,1,0,2:T(4,128)(2,1)}), bf16[64,4,128,128]{3,1,0,2:T(4,128)(2,1)}, u32[]{:S(2)}, u32[]{:S(2)}) %all-to-all-start.3) | async-done | bytes 8388640 | tf_op jit(solution)/shard_map/all_to_all | solution.py:124
  400.9 13.4 %reshape.276 = bf16[64,16,4096]{2,1,0:T(8,128)(2,1)} reshape(bf16[64,16,32,128]{3,2,1,0:T(8,128)(2,1)} %param.10) | data formatting | bytes 16777216 | tf_op jit(solution)/shard_map/reshape | solution.py:128
  434.6 18.2 %reshape.262 = f32[64,16,4096]{2,1,0:T(8,128)} reshape(f32[64,512,128]{2,1,0:T(8,128)} %fusion.91) | data formatting | bytes 33554432 | tf_op jit(solution)/shard_map/convert_element_type | solution.py:126
  452.8 11.2 %copy.74 = bf16[64,16,4096]{2,0,1:T(8,128)(2,1)} copy(bf16[64,16,4096]{2,1,0:T(8,128)(2,1)} %reshape.276) | data formatting | bytes 16777216 | tf_op jit(solution)/shard_map/reshape | solution.py:128
  469.1 11.7 %copy.60 = f32[64,4,4,32,128]{4,3,0,2,1:T(8,128)} copy(f32[64,4,4,32,128]{4,2,0,3,1:T(4,128)S(1)} %convert_bitcast_fusion) | data formatting | bytes 33554432 | tf_op jit(solution)/shard_map/convert_element_type | solution.py:125
  480.8 18.2 %reshape.261 = f32[64,16,4096]{2,0,1:T(8,128)} reshape(f32[64,4,4,32,128]{4,3,0,2,1:T(8,128)} %copy.60) | data formatting | bytes 33554432 | tf_op jit(solution)/shard_map/convert_element_type | solution.py:125
  499.0 85.7 %all-to-all-done.1 = bf16[64,128,4,128]{3,2,0,1:T(4,128)(2,1)} async-done(((bf16[64,128,4,128]{3,2,0,1:T(4,128)(2,1)}), bf16[64,128,4,128]{3,2,0,1:T(4,128)(2,1)}, u32[]{:S(2)}, u32[]{:S(2)}) %all-to-all-start.1) | async-done | bytes 8388640 | tf_op jit(solution)/shard_map/all_to_all | solution.py:120
  598.0 20.0 %reshape.260 = f32[64,16,4096]{2,0,1:T(8,128)} reshape(f32[64,16,8,4,128]{4,3,2,0,1:T(4,128)} %copy.52) | data formatting | bytes 33554432 | tf_op jit(solution)/shard_map/convert_element_type | solution.py:125
  618.0 22.5 %fusion.90 = bf16[64,16,4096]{2,0,1:T(8,128)(2,1)} fusion(f32[64,16,4096]{2,1,0:T(8,128)} %reshape.262, f32[64,16,4096]{2,0,1:T(8,128)} %reshape.260, f32[64,16,4096]{2,0,1:T(8,128)} %reshape.261), kind=kLoop, calls=%fused_computation.100 | loop fusion | flops 20971520 | bytes 58720256 | tf_op jit(solution)/shard_map/convert_element_type | solution.py:126
  640.5 193.1 %while.13 = (s32[]{:T(128)}, bf16[64,16,4096]{2,0,1:T(8,128)(2,1)}, bf16[64,16,4096]{2,0,1:T(8,128)(2,1)}, bf16[64,256]{1,0:T(8,128)(2,1)S(1)}, f32[256]{0:T(256...) while((s32[]{:T(128)}, bf16[64,16,4096]{2,0,1:T(8,128)(2,1)}, ...), condition=%wide.region_1.2_spmd, body=%wide.region_0.1_spmd.sunk | while | flops 338690048 | bytes 1640797 | solution.py:107
  640.7 12.0 %fusion.175 = bf16[64,16,4096]{2,0,1:T(8,128)(2,1)} fusion(bf16[64,16,4096]{2,0,1:T(8,128)(2,1)} %get-tuple-element.230, s32[]{:T(128)} %get-tuple-element.229, bf16[256,64]{0,1:T(8,128)(2,1)S(1)} %get-tuple-element.243, bf16[64,256]{1,0:T(8,128)(2,1)S(1)} %get-tuple-element.241, f32[256]{0:T(256)S(1)} %get-tuple-element.242, ...), kind=kOutput, calls=%fused_computation.7.clone.1 | convolution fusion | flops 338690048 | bytes 1640704 | tf_op jit(solution)/shard_map/while/body/eval_jaxpr/hc,hk->ck/dot_general | solution.py:103
  652.8 12.0 %fusion.175 = bf16[64,16,4096]{2,0,1:T(8,128)(2,1)} fusion(bf16[64,16,4096]{2,0,1:T(8,128)(2,1)} %get-tuple-element.230, s32[]{:T(128)} %get-tuple-element.229, bf16[256,64]{0,1:T(8,128)(2,1)S(1)} %get-tuple-element.243, bf16[64,256]{1,0:T(8,128)(2,1)S(1)} %get-tuple-element.241, f32[256]{0:T(256)S(1)} %get-tuple-element.242, ...), kind=kOutput, calls=%fused_computation.7.clone.1 | convolution fusion | flops 338690048 | bytes 1640704 | tf_op jit(solution)/shard_map/while/body/eval_jaxpr/hc,hk->ck/dot_general | solution.py:103
  664.8 12.0 %fusion.175 = bf16[64,16,4096]{2,0,1:T(8,128)(2,1)} fusion(bf16[64,16,4096]{2,0,1:T(8,128)(2,1)} %get-tuple-element.230, s32[]{:T(128)} %get-tuple-element.229, bf16[256,64]{0,1:T(8,128)(2,1)S(1)} %get-tuple-element.243, bf16[64,256]{1,0:T(8,128)(2,1)S(1)} %get-tuple-element.241, f32[256]{0:T(256)S(1)} %get-tuple-element.242, ...), kind=kOutput, calls=%fused_computation.7.clone.1 | convolution fusion | flops 338690048 | bytes 1640704 | tf_op jit(solution)/shard_map/while/body/eval_jaxpr/hc,hk->ck/dot_general | solution.py:103
  676.9 12.0 %fusion.175 = bf16[64,16,4096]{2,0,1:T(8,128)(2,1)} fusion(bf16[64,16,4096]{2,0,1:T(8,128)(2,1)} %get-tuple-element.230, s32[]{:T(128)} %get-tuple-element.229, bf16[256,64]{0,1:T(8,128)(2,1)S(1)} %get-tuple-element.243, bf16[64,256]{1,0:T(8,128)(2,1)S(1)} %get-tuple-element.241, f32[256]{0:T(256)S(1)} %get-tuple-element.242, ...), kind=kOutput, calls=%fused_computation.7.clone.1 | convolution fusion | flops 338690048 | bytes 1640704 | tf_op jit(solution)/shard_map/while/body/eval_jaxpr/hc,hk->ck/dot_general | solution.py:103
  688.9 12.0 %fusion.175 = bf16[64,16,4096]{2,0,1:T(8,128)(2,1)} fusion(bf16[64,16,4096]{2,0,1:T(8,128)(2,1)} %get-tuple-element.230, s32[]{:T(128)} %get-tuple-element.229, bf16[256,64]{0,1:T(8,128)(2,1)S(1)} %get-tuple-element.243, bf16[64,256]{1,0:T(8,128)(2,1)S(1)} %get-tuple-element.241, f32[256]{0:T(256)S(1)} %get-tuple-element.242, ...), kind=kOutput, calls=%fused_computation.7.clone.1 | convolution fusion | flops 338690048 | bytes 1640704 | tf_op jit(solution)/shard_map/while/body/eval_jaxpr/hc,hk->ck/dot_general | solution.py:103
  700.9 12.0 %fusion.175 = bf16[64,16,4096]{2,0,1:T(8,128)(2,1)} fusion(bf16[64,16,4096]{2,0,1:T(8,128)(2,1)} %get-tuple-element.230, s32[]{:T(128)} %get-tuple-element.229, bf16[256,64]{0,1:T(8,128)(2,1)S(1)} %get-tuple-element.243, bf16[64,256]{1,0:T(8,128)(2,1)S(1)} %get-tuple-element.241, f32[256]{0:T(256)S(1)} %get-tuple-element.242, ...), kind=kOutput, calls=%fused_computation.7.clone.1 | convolution fusion | flops 338690048 | bytes 1640704 | tf_op jit(solution)/shard_map/while/body/eval_jaxpr/hc,hk->ck/dot_general | solution.py:103
  713.0 12.0 %fusion.175 = bf16[64,16,4096]{2,0,1:T(8,128)(2,1)} fusion(bf16[64,16,4096]{2,0,1:T(8,128)(2,1)} %get-tuple-element.230, s32[]{:T(128)} %get-tuple-element.229, bf16[256,64]{0,1:T(8,128)(2,1)S(1)} %get-tuple-element.243, bf16[64,256]{1,0:T(8,128)(2,1)S(1)} %get-tuple-element.241, f32[256]{0:T(256)S(1)} %get-tuple-element.242, ...), kind=kOutput, calls=%fused_computation.7.clone.1 | convolution fusion | flops 338690048 | bytes 1640704 | tf_op jit(solution)/shard_map/while/body/eval_jaxpr/hc,hk->ck/dot_general | solution.py:103
  725.0 12.0 %fusion.175 = bf16[64,16,4096]{2,0,1:T(8,128)(2,1)} fusion(bf16[64,16,4096]{2,0,1:T(8,128)(2,1)} %get-tuple-element.230, s32[]{:T(128)} %get-tuple-element.229, bf16[256,64]{0,1:T(8,128)(2,1)S(1)} %get-tuple-element.243, bf16[64,256]{1,0:T(8,128)(2,1)S(1)} %get-tuple-element.241, f32[256]{0:T(256)S(1)} %get-tuple-element.242, ...), kind=kOutput, calls=%fused_computation.7.clone.1 | convolution fusion | flops 338690048 | bytes 1640704 | tf_op jit(solution)/shard_map/while/body/eval_jaxpr/hc,hk->ck/dot_general | solution.py:103
  737.0 12.0 %fusion.175 = bf16[64,16,4096]{2,0,1:T(8,128)(2,1)} fusion(bf16[64,16,4096]{2,0,1:T(8,128)(2,1)} %get-tuple-element.230, s32[]{:T(128)} %get-tuple-element.229, bf16[256,64]{0,1:T(8,128)(2,1)S(1)} %get-tuple-element.243, bf16[64,256]{1,0:T(8,128)(2,1)S(1)} %get-tuple-element.241, f32[256]{0:T(256)S(1)} %get-tuple-element.242, ...), kind=kOutput, calls=%fused_computation.7.clone.1 | convolution fusion | flops 338690048 | bytes 1640704 | tf_op jit(solution)/shard_map/while/body/eval_jaxpr/hc,hk->ck/dot_general | solution.py:103
  749.1 12.0 %fusion.175 = bf16[64,16,4096]{2,0,1:T(8,128)(2,1)} fusion(bf16[64,16,4096]{2,0,1:T(8,128)(2,1)} %get-tuple-element.230, s32[]{:T(128)} %get-tuple-element.229, bf16[256,64]{0,1:T(8,128)(2,1)S(1)} %get-tuple-element.243, bf16[64,256]{1,0:T(8,128)(2,1)S(1)} %get-tuple-element.241, f32[256]{0:T(256)S(1)} %get-tuple-element.242, ...), kind=kOutput, calls=%fused_computation.7.clone.1 | convolution fusion | flops 338690048 | bytes 1640704 | tf_op jit(solution)/shard_map/while/body/eval_jaxpr/hc,hk->ck/dot_general | solution.py:103
  761.1 12.0 %fusion.175 = bf16[64,16,4096]{2,0,1:T(8,128)(2,1)} fusion(bf16[64,16,4096]{2,0,1:T(8,128)(2,1)} %get-tuple-element.230, s32[]{:T(128)} %get-tuple-element.229, bf16[256,64]{0,1:T(8,128)(2,1)S(1)} %get-tuple-element.243, bf16[64,256]{1,0:T(8,128)(2,1)S(1)} %get-tuple-element.241, f32[256]{0:T(256)S(1)} %get-tuple-element.242, ...), kind=kOutput, calls=%fused_computation.7.clone.1 | convolution fusion | flops 338690048 | bytes 1640704 | tf_op jit(solution)/shard_map/while/body/eval_jaxpr/hc,hk->ck/dot_general | solution.py:103
  773.1 12.0 %fusion.175 = bf16[64,16,4096]{2,0,1:T(8,128)(2,1)} fusion(bf16[64,16,4096]{2,0,1:T(8,128)(2,1)} %get-tuple-element.230, s32[]{:T(128)} %get-tuple-element.229, bf16[256,64]{0,1:T(8,128)(2,1)S(1)} %get-tuple-element.243, bf16[64,256]{1,0:T(8,128)(2,1)S(1)} %get-tuple-element.241, f32[256]{0:T(256)S(1)} %get-tuple-element.242, ...), kind=kOutput, calls=%fused_computation.7.clone.1 | convolution fusion | flops 338690048 | bytes 1640704 | tf_op jit(solution)/shard_map/while/body/eval_jaxpr/hc,hk->ck/dot_general | solution.py:103
  785.2 12.0 %fusion.175 = bf16[64,16,4096]{2,0,1:T(8,128)(2,1)} fusion(bf16[64,16,4096]{2,0,1:T(8,128)(2,1)} %get-tuple-element.230, s32[]{:T(128)} %get-tuple-element.229, bf16[256,64]{0,1:T(8,128)(2,1)S(1)} %get-tuple-element.243, bf16[64,256]{1,0:T(8,128)(2,1)S(1)} %get-tuple-element.241, f32[256]{0:T(256)S(1)} %get-tuple-element.242, ...), kind=kOutput, calls=%fused_computation.7.clone.1 | convolution fusion | flops 338690048 | bytes 1640704 | tf_op jit(solution)/shard_map/while/body/eval_jaxpr/hc,hk->ck/dot_general | solution.py:103
  797.2 12.0 %fusion.175 = bf16[64,16,4096]{2,0,1:T(8,128)(2,1)} fusion(bf16[64,16,4096]{2,0,1:T(8,128)(2,1)} %get-tuple-element.230, s32[]{:T(128)} %get-tuple-element.229, bf16[256,64]{0,1:T(8,128)(2,1)S(1)} %get-tuple-element.243, bf16[64,256]{1,0:T(8,128)(2,1)S(1)} %get-tuple-element.241, f32[256]{0:T(256)S(1)} %get-tuple-element.242, ...), kind=kOutput, calls=%fused_computation.7.clone.1 | convolution fusion | flops 338690048 | bytes 1640704 | tf_op jit(solution)/shard_map/while/body/eval_jaxpr/hc,hk->ck/dot_general | solution.py:103
  809.2 12.0 %fusion.175 = bf16[64,16,4096]{2,0,1:T(8,128)(2,1)} fusion(bf16[64,16,4096]{2,0,1:T(8,128)(2,1)} %get-tuple-element.230, s32[]{:T(128)} %get-tuple-element.229, bf16[256,64]{0,1:T(8,128)(2,1)S(1)} %get-tuple-element.243, bf16[64,256]{1,0:T(8,128)(2,1)S(1)} %get-tuple-element.241, f32[256]{0:T(256)S(1)} %get-tuple-element.242, ...), kind=kOutput, calls=%fused_computation.7.clone.1 | convolution fusion | flops 338690048 | bytes 1640704 | tf_op jit(solution)/shard_map/while/body/eval_jaxpr/hc,hk->ck/dot_general | solution.py:103
  821.3 12.0 %fusion.175 = bf16[64,16,4096]{2,0,1:T(8,128)(2,1)} fusion(bf16[64,16,4096]{2,0,1:T(8,128)(2,1)} %get-tuple-element.230, s32[]{:T(128)} %get-tuple-element.229, bf16[256,64]{0,1:T(8,128)(2,1)S(1)} %get-tuple-element.243, bf16[64,256]{1,0:T(8,128)(2,1)S(1)} %get-tuple-element.241, f32[256]{0:T(256)S(1)} %get-tuple-element.242, ...), kind=kOutput, calls=%fused_computation.7.clone.1 | convolution fusion | flops 338690048 | bytes 1640704 | tf_op jit(solution)/shard_map/while/body/eval_jaxpr/hc,hk->ck/dot_general | solution.py:103
  (56 shorter events, 171.9 us)
Async XLA Ops:
  8.8 99.5 %all-to-all-start.2 = ((bf16[64,16,32,128]{3,2,0,1:T(8,128)(2,1)}), bf16[64,16,32,128]{3,2,0,1:T(8,128)(2,1)}, u32[]{:S(2)}, u32[]{:S(2)}) async-start(bf16[64,16,32,128]{3,2,0,1:T(8,128)(2,1)} %copy.55), calls=%async_computation.2 | async-start | bytes 16777216 | tf_op jit(solution)/shard_map/all_to_all | solution.py:122
  24.5 89.2 %copy-start = (bf16[2,32,64,64]{3,2,1,0:T(8,128)(2,1)S(1)}, bf16[2,32,64,64]{3,2,1,0:T(8,128)(2,1)}, u32[]{:S(2)}) copy-start(bf16[2,32,64,64]{3,2,1,0:T(8,128)(2,1)} %param.12) | copy-start | bytes 1572868
  108.3 189.4 %all-to-all-start = ((bf16[64,16,32,128]{3,1,0,2:T(8,128)(2,1)}), bf16[64,16,32,128]{3,1,0,2:T(8,128)(2,1)}, u32[]{:S(2)}, u32[]{:S(2)}) async-start(bf16[64,16,32,128]{3,1,0,2:T(8,128)(2,1)} %copy.47), calls=%async_computation | async-start | bytes 16777216 | tf_op jit(solution)/shard_map/all_to_all | solution.py:116
  177.2 126.1 %copy-start.1 = (bf16[2,32,64,64]{3,2,1,0:T(8,128)(2,1)S(1)}, bf16[2,32,64,64]{3,2,1,0:T(8,128)(2,1)}, u32[]{:S(2)}) copy-start(bf16[2,32,64,64]{3,2,1,0:T(8,128)(2,1)} %param.11) | copy-start | bytes 1572868
  297.7 98.1 %all-to-all-start.3 = ((bf16[64,4,128,128]{3,1,0,2:T(4,128)(2,1)}), bf16[64,4,128,128]{3,1,0,2:T(4,128)(2,1)}, u32[]{:S(2)}, u32[]{:S(2)}) async-start(bf16[64,4,128,128]{3,1,0,2:T(4,128)(2,1)} %copy.59), calls=%async_computation.3 | async-start | bytes 16777216 | tf_op jit(solution)/shard_map/all_to_all | solution.py:124
  395.7 189.0 %all-to-all-start.1 = ((bf16[64,128,4,128]{3,2,0,1:T(4,128)(2,1)}), bf16[64,128,4,128]{3,2,0,1:T(4,128)(2,1)}, u32[]{:S(2)}, u32[]{:S(2)}) async-start(bf16[64,128,4,128]{3,2,0,1:T(4,128)(2,1)} %copy.51), calls=%async_computation.1 | async-start | bytes 16777216 | tf_op jit(solution)/shard_map/all_to_all | solution.py:120
  400.9 13.4 %copy-start.2 = (bf16[2,32,64,64]{3,2,1,0:T(8,128)(2,1)S(1)}, bf16[2,32,64,64]{3,2,1,0:T(8,128)(2,1)}, u32[]{:S(2)}) copy-start(bf16[2,32,64,64]{3,2,1,0:T(8,128)(2,1)} %param.13) | copy-start | bytes 1572868
  618.0 22.5 %copy-start.3 = (bf16[64,256]{1,0:T(8,128)(2,1)S(1)}, bf16[64,256]{1,0:T(8,128)(2,1)}, u32[]{:S(2)}) copy-start(bf16[64,256]{1,0:T(8,128)(2,1)} %param.14) | copy-start | bytes 98308
  618.0 22.5 %copy-start.4 = (bf16[256,64]{0,1:T(8,128)(2,1)S(1)}, bf16[256,64]{0,1:T(8,128)(2,1)}, u32[]{:S(2)}) copy-start(bf16[256,64]{0,1:T(8,128)(2,1)} %param.15) | copy-start | bytes 98308
  618.0 22.5 %copy-start.5 = (f32[256]{0:T(256)S(1)}, f32[256]{0:T(256)}, u32[]{:S(2)}) copy-start(f32[256]{0:T(256)} %param.16) | copy-start | bytes 3076
  618.0 22.5 %copy-start.6 = (f32[64]{0:T(128)S(1)}, f32[64]{0:T(128)}, u32[]{:S(2)}) copy-start(f32[64]{0:T(128)} %param.17) | copy-start | bytes 772
where the time goes:
time: 861 us; the launch traced here: 853 us
  waiting for transfers between devices  309 us (36%)
  matrix products  248 us (29%)
  local copies, waits for them, and re-layouts  239 us (28%)
  other arithmetic  32.8 us (4%)
  starting transfers between devices  21.9 us (3%)
    dot_general x16, matrix products, update(): jnp.einsum('hc,hk->ck', ffn_out, hidden, preferred_element_type=jnp.float32)  193 us
    all_to_all x1, waiting for transfers between devices, body(): lax.all_to_all(ocean_field, 'row', split_axis=2, concat_axis=1, tiled=True)  120 us
    all_to_all x1, waiting for transfers between devices, body(): lax.all_to_all(lines, 'row', split_axis=1, concat_axis=2, tiled=True)  85.7 us
    all_to_all x1, waiting for transfers between devices, body(): lax.all_to_all(ocean_field, 'col', split_axis=1, concat_axis=2, tiled=True)  83.8 us
    unnamed x23, local copies, waits for them, and re-layouts  30 us
    convert_element_type x2, local copies, waits for them, and re-layouts, body(): second_part.astype(jnp.float32)  29.9 us
    convert_element_type x2, local copies, waits for them, and re-layouts, body(): first_part.astype(jnp.float32) + second_part.astype(jnp.float32)  28.4 us
    reshape x2, local copies, waits for them, and re-layouts, body(): ocean_field.reshape(channels, row_cells, col_cells * line_cells)  24.6 us
  transfers between devices with their start and end apart: 4, of which 4 were waited for; matrix products, arithmetic and copies ran while one was open for 29% of the time, Pallas kernels for 0%

commit v1 on v0

v1 whole, which is shorter than its diff:
```python
import functools
import math

import jax
import jax.numpy as jnp
from jax import lax
from jax.experimental import pallas as pl
from jax.experimental.pallas import tpu as pltpu
from jax.sharding import PartitionSpec as P

MIB = 1024 * 1024
HALF_ROOT = math.sqrt(0.5)


def forward_rows(length, mode_count):
    grid_pos = jnp.arange(length, dtype=jnp.int32)[None, :]
    mode_location = jnp.arange(mode_count, dtype=jnp.int32)[:, None]
    phase = (grid_pos * mode_location % length).astype(jnp.float32) * (2.0 * math.pi / length)
    return jnp.concatenate([jnp.cos(phase), -jnp.sin(phase)], axis=0).astype(jnp.bfloat16)


def inverse_rows(length, mode_count):
    mode_location = jnp.arange(mode_count, dtype=jnp.int32)[:, None]
    grid_pos = jnp.arange(length, dtype=jnp.int32)[None, :]
    phase = (grid_pos * mode_location % length).astype(jnp.float32) * (2.0 * math.pi / length)
    factor = jnp.where(mode_location == 0, 1.0, 2.0).astype(jnp.float32) / length
    return jnp.concatenate(
        [factor * jnp.cos(phase), -factor * jnp.sin(phase)], axis=0
    ).astype(jnp.bfloat16)


def mix_kernel(*refs):
    count = len(refs) // 2
    for spec, out in zip(refs[:count], refs[count:]):
        channels = spec.shape[-1]
        for mode in range(spec.shape[1]):
            real = spec[0, mode].astype(jnp.float32).T
            imag = spec[1, mode].astype(jnp.float32).T
            upper = jnp.concatenate([real, -imag], axis=1)
            lower = jnp.concatenate([imag, real], axis=1)
            out[mode, :channels] = upper.astype(jnp.bfloat16)
            out[mode, channels:] = lower.astype(jnp.bfloat16)


def mix_rows(after, *specs):
    _, mode_count, channels, _ = specs[0].shape
    block = min(8, mode_count)
    kernel, token_specs, token = ordered(mix_kernel, after)
    return pl.pallas_call(
        kernel,
        grid=(mode_count // block,),
        in_specs=token_specs
        + [pl.BlockSpec((2, block, channels, channels), lambda g: (0, g, 0, 0))]
        * len(specs),
        out_specs=[pl.BlockSpec((block, 2 * channels, 2 * channels), lambda g: (g, 0, 0))]
        * len(specs),
        out_shape=[
            jax.ShapeDtypeStruct((mode_count, 2 * channels, 2 * channels), jnp.bfloat16)
        ]
        * len(specs),
        compiler_params=pltpu.CompilerParams(vmem_limit_bytes=12 * MIB),
        cost_estimate=cost(2.5, 4 * MIB),
        name="mixing_matrices",
    )(*token, *specs)


def cost(micros, size):
    return pl.CostEstimate(
        flops=int(micros * 1.15e9), bytes_accessed=int(size), transcendentals=0
    )


def ordered(kernel, after):
    if after is None:
        return kernel, [], []
    return (
        lambda _, *refs: kernel(*refs),
        [pl.BlockSpec(memory_space=pl.ANY)],
        [after],
    )


def mm(left, right, dims=(1, 0)):
    return lax.dot_general(
        left, right, (((dims[0],), (dims[1],)), ((), ())), preferred_element_type=jnp.float32
    )


def stack_rows(parts):
    if parts[0].shape[0] % 16 == 0:
        return jnp.concatenate(parts, axis=0)
    return jnp.concatenate([p.astype(jnp.float32) for p in parts], axis=0).astype(jnp.bfloat16)


def partners(ways):
    steps, half = [0], ways // 2
    while half:
        steps += range(half, 2 * half)
        half //= 2
    return steps


def pack_kernel(ways, me_ref, x_ref, *refs):
    outs, wide = refs[:ways], refs[ways]
    channels, rows, _, lanes = x_ref.shape
    wide[...] = x_ref[...].astype(jnp.float32).reshape(channels * rows * ways, lanes)
    for out, step in zip(outs, partners(ways)):
        picked = wide[pl.ds(me_ref[0] ^ step, channels * rows, stride=ways), :]
        out[...] = picked.reshape(channels, rows, lanes).astype(jnp.bfloat16)


def pack(field, first, count, ways, me, after):
    channels, rows, _, lanes = field.shape
    depth = min(16, channels)
    token_specs = [] if after is None else [pl.BlockSpec(memory_space=pl.ANY)]
    token = [] if after is None else [after]

    def kernel(me_ref, x_ref, *refs):
        pack_kernel(ways, me_ref, x_ref, *refs[len(token) :])

    return pl.pallas_call(
        kernel,
        grid_spec=pltpu.PrefetchScalarGridSpec(
            num_scalar_prefetch=1,
            grid=(count, channels // depth),
            in_specs=[
                pl.BlockSpec((depth, rows, ways, lanes), lambda k, g, me: (g, 0, first + k, 0))
            ]
            + token_specs,
            out_specs=[pl.BlockSpec((None, depth, rows, lanes), lambda k, g, me: (k, g, 0, 0))]
            * ways,
            scratch_shapes=[pltpu.VMEM((depth * rows * ways, lanes), jnp.float32)],
        ),
        out_shape=[jax.ShapeDtypeStruct((count, channels, rows, lanes), jnp.bfloat16)] * ways,
        compiler_params=pltpu.CompilerParams(vmem_limit_bytes=12 * MIB),
        cost_estimate=cost(3 * count, 4 * count * channels * rows * ways * lanes),
        name="pack_columns",
    )(me, field, *token)


def side_kernel(x_ref, _, out_ref):
    out_ref[...] = x_ref[...]


def rows_first(field, after):
    channels, rows, cols, lanes = field.shape
    return pl.pallas_call(
        side_kernel,
        grid=(rows,),
        in_specs=[
            pl.BlockSpec((channels, None, cols, lanes), lambda r: (0, r, 0, 0)),
            pl.BlockSpec(memory_space=pl.ANY),
        ],
        out_specs=pl.BlockSpec((None, channels, cols, lanes), lambda r: (r, 0, 0, 0)),
        out_shape=jax.ShapeDtypeStruct((rows, channels, cols, lanes), jnp.bfloat16),
        compiler_params=pltpu.CompilerParams(vmem_limit_bytes=12 * MIB),
        cost_estimate=cost(6, 16 * MIB),
        name="rows_first",
    )(field, after)


def mix_modes(mix_ref, spectra, mixed):
    mode_count, depth, _ = mix_ref.shape
    channels = depth // 2

    def one(mode, _):
        block = spectra[pl.ds(pl.multiple_of(mode * depth, depth), depth), :].astype(jnp.bfloat16)
        result = mm(mix_ref[mode], block)
        for part in range(2):
            mixed[pl.ds(part * mode_count + mode, channels, stride=2 * mode_count), :] = result[
                part * channels : (part + 1) * channels
            ]
        return 0

    lax.fori_loop(0, mode_count, one, 0, unroll=4)


def keep_spectra(spectra, result, channel, mode_count, channels, lanes):
    for at in range(2):
        for part in range(2):
            spectra[pl.ds(part * channels + channel + at, mode_count, stride=2 * channels), :] = (
                result[part * mode_count : (part + 1) * mode_count, at * lanes : (at + 1) * lanes]
            )


def mixed_pair(mixed, channel, coefs):
    start = pl.multiple_of(channel * coefs, 2 * coefs)
    return jnp.concatenate(
        [mixed[pl.ds(start, coefs), :], mixed[pl.ds(start + coefs, coefs), :]], axis=1
    ).astype(jnp.bfloat16)


def lines_kernel(ways, ft_ref, it_ref, mix_ref, *refs):
    count = (len(refs) - 3) // 2
    pieces, outs = refs[:count], refs[count : 2 * count]
    spectra, mixed, wide = refs[2 * count :]
    if count < ways:
        pieces = [pieces[0].at[step] for step in range(ways)]
        outs = [outs[0].at[step] for step in range(ways)]
    channels, length, lanes = pieces[0].shape
    mode_count = mix_ref.shape[0]
    total = ways * length

    def forward(pair, _):
        channel = 2 * pair
        right = jnp.concatenate(
            [stack_rows([piece[channel + at] for piece in pieces]) for at in range(2)], axis=1
        )
        keep_spectra(spectra, mm(ft_ref[...], right), channel, mode_count, channels, lanes)
        return 0

    lax.fori_loop(0, channels // 2, forward, 0, unroll=4)
    mix_modes(mix_ref, spectra, mixed)

    def inverse(pair, _):
        channel = 2 * pair
        result = mm(it_ref[...], mixed_pair(mixed, channel, 2 * mode_count))
        for at in range(2):
            wide[pl.ds(channel + at, total, stride=channels), :] = result[
                :, at * lanes : (at + 1) * lanes
            ]
        return 0

    lax.fori_loop(0, channels // 2, inverse, 0, unroll=4)
    for step in range(ways):
        part = wide[pl.ds(step * length * channels, length * channels), :]
        outs[step][...] = part.reshape(length, channels, lanes).astype(jnp.bfloat16)


def transform_cost(channels, mode_count, length, lines):
    macs = lines * channels * mode_count * 2 * (2 * length + 2 * channels)
    return cost(macs * 5e-8, 4 * lines * channels * length)


def along_lines(pieces, weights, order=None, which=None, after=None):
    stacked = not isinstance(pieces, list)
    if stacked:
        ways, across, channels, length, lanes = pieces.shape
        pieces = [pieces]
        piece_spec = pl.BlockSpec(
            (ways, None, channels, length, lanes), lambda g: (0, g, 0, 0, 0)
        )
        out_spec = pl.BlockSpec((ways, None, length, channels, lanes), lambda g: (0, g, 0, 0, 0))
        out_shape = (ways, across, length, channels, lanes)
    else:
        ways = len(pieces)
        begin, across = which
        _, channels, length, lanes = pieces[0].shape
        piece_spec = pl.BlockSpec(
            (None, channels, length, lanes), lambda g: (begin + g, 0, 0, 0)
        )
        out_spec = pl.BlockSpec((None, length, channels, lanes), lambda g: (g, 0, 0, 0))
        out_shape = (across, length, channels, lanes)
    mode_count = weights.shape[0]
    total = ways * length
    forward = forward_rows(total, mode_count)
    back = inverse_rows(total, mode_count).T
    if not stacked:
        forward = forward.reshape(2 * mode_count, ways, length)
        forward = jnp.take(forward, order, axis=1).reshape(2 * mode_count, total)
        back = back.reshape(ways, length, 2 * mode_count)
        back = jnp.take(back, order, axis=0).reshape(total, 2 * mode_count)
    whole = lambda shape: pl.BlockSpec(shape, lambda g: (0,) * len(shape))
    kernel, token_specs, token = ordered(functools.partial(lines_kernel, ways), after)
    return pl.pallas_call(
        kernel,
        grid=(across,),
        in_specs=token_specs
        + [whole(forward.shape), whole(back.shape), whole(weights.shape)]
        + [piece_spec] * len(pieces),
        out_specs=[out_spec] * len(pieces),
        out_shape=[jax.ShapeDtypeStruct(out_shape, jnp.bfloat16)] * len(pieces),
        scratch_shapes=[
            pltpu.VMEM((2 * channels * mode_count, lanes), jnp.float32),
            pltpu.VMEM((2 * channels * mode_count, lanes), jnp.float32),
            pltpu.VMEM((total * channels, lanes), jnp.float32),
        ],
        compiler_params=pltpu.CompilerParams(vmem_limit_bytes=26 * MIB),
        cost_estimate=transform_cost(channels, mode_count, total, across * lanes),
        name="line_branch",
    )(*token, forward, back, weights, *pieces)


def last_kernel(ft_ref, it_ref, mix_ref, x_ref, out_ref, spectra, mixed, wide):
    channels, rows, cols, length = x_ref.shape
    mode_count = mix_ref.shape[0]
    cells = rows * cols

    def forward(pair, _):
        channel = 2 * pair
        right = jnp.concatenate(
            [x_ref[channel + at].reshape(cells, length) for at in range(2)], axis=0
        )
        keep_spectra(
            spectra, mm(ft_ref[...], right, (1, 1)), channel, mode_count, channels, cells
        )
        return 0

    lax.fori_loop(0, channels // 2, forward, 0, unroll=4)
    mix_modes(mix_ref, spectra, mixed)

    def inverse(pair, _):
        channel = 2 * pair
        result = mm(mixed_pair(mixed, channel, 2 * mode_count), it_ref[...], (0, 0))
        for at in range(2):
            wide[pl.ds(channel + at, cells, stride=channels), :] = result[
                at * cells : (at + 1) * cells
            ]
        return 0

    lax.fori_loop(0, channels // 2, inverse, 0, unroll=4)
    out_ref[...] = wide[...].reshape(rows, cols, channels, length).astype(jnp.bfloat16)


def last_branch(field, weights, part, parts, done, after):
    channels, rows, cols, length = field.shape
    mode_count = weights.shape[0]
    block = max(1, min(rows // parts, 128 // cols))
    steps = rows // block // parts
    forward, back = forward_rows(length, mode_count), inverse_rows(length, mode_count)
    whole = lambda shape: pl.BlockSpec(shape, lambda g: (0,) * len(shape))
    _, token_specs, token = ordered(last_kernel, after)
    aliases = {}
    if done is not None:
        token_specs, token = token_specs + [pl.BlockSpec(memory_space=pl.ANY)], token + [done]
        aliases = {len(token) - 1: 0}
    skipped = len(token)
    return pl.pallas_call(
        lambda *refs: last_kernel(*refs[skipped:]),
        grid=(steps,),
        in_specs=token_specs
        + [
            whole(forward.shape),
            whole(back.shape),
            whole(weights.shape),
            pl.BlockSpec(
                (channels, block, cols, length), lambda g: (0, part * steps + g, 0, 0)
            ),
        ],
        out_specs=pl.BlockSpec(
            (block, cols, channels, length), lambda g: (part * steps + g, 0, 0, 0)
        ),
        out_shape=jax.ShapeDtypeStruct((rows, cols, channels, length), jnp.bfloat16),
        input_output_aliases=aliases,
        scratch_shapes=[
            pltpu.VMEM((2 * channels * mode_count, block * cols), jnp.float32),
            pltpu.VMEM((2 * channels * mode_count, block * cols), jnp.float32),
            pltpu.VMEM((block * cols * channels, length), jnp.float32),
        ],
        compiler_params=pltpu.CompilerParams(vmem_limit_bytes=26 * MIB),
        cost_estimate=transform_cost(channels, mode_count, length, steps * block * cols),
        name="last_branch",
    )(*token, forward, back, weights, field)


def cell_kernel(ways, me_ref, x_ref, win_ref, wout_ref, bin_ref, bout_ref, *refs):
    first = refs[:ways]
    second, third = refs[ways : ways + 2]
    out_ref, wide = refs[-2:]
    channels, _, _, lanes = x_ref.shape
    steps = partners(ways)
    for place in range(0, ways, 2):
        summed = []
        for at in range(2):
            col = me_ref[0] ^ steps[place + at]
            pair = first[place + at][...].astype(jnp.float32) + second[col].astype(jnp.float32)
            pair = pair.astype(jnp.bfloat16).astype(jnp.float32)
            summed.append((pair + third[col].astype(jnp.float32)).astype(jnp.bfloat16))
        pre = mm(win_ref[...], jnp.concatenate(summed, axis=1)) + bin_ref[...]
        hidden = (0.5 * pre * (1.0 + lax.erf(pre * HALF_ROOT))).astype(jnp.bfloat16)
        result = mm(wout_ref[...], hidden) + bout_ref[...]
        for at in range(2):
            col = me_ref[0] ^ steps[place + at]
            wide[pl.ds(col, channels, stride=ways), :] = result[:, at * lanes : (at + 1) * lanes]
    total = wide[...].reshape(channels, ways, lanes) + x_ref[:, 0].astype(jnp.float32)
    out_ref[:, 0] = total.astype(jnp.bfloat16)


def cells(field, first, which, second, third, ffn, chunk, me, done):
    channels, rows, cols, lanes = field.shape
    ways = len(first)
    whole = lambda shape: pl.BlockSpec(shape, lambda *_: (0,) * len(shape))
    tile = pl.BlockSpec((channels, 1, ways, lanes), lambda r, me: (0, r, chunk, 0))
    branch = pl.BlockSpec((None, ways, channels, lanes), lambda r, me: (r, chunk, 0, 0))
    in_specs = [tile] + [whole(w.shape) for w in ffn]
    in_specs += [
        pl.BlockSpec((None, None, channels, lanes), lambda r, me: (which, r, 0, 0))
    ] * ways
    in_specs += [branch, branch]
    operands = [me, field, *ffn, *first, second, third]
    aliases = {}
    if done is not None:
        in_specs.append(pl.BlockSpec(memory_space=pl.ANY))
        aliases = {len(operands): 0}
        operands.append(done)
    hidden = ffn[0].shape[0]
    count = rows * ways * lanes
    return pl.pallas_call(
        functools.partial(cell_kernel, ways),
        grid_spec=pltpu.PrefetchScalarGridSpec(
            num_scalar_prefetch=1,
            grid=(rows,),
            in_specs=in_specs,
            out_specs=tile,
            scratch_shapes=[pltpu.VMEM((channels * ways, lanes), jnp.float32)],
        ),
        out_shape=jax.ShapeDtypeStruct(field.shape, jnp.bfloat16),
        input_output_aliases=aliases,
        compiler_params=pltpu.CompilerParams(vmem_limit_bytes=16 * MIB),
        cost_estimate=cost(4.6e-6 * count * hidden, 10 * count * channels),
        name="feed_forward",
    )(*operands)


def exchange(pieces, axis):
    ways = len(pieces)
    return [
        lax.ppermute(piece, axis, [(at, at ^ step) for at in range(ways)]) if step else piece
        for piece, step in zip(pieces, partners(ways))
    ]


def body(field, spec_first, spec_second, spec_third, ffn_in, ffn_out, bias_in, bias_out):
    channels, rows, cols, lanes = field.shape
    ways, col_ways = lax.axis_size("row"), lax.axis_size("col")
    row_me = lax.axis_index("row")
    me = row_me.reshape(1).astype(jnp.int32)
    row_order = row_me ^ jnp.array(partners(ways))
    chunks = cols // ways
    across = rows // col_ways
    ffn = (ffn_in.T, ffn_out.T, bias_in[:, None], bias_out[:, None])

    half = max(1, chunks // 2)
    rest = chunks - half
    early = pack(field, 0, half, ways, me, None)
    late = pack(field, half, rest, ways, me, early[0])
    early_in, late_in = exchange(early, "row"), exchange(late, "row")
    side = rows_first(field, late[0])
    first_mix, second_mix, third_mix = mix_rows(side, spec_first, spec_second, spec_third)
    side = side.reshape(col_ways, across, channels, cols, lanes)
    side = lax.all_to_all(side, "col", split_axis=0, concat_axis=0)

    third = last_branch(field, third_mix, 0, 2, None, None)
    third = last_branch(field, third_mix, 1, 2, third, early_in[-3])
    parts = along_lines(early_in, first_mix, row_order, (0, half))
    back = exchange(parts, "row")
    first = [(back, which) for which in range(half)]
    (second,) = along_lines(side, second_mix, after=parts[0])
    second = lax.all_to_all(second, "col", split_axis=0, concat_axis=0)
    second = second.reshape(rows, cols, channels, lanes)
    for which in range(rest):
        parts = along_lines(late_in, first_mix, row_order, (which, 1))
        first.append((exchange(parts, "row"), 0))

    result = None
    for chunk, (branch, which) in enumerate(first):
        result = cells(field, branch, which, second, third, ffn, chunk, me, result)
    return result


def solution(mesh):
    return jax.shard_map(
        body,
        mesh=mesh,
        in_specs=(P("grp", "row", "col", None), P(), P(), P(), P(), P(), P(), P()),
        out_specs=P("grp", "row", "col", None),
        check_vma=False,
    )
```

time: 861 us -> 475 us (0.55)
  matrix products: 248 us -> 0 us
  Pallas kernels: 0 us -> 203 us
  waiting for transfers between devices: 309 us -> 117 us
  local copies, waits for them, and re-layouts: 239 us -> 63.5 us
  starting transfers between devices: 21.9 us -> 88.6 us
  other arithmetic: 32.8 us -> 0.8 us
    all_to_all x4 -> x2, waiting for transfers between devices: 309 us -> 0.01 us  [the longest x1 0.01 us: body(): side = lax.all_to_all(side, 'col', split_axis=0, concat_axis=0)]
    dot_general x25 -> x0, matrix products: 248 us -> none  [the longest x16 193 us: update(): jnp.einsum('hc,hk->ck', ffn_out, hidden, preferred_element_type=jnp.float32)]
    pallas_call x0 -> x14, Pallas kernels: none -> 203 us  [the longest x4 76.5 us: along_lines(): pl.pallas_call(kernel, grid=(across,), in_specs=token_specs + [whole(forw...]
    ppermute x0 -> x35, waiting for transfers between devices: none -> 117 us  [exchange(): lax.ppermute(piece, axis, [(at, at ^ step) for at in range(ways)])]
    convert_element_type x8 -> x0, local copies, waits for them, and re-layouts: 107 us -> none  [the longest x2 29.9 us: body(): second_part.astype(jnp.float32)]
    ppermute x0 -> x35, starting transfers between devices: none -> 76.8 us  [exchange(): lax.ppermute(piece, axis, [(at, at ^ step) for at in range(ways)])]
    reshape x6 -> x1, local copies, waits for them, and re-layouts: 61.9 us -> 0.08 us  [along_lines(): forward = jnp.take(forward, order, axis=1).reshape(2 * mode_count, total)]
    convert_element_type x3 -> x0, other arithmetic: 32.4 us -> none  [the longest x1 22.5 us: body(): (pair.astype(jnp.float32) + third_part.astype(jnp.float32)).astype(jnp.bf...]
  transfers between devices with their start and end apart: 4 -> 37, of which waited for: 4 -> 5; matrix products, arithmetic and copies ran while one was open for 29% -> 1% of each run, Pallas kernels for 0% -> 37%
where the time goes in v1:
time: 475 us; the launch traced here: 474 us
  Pallas kernels  203 us (43%)
  waiting for transfers between devices  117 us (25%)
  starting transfers between devices  88.6 us (19%)
  local copies, waits for them, and re-layouts  63.5 us (13%)
    ppermute x35, waiting for transfers between devices, exchange(): lax.ppermute(piece, axis, [(at, at ^ step) for at in range(ways)])  117 us
    ppermute x35, starting transfers between devices, exchange(): lax.ppermute(piece, axis, [(at, at ^ step) for at in range(ways)])  76.8 us
    pallas_call x4, Pallas kernels, along_lines(): pl.pallas_call(kernel, grid=(across,), in_specs=token_specs + [whole(forw...  76.5 us
    pallas_call x4, Pallas kernels, cells(): pl.pallas_call(functools.partial(cell_kernel, ways), grid_spec=pltpu.Pref...  75.3 us
    unnamed x155, local copies, waits for them, and re-layouts  61.9 us
    pallas_call x2, Pallas kernels, last_branch(): pl.pallas_call(lambda *refs: last_kernel(*refs[skipped:]), grid=(steps,),...  38.8 us
  transfers between devices with their start and end apart: 37, of which 5 were waited for; matrix products, arithmetic and copies ran while one was open for 1% of the time, Pallas kernels for 37%

profile of v1, /device:TPU:0, one launch (start us, length us, event | category | flops | bytes accessed | tf_op | source)
XLA Modules:
  0.0 474.1 jit_solution(1962975425231688117)
XLA Ops:
  0.0 3.4 copy-done.6
  3.4 3.6 pack_columns.2
  12.7 5.1 %pack_columns.3 = (bf16[2,64,16,128]{3,2,1,0:T(8,128)(2,1)S(1)}, bf16[2,64,16,128]{3,2,1,0:T(8,128)(2,1)}, bf16[2,64,16,128]{3,2,1,0:T(8,128)(2,1)}, bf16[2,64,1...) custom-call(s32[1]{0:T(128)} %bitcast.me_ref, ...), custom_call_target="tpu_custom_call" | custom-call | flops 6899999744 | bytes 8388608 | tf_op jit(solution)/shard_map/pack_columns/pallas_call | solution.py:121
  20.0 3.4 copy-done
  23.4 5.9 %all-to-all-start = ((bf16[4,4,64,32,128]{4,3,2,1,0:T(8,128)(2,1)}), bf16[4,4,64,32,128]{4,3,2,1,0:T(8,128)(2,1)}, u32[]{:S(2)}, u32[]{:S(2)}) async-start(bf16[4,4,64,32,128]{4,3,2,1,0:T(8,128)(2,1)} %bitcast.14), calls=%async_computation | async-start | bytes 16777216 | tf_op jit(solution)/shard_map/all_to_all | solution.py:441
  29.3 4.1 collective-permute-start.14
  38.4 53.0 %collective-permute-done.14.refs_1_ = bf16[2,64,16,128]{3,2,1,0:T(8,128)(2,1)} collective-permute-done((bf16[2,64,16,128]{3,2,1,0:T(8,128)(2,1)}, bf16[2,64,16,128]{3,2,1,0:T(8,128)(2,1)}, u32[]{:S(2)}, u32[]{:S(2)}) %collective-permute-start.14) | collective-permute-done | bytes 524320 | tf_op jit(solution)/shard_map/ppermute | solution.py:418
  91.4 9.7 %collective-permute-done.15.refs_2_ = bf16[2,64,16,128]{3,2,1,0:T(8,128)(2,1)} collective-permute-done((bf16[2,64,16,128]{3,2,1,0:T(8,128)(2,1)}, bf16[2,64,16,128]{3,2,1,0:T(8,128)(2,1)}, u32[]{:S(2)}, u32[]{:S(2)}) %collective-permute-start.15) | collective-permute-done | bytes 524320 | tf_op jit(solution)/shard_map/ppermute | solution.py:418
  103.4 3.4 copy-done.1
  111.3 4.6 collective-permute-start
  115.8 22.0 %collective-permute-start.1 = (bf16[2,64,16,128]{3,2,1,0:T(8,128)(2,1)}, bf16[2,64,16,128]{3,2,1,0:T(8,128)(2,1)}, u32[]{:S(2)}, u32[]{:S(2)}) collective-permute-start(bf16[2,64,16,128]{3,2,1,0:T(8,128)(2,1)} %get-tuple-element.54), channel_id=1, source_target_pairs={{0,20},{4,16},{8,28},{12,24},{16,4},{20,0},{24,12},{28,8},{1,21},{... | collective-permute-start | bytes 1572872 | tf_op jit(solution)/shard_map/ppermute | solution.py:418
  141.4 18.9 %line_branch.5 = (bf16[2,16,64,128]{3,2,1,0:T(8,128)(2,1)S(1)}, bf16[2,16,64,128]{3,2,1,0:T(8,128)(2,1)S(1)}, bf16[2,16,64,128]{3,2,1,0:T(8,128)(2,1)S(1)}, bf16...) custom-call(bf16[64,128]{1,0:T(8,128)(2,1)S(1)} %copy.22.ft_ref, ...), custom_call_target="tpu_custom_call" | custom-call | flops 23152558080 | bytes 8388608 | tf_op jit(solution)/shard_map/line_branch/pallas_call | solution.py:265
  166.6 36.8 %line_branch.6 = bf16[4,4,32,64,128]{4,3,2,1,0:T(8,128)(2,1)S(1)} custom-call(bf16[2,16,64,128]{3,2,1,0:T(8,128)(2,1)S(1)} %copy-done.65, bf16[64,128]{1,0:T(8,128)(2,1)S(1)} %pad_maximum_fusion.2.refs_0_.refs_2_, bf16[128,64]{1,0:T(8,128)(2,1)S(1)} %copy.21.refs_1_, bf16[32,128,128]{2,1,0:T(8,128)(2,1)S(1)} %copy-done.15, ...), custom_call_target="tpu_custom_call" | custom-call | flops 46305116160 | bytes 16777216 | tf_op jit(solution)/shard_map/line_branch/pallas_call | solution.py:265
  203.5 3.4 copy-done.2
  206.8 5.9 %all-to-all-start.1 = ((bf16[4,4,32,64,128]{4,3,2,1,0:T(8,128)(2,1)}), bf16[4,4,32,64,128]{4,3,2,1,0:T(8,128)(2,1)}, u32[]{:S(2)}, u32[]{:S(2)}) async-start(bf16[4,4,32,64,128]{4,3,2,1,0:T(8,128)(2,1)} %copy-done.2), calls=%async_computation.1 | async-start | bytes 16777216 | tf_op jit(solution)/shard_map/all_to_all | solution.py:449
  212.8 3.4 copy-done.7
  216.2 19.4 %last_branch.2.refs_1_ = bf16[16,32,64,128]{3,2,1,0:T(8,128)(2,1)S(1)} custom-call(bf16[64,128]{1,0:T(8,128)(2,1)S(1)} %pad_maximum_fusion.2.refs_0_.refs_2_, bf16[64,128]{1,0:T(8,128)(2,1)S(1)} %get-tuple-element.95.refs_1_.refs_3_, bf16[32,128,128]{2,1,0:T(8,128)(2,1)S(1)} %copy-done.13, bf16[64,16,32,128]{3,2,1,0:T(8,128)(2,1)S(1)} %copy-done.7), custom_call_target="tpu_custom_call" | custom-call | flops 23152558080 | bytes 8388608 | tf_op jit(solution)/shard_map/last_branch/pallas_call | solution.py:328
  241.5 3.4 copy-done.8
  244.9 3.4 copy-done.59
  248.3 19.4 %last_branch.3.refs_9_ = bf16[16,32,64,128]{3,2,1,0:T(8,128)(2,1)S(1)} custom-call(bf16[2,64,16,128]{3,2,1,0:T(8,128)(2,1)} %collective-permute-done.18.refs_5_.refs_0_, bf16[16,32,64,128]{3,2,1,0:T(8,128)(2,1)S(1)} %copy-done.59, bf16[64,128]{1,0:T(8,128)(2,1)S(1)} %pad_maximum_fusion.2.refs_0_.refs_2_, ...), custom_call_target="tpu_custom_call", output_to_operand_aliasing={{}: (1, {})} | custom-call | flops 23152558080 | bytes 8388608 | tf_op jit(solution)/shard_map/last_branch/pallas_call | solution.py:328
  277.4 10.9 %line_branch.7 = (bf16[1,16,64,128]{3,2,1,0:T(8,128)(2,1)S(1)}, bf16[1,16,64,128]{3,2,1,0:T(8,128)(2,1)}, bf16[1,16,64,128]{3,2,1,0:T(8,128)(2,1)}, bf16[1,16,64...) custom-call(bf16[64,128]{1,0:T(8,128)(2,1)S(1)} %copy.22.ft_ref, ...), custom_call_target="tpu_custom_call" | custom-call | flops 11576279040 | bytes 4194304 | tf_op jit(solution)/shard_map/line_branch/pallas_call | solution.py:265
  289.8 40.9 %collective-permute-done.28.refs_1_ = bf16[2,16,64,128]{3,2,1,0:T(8,128)(2,1)S(1)} collective-permute-done((bf16[2,16,64,128]{3,2,1,0:T(8,128)(2,1)S(1)}, bf16[2,16,64,128]{3,2,1,0:T(8,128)(2,1)S(1)}, u32[]{:S(2)}, u32[]{:S(2)}) %collective-permute-start.28) | collective-permute-done | bytes 524320 | tf_op jit(solution)/shard_map/ppermute | solution.py:418
  330.7 11.2 %collective-permute-done.29.refs_2_ = bf16[2,16,64,128]{3,2,1,0:T(8,128)(2,1)S(1)} collective-permute-done((bf16[2,16,64,128]{3,2,1,0:T(8,128)(2,1)S(1)}, bf16[2,16,64,128]{3,2,1,0:T(8,128)(2,1)S(1)}, u32[]{:S(2)}, u32[]{:S(2)}) %collective-permute-start.29) | collective-permute-done | bytes 524320 | tf_op jit(solution)/shard_map/ppermute | solution.py:418
  342.0 9.9 %line_branch.4 = (bf16[1,16,64,128]{3,2,1,0:T(8,128)(2,1)S(1)}, bf16[1,16,64,128]{3,2,1,0:T(8,128)(2,1)S(1)}, bf16[1,16,64,128]{3,2,1,0:T(8,128)(2,1)S(1)}, bf16...) custom-call(bf16[64,128]{1,0:T(8,128)(2,1)S(1)} %copy.22.ft_ref, ...), custom_call_target="tpu_custom_call" | custom-call | flops 11576279040 | bytes 4194304 | tf_op jit(solution)/shard_map/line_branch/pallas_call | solution.py:265
  358.3 11.7 %collective-permute-start.22 = (bf16[1,16,64,128]{3,2,1,0:T(8,128)(2,1)}, bf16[1,16,64,128]{3,2,1,0:T(8,128)(2,1)}, u32[]{:S(2)}, u32[]{:S(2)}) collective-permute-start(bf16[1,16,64,128]{3,2,1,0:T(8,128)(2,1)} %get-tuple-element.80), channel_id=1, source_target_pairs={{0,20},{4,16},{8,28},{12,24},{16,4},{20,0},{24,12},{28,8},{1,21},{... | collective-permute-start | bytes 786440 | tf_op jit(solution)/shard_map/ppermute | solution.py:418
  373.2 3.4 copy-done.9
  377.6 3.4 copy-done.61
  382.1 18.8 %feed_forward.4.refs_10_ = bf16[64,16,32,128]{3,2,1,0:T(8,128)(2,1)} custom-call(s32[1]{0:T(128)} %bitcast.me_ref, bf16[64,16,32,128]{3,2,1,0:T(8,128)(2,1)S(1)} %copy-done.9, bf16[256,64]{1,0:T(8,128)(2,1)S(1)} %bitcast.16, bf16[64,256]{1,0:T(8,128)(2,1)S(1)} %bitcast.23, f32[256,1]{1,0:T(8,128)S(1)} %copy.32.bin_ref, f32[64,1]{1,0:T(8,128)S(1)} %copy.33.bout_ref, ...), custom_call_target="tpu_custom_call" | custom-call | flops 22187868160 | bytes 10485760 | tf_op jit(solution)/shard_map/feed_forward/pallas_call | solution.py:398
  404.7 5.0 %collective-permute-start.8 = (bf16[1,16,64,128]{3,2,1,0:T(8,128)(2,1)S(1)}, bf16[1,16,64,128]{3,2,1,0:T(8,128)(2,1)S(1)}, u32[]{:S(2)}, u32[]{:S(2)}) collective-permute-start(bf16[1,16,64,128]{3,2,1,0:T(8,128)(2,1)S(1)} %copy-done.50), channel_id=1, source_target_pairs={{0,20},{4,16},{8,28},{12,24},{16,4},{20,0},{24,12},{28,8},{1,21},{... | collective-permute-start | bytes 786440 | tf_op jit(solution)/shard_map/ppermute | solution.py:418
  409.8 18.7 %feed_forward.5.refs_10_ = bf16[64,16,32,128]{3,2,1,0:T(8,128)(2,1)} custom-call(s32[1]{0:T(128)} %bitcast.me_ref, bf16[64,16,32,128]{3,2,1,0:T(8,128)(2,1)S(1)} %copy-done.9, bf16[256,64]{1,0:T(8,128)(2,1)S(1)} %bitcast.17, bf16[64,256]{1,0:T(8,128)(2,1)S(1)} %bitcast.24, f32[256,1]{1,0:T(8,128)S(1)} %copy.32.bin_ref, ...), custom_call_target="tpu_custom_call", output_to_operand_aliasing={{}: (16, {})} | custom-call | flops 22187868160 | bytes 10485760 | tf_op jit(solution)/shard_map/feed_forward/pallas_call | solution.py:398
  433.9 19.0 %feed_forward.6.refs_10_ = bf16[64,16,32,128]{3,2,1,0:T(8,128)(2,1)} custom-call(s32[1]{0:T(128)} %bitcast.me_ref, bf16[64,16,32,128]{3,2,1,0:T(8,128)(2,1)S(1)} %copy-done.9, bf16[256,64]{1,0:T(8,128)(2,1)S(1)} %bitcast.18, bf16[64,256]{1,0:T(8,128)(2,1)S(1)} %bitcast.25, f32[256,1]{1,0:T(8,128)S(1)} %copy.32.bin_ref, ...), custom_call_target="tpu_custom_call", output_to_operand_aliasing={{}: (16, {})} | custom-call | flops 22187868160 | bytes 10485760 | tf_op jit(solution)/shard_map/feed_forward/pallas_call | solution.py:398
  455.3 18.7 %feed_forward.7 = bf16[64,16,32,128]{3,2,1,0:T(8,128)(2,1)} custom-call(s32[1]{0:T(128)} %bitcast.me_ref, bf16[64,16,32,128]{3,2,1,0:T(8,128)(2,1)S(1)} %copy-done.9, bf16[256,64]{1,0:T(8,128)(2,1)S(1)} %bitcast.19, bf16[64,256]{1,0:T(8,128)(2,1)S(1)} %bitcast.26, f32[256,1]{1,0:T(8,128)S(1)} %copy.32.bin_ref, ...), custom_call_target="tpu_custom_call", output_to_operand_aliasing={{}: (16, {})} | custom-call | flops 22187868160 | bytes 10485760 | tf_op jit(solution)/shard_map/feed_forward/pallas_call | solution.py:398
  (231 shorter events, 69.8 us)
Async XLA Ops:
  23.4 142.0 %all-to-all-start = ((bf16[4,4,64,32,128]{4,3,2,1,0:T(8,128)(2,1)}), bf16[4,4,64,32,128]{4,3,2,1,0:T(8,128)(2,1)}, u32[]{:S(2)}, u32[]{:S(2)}) async-start(bf16[4,4,64,32,128]{4,3,2,1,0:T(8,128)(2,1)} %bitcast.14), calls=%async_computation | async-start | bytes 16777216 | tf_op jit(solution)/shard_map/all_to_all | solution.py:441
  29.3 62.1 %collective-permute-start.14 = (bf16[2,64,16,128]{3,2,1,0:T(8,128)(2,1)}, bf16[2,64,16,128]{3,2,1,0:T(8,128)(2,1)}, u32[]{:S(2)}, u32[]{:S(2)}) collective-permute-start(bf16[2,64,16,128]{3,2,1,0:T(8,128)(2,1)} %copy-done.36), channel_id=1, source_target_pairs={{0,16},{4,20},{8,24},{12,28},{16,0},{20,4},{24,8},{28,12},{1,17},{... | collective-permute-start | bytes 1572872 | tf_op jit(solution)/shard_map/ppermute | solution.py:418
  33.4 67.7 %collective-permute-start.15 = (bf16[2,64,16,128]{3,2,1,0:T(8,128)(2,1)}, bf16[2,64,16,128]{3,2,1,0:T(8,128)(2,1)}, u32[]{:S(2)}, u32[]{:S(2)}) collective-permute-start(bf16[2,64,16,128]{3,2,1,0:T(8,128)(2,1)} %copy-done.35), channel_id=1, source_target_pairs={{0,20},{4,16},{8,28},{12,24},{16,4},{20,0},{24,12},{28,8},{1,21},{... | collective-permute-start | bytes 1572872 | tf_op jit(solution)/shard_map/ppermute | solution.py:418
  33.4 77.9 %collective-permute-start.16 = (bf16[2,64,16,128]{3,2,1,0:T(8,128)(2,1)}, bf16[2,64,16,128]{3,2,1,0:T(8,128)(2,1)}, u32[]{:S(2)}, u32[]{:S(2)}) collective-permute-start(bf16[2,64,16,128]{3,2,1,0:T(8,128)(2,1)} %copy-done.34), channel_id=1, source_target_pairs={{0,24},{4,28},{8,16},{12,20},{16,8},{20,12},{24,0},{28,4},{1,25},{... | collective-permute-start | bytes 1572872 | tf_op jit(solution)/shard_map/ppermute | solution.py:418
  36.5 79.3 %collective-permute-start.17 = (bf16[2,64,16,128]{3,2,1,0:T(8,128)(2,1)}, bf16[2,64,16,128]{3,2,1,0:T(8,128)(2,1)}, u32[]{:S(2)}, u32[]{:S(2)}) collective-permute-start(bf16[2,64,16,128]{3,2,1,0:T(8,128)(2,1)} %copy-done.33), channel_id=1, source_target_pairs={{0,28},{4,24},{8,20},{12,16},{16,12},{20,8},{24,4},{28,0},{1,29},{... | collective-permute-start | bytes 1572872 | tf_op jit(solution)/shard_map/ppermute | solution.py:418
  37.1 100.7 %collective-permute-start.18 = (bf16[2,64,16,128]{3,2,1,0:T(8,128)(2,1)}, bf16[2,64,16,128]{3,2,1,0:T(8,128)(2,1)}, u32[]{:S(2)}, u32[]{:S(2)}) collective-permute-start(bf16[2,64,16,128]{3,2,1,0:T(8,128)(2,1)} %copy-done.32), channel_id=1, source_target_pairs={{0,8},{4,12},{8,0},{12,4},{16,24},{20,28},{24,16},{28,20},{1,9},{5... | collective-permute-start | bytes 1572872 | tf_op jit(solution)/shard_map/ppermute | solution.py:418
  91.4 47.4 %collective-permute-start.19 = (bf16[2,64,16,128]{3,2,1,0:T(8,128)(2,1)}, bf16[2,64,16,128]{3,2,1,0:T(8,128)(2,1)}, u32[]{:S(2)}, u32[]{:S(2)}) collective-permute-start(bf16[2,64,16,128]{3,2,1,0:T(8,128)(2,1)} %copy-done.31), channel_id=1, source_target_pairs={{0,12},{4,8},{8,4},{12,0},{16,28},{20,24},{24,20},{28,16},{1,13},{... | collective-permute-start | bytes 1572872 | tf_op jit(solution)/shard_map/ppermute | solution.py:418
  101.1 40.3 %collective-permute-start.20 = (bf16[2,64,16,128]{3,2,1,0:T(8,128)(2,1)}, bf16[2,64,16,128]{3,2,1,0:T(8,128)(2,1)}, u32[]{:S(2)}, u32[]{:S(2)}) collective-permute-start(bf16[2,64,16,128]{3,2,1,0:T(8,128)(2,1)} %copy-done.30), channel_id=1, source_target_pairs={{0,4},{4,0},{8,12},{12,8},{16,20},{20,16},{24,28},{28,24},{1,5},{5... | collective-permute-start | bytes 1572872 | tf_op jit(solution)/shard_map/ppermute | solution.py:418
  111.3 128.0 %collective-permute-start = (bf16[2,64,16,128]{3,2,1,0:T(8,128)(2,1)}, bf16[2,64,16,128]{3,2,1,0:T(8,128)(2,1)}, u32[]{:S(2)}, u32[]{:S(2)}) collective-permute-start(bf16[2,64,16,128]{3,2,1,0:T(8,128)(2,1)} %get-tuple-element.53), channel_id=1, source_target_pairs={{0,16},{4,20},{8,24},{12,28},{16,0},{20,4},{24,8},{28,12},{1,17},{... | collective-permute-start | bytes 1572872 | tf_op jit(solution)/shard_map/ppermute | solution.py:418
  115.8 125.2 %collective-permute-start.1 = (bf16[2,64,16,128]{3,2,1,0:T(8,128)(2,1)}, bf16[2,64,16,128]{3,2,1,0:T(8,128)(2,1)}, u32[]{:S(2)}, u32[]{:S(2)}) collective-permute-start(bf16[2,64,16,128]{3,2,1,0:T(8,128)(2,1)} %get-tuple-element.54), channel_id=1, source_target_pairs={{0,20},{4,16},{8,28},{12,24},{16,4},{20,0},{24,12},{28,8},{1,21},{... | collective-permute-start | bytes 1572872 | tf_op jit(solution)/shard_map/ppermute | solution.py:418
  137.8 133.2 %collective-permute-start.2 = (bf16[2,64,16,128]{3,2,1,0:T(8,128)(2,1)}, bf16[2,64,16,128]{3,2,1,0:T(8,128)(2,1)}, u32[]{:S(2)}, u32[]{:S(2)}) collective-permute-start(bf16[2,64,16,128]{3,2,1,0:T(8,128)(2,1)} %get-tuple-element.55), channel_id=1, source_target_pairs={{0,24},{4,28},{8,16},{12,20},{16,8},{20,12},{24,0},{28,4},{1,25},{... | collective-permute-start | bytes 1572872 | tf_op jit(solution)/shard_map/ppermute | solution.py:418
  138.8 132.3 %collective-permute-start.3 = (bf16[2,64,16,128]{3,2,1,0:T(8,128)(2,1)}, bf16[2,64,16,128]{3,2,1,0:T(8,128)(2,1)}, u32[]{:S(2)}, u32[]{:S(2)}) collective-permute-start(bf16[2,64,16,128]{3,2,1,0:T(8,128)(2,1)} %get-tuple-element.56), channel_id=1, source_target_pairs={{0,28},{4,24},{8,20},{12,16},{16,12},{20,8},{24,4},{28,0},{1,29},{... | collective-permute-start | bytes 1572872 | tf_op jit(solution)/shard_map/ppermute | solution.py:418
  141.4 132.0 %collective-permute-start.4 = (bf16[2,64,16,128]{3,2,1,0:T(8,128)(2,1)}, bf16[2,64,16,128]{3,2,1,0:T(8,128)(2,1)}, u32[]{:S(2)}, u32[]{:S(2)}) collective-permute-start(bf16[2,64,16,128]{3,2,1,0:T(8,128)(2,1)} %get-tuple-element.57), channel_id=1, source_target_pairs={{0,8},{4,12},{8,0},{12,4},{16,24},{20,28},{24,16},{28,20},{1,9},{5... | collective-permute-start | bytes 1572872 | tf_op jit(solution)/shard_map/ppermute | solution.py:418
  206.8 166.3 %all-to-all-start.1 = ((bf16[4,4,32,64,128]{4,3,2,1,0:T(8,128)(2,1)}), bf16[4,4,32,64,128]{4,3,2,1,0:T(8,128)(2,1)}, u32[]{:S(2)}, u32[]{:S(2)}) async-start(bf16[4,4,32,64,128]{4,3,2,1,0:T(8,128)(2,1)} %copy-done.2), calls=%async_computation.1 | async-start | bytes 16777216 | tf_op jit(solution)/shard_map/all_to_all | solution.py:449
  239.3 35.0 %collective-permute-start.5 = (bf16[2,64,16,128]{3,2,1,0:T(8,128)(2,1)}, bf16[2,64,16,128]{3,2,1,0:T(8,128)(2,1)S(1)}, u32[]{:S(2)}, u32[]{:S(2)}) collective-permute-start(bf16[2,64,16,128]{3,2,1,0:T(8,128)(2,1)} %get-tuple-element.58), channel_id=1, source_target_pairs={{0,12},{4,8},{8,4},{12,0},{16,28},{20,24},{24,20},{28,16},{1,13},{... | collective-permute-start | bytes 1572872 | tf_op jit(solution)/shard_map/ppermute | solution.py:418
  241.1 36.2 %collective-permute-start.6 = (bf16[2,64,16,128]{3,2,1,0:T(8,128)(2,1)S(1)}, bf16[2,64,16,128]{3,2,1,0:T(8,128)(2,1)S(1)}, u32[]{:S(2)}, u32[]{:S(2)}) collective-permute-start(bf16[2,64,16,128]{3,2,1,0:T(8,128)(2,1)S(1)} %copy-done.17), channel_id=1, source_target_pairs={{0,4},{4,0},{8,12},{12,8},{16,20},{20,16},{24,28},{28,24},{1,5},{5... | collective-permute-start | bytes 1572872 | tf_op jit(solution)/shard_map/ppermute | solution.py:418
  271.1 59.7 %collective-permute-start.28 = (bf16[2,16,64,128]{3,2,1,0:T(8,128)(2,1)S(1)}, bf16[2,16,64,128]{3,2,1,0:T(8,128)(2,1)S(1)}, u32[]{:S(2)}, u32[]{:S(2)}) collective-permute-start(bf16[2,16,64,128]{3,2,1,0:T(8,128)(2,1)S(1)} %get-tuple-element.86), channel_id=1, source_target_pairs={{0,16},{4,20},{8,24},{12,28},{16,0},{20,4},{24,8},{28,12},{1,17},{... | collective-permute-start | bytes 1572872 | tf_op jit(solution)/shard_map/ppermute | solution.py:418
  271.1 70.8 %collective-permute-start.29 = (bf16[2,16,64,128]{3,2,1,0:T(8,128)(2,1)S(1)}, bf16[2,16,64,128]{3,2,1,0:T(8,128)(2,1)S(1)}, u32[]{:S(2)}, u32[]{:S(2)}) collective-permute-start(bf16[2,16,64,128]{3,2,1,0:T(8,128)(2,1)S(1)} %get-tuple-element.87), channel_id=1, source_target_pairs={{0,20},{4,16},{8,28},{12,24},{16,4},{20,0},{24,12},{28,8},{1,21},{... | collective-permute-start | bytes 1572872 | tf_op jit(solution)/shard_map/ppermute | solution.py:418
  273.4 84.1 %collective-permute-start.30 = (bf16[2,16,64,128]{3,2,1,0:T(8,128)(2,1)S(1)}, bf16[2,16,64,128]{3,2,1,0:T(8,128)(2,1)S(1)}, u32[]{:S(2)}, u32[]{:S(2)}) collective-permute-start(bf16[2,16,64,128]{3,2,1,0:T(8,128)(2,1)S(1)} %copy-done.29), channel_id=1, source_target_pairs={{0,24},{4,28},{8,16},{12,20},{16,8},{20,12},{24,0},{28,4},{1,25},{... | collective-permute-start | bytes 1572872 | tf_op jit(solution)/shard_map/ppermute | solution.py:418
  274.4 83.9 %collective-permute-start.31 = (bf16[2,16,64,128]{3,2,1,0:T(8,128)(2,1)S(1)}, bf16[2,16,64,128]{3,2,1,0:T(8,128)(2,1)S(1)}, u32[]{:S(2)}, u32[]{:S(2)}) collective-permute-start(bf16[2,16,64,128]{3,2,1,0:T(8,128)(2,1)S(1)} %copy-done.25), channel_id=1, source_target_pairs={{0,28},{4,24},{8,20},{12,16},{16,12},{20,8},{24,4},{28,0},{1,29},{... | collective-permute-start | bytes 1572872 | tf_op jit(solution)/shard_map/ppermute | solution.py:418
  277.3 92.7 %collective-permute-start.32 = (bf16[2,16,64,128]{3,2,1,0:T(8,128)(2,1)S(1)}, bf16[2,16,64,128]{3,2,1,0:T(8,128)(2,1)S(1)}, u32[]{:S(2)}, u32[]{:S(2)}) collective-permute-start(bf16[2,16,64,128]{3,2,1,0:T(8,128)(2,1)S(1)} %copy-done.23), channel_id=1, source_target_pairs={{0,8},{4,12},{8,0},{12,4},{16,24},{20,28},{24,16},{28,20},{1,9},{5... | collective-permute-start | bytes 1572872 | tf_op jit(solution)/shard_map/ppermute | solution.py:418
  330.7 41.8 %collective-permute-start.33 = (bf16[2,16,64,128]{3,2,1,0:T(8,128)(2,1)S(1)}, bf16[2,16,64,128]{3,2,1,0:T(8,128)(2,1)S(1)}, u32[]{:S(2)}, u32[]{:S(2)}) collective-permute-start(bf16[2,16,64,128]{3,2,1,0:T(8,128)(2,1)S(1)} %copy-done.21), channel_id=1, source_target_pairs={{0,12},{4,8},{8,4},{12,0},{16,28},{20,24},{24,20},{28,16},{1,13},{... | collective-permute-start | bytes 1572872 | tf_op jit(solution)/shard_map/ppermute | solution.py:418
  341.9 31.3 %collective-permute-start.34 = (bf16[2,16,64,128]{3,2,1,0:T(8,128)(2,1)S(1)}, bf16[2,16,64,128]{3,2,1,0:T(8,128)(2,1)S(1)}, u32[]{:S(2)}, u32[]{:S(2)}) collective-permute-start(bf16[2,16,64,128]{3,2,1,0:T(8,128)(2,1)S(1)} %copy-done.19), channel_id=1, source_target_pairs={{0,4},{4,0},{8,12},{12,8},{16,20},{20,16},{24,28},{28,24},{1,5},{5... | collective-permute-start | bytes 1572872 | tf_op jit(solution)/shard_map/ppermute | solution.py:418
  358.3 42.6 %collective-permute-start.21 = (bf16[1,16,64,128]{3,2,1,0:T(8,128)(2,1)}, bf16[1,16,64,128]{3,2,1,0:T(8,128)(2,1)}, u32[]{:S(2)}, u32[]{:S(2)}) collective-permute-start(bf16[1,16,64,128]{3,2,1,0:T(8,128)(2,1)} %get-tuple-element.79), channel_id=1, source_target_pairs={{0,16},{4,20},{8,24},{12,28},{16,0},{20,4},{24,8},{28,12},{1,17},{... | collective-permute-start | bytes 786440 | tf_op jit(solution)/shard_map/ppermute | solution.py:418
  358.3 44.7 %collective-permute-start.22 = (bf16[1,16,64,128]{3,2,1,0:T(8,128)(2,1)}, bf16[1,16,64,128]{3,2,1,0:T(8,128)(2,1)}, u32[]{:S(2)}, u32[]{:S(2)}) collective-permute-start(bf16[1,16,64,128]{3,2,1,0:T(8,128)(2,1)} %get-tuple-element.80), channel_id=1, source_target_pairs={{0,20},{4,16},{8,28},{12,24},{16,4},{20,0},{24,12},{28,8},{1,21},{... | collective-permute-start | bytes 786440 | tf_op jit(solution)/shard_map/ppermute | solution.py:418
  370.0 33.1 %collective-permute-start.23 = (bf16[1,16,64,128]{3,2,1,0:T(8,128)(2,1)}, bf16[1,16,64,128]{3,2,1,0:T(8,128)(2,1)}, u32[]{:S(2)}, u32[]{:S(2)}) collective-permute-start(bf16[1,16,64,128]{3,2,1,0:T(8,128)(2,1)} %get-tuple-element.81), channel_id=1, source_target_pairs={{0,24},{4,28},{8,16},{12,20},{16,8},{20,12},{24,0},{28,4},{1,25},{... | collective-permute-start | bytes 786440 | tf_op jit(solution)/shard_map/ppermute | solution.py:418
  372.6 32.1 %collective-permute-start.24 = (bf16[1,16,64,128]{3,2,1,0:T(8,128)(2,1)}, bf16[1,16,64,128]{3,2,1,0:T(8,128)(2,1)}, u32[]{:S(2)}, u32[]{:S(2)}) collective-permute-start(bf16[1,16,64,128]{3,2,1,0:T(8,128)(2,1)} %get-tuple-element.82), channel_id=1, source_target_pairs={{0,28},{4,24},{8,20},{12,16},{16,12},{20,8},{24,4},{28,0},{1,29},{... | collective-permute-start | bytes 786440 | tf_op jit(solution)/shard_map/ppermute | solution.py:418
  373.2 55.3 %collective-permute-start.25 = (bf16[1,16,64,128]{3,2,1,0:T(8,128)(2,1)}, bf16[1,16,64,128]{3,2,1,0:T(8,128)(2,1)}, u32[]{:S(2)}, u32[]{:S(2)}) collective-permute-start(bf16[1,16,64,128]{3,2,1,0:T(8,128)(2,1)} %get-tuple-element.83), channel_id=1, source_target_pairs={{0,8},{4,12},{8,0},{12,4},{16,24},{20,28},{24,16},{28,20},{1,9},{5... | collective-permute-start | bytes 786440 | tf_op jit(solution)/shard_map/ppermute | solution.py:418
  400.9 30.1 %collective-permute-start.26 = (bf16[1,16,64,128]{3,2,1,0:T(8,128)(2,1)S(1)}, bf16[1,16,64,128]{3,2,1,0:T(8,128)(2,1)S(1)}, u32[]{:S(2)}, u32[]{:S(2)}) collective-permute-start(bf16[1,16,64,128]{3,2,1,0:T(8,128)(2,1)S(1)} %copy-done.52), channel_id=1, source_target_pairs={{0,12},{4,8},{8,4},{12,0},{16,28},{20,24},{24,20},{28,16},{1,13},{... | collective-permute-start | bytes 786440 | tf_op jit(solution)/shard_map/ppermute | solution.py:418
  403.0 28.5 %collective-permute-start.27 = (bf16[1,16,64,128]{3,2,1,0:T(8,128)(2,1)S(1)}, bf16[1,16,64,128]{3,2,1,0:T(8,128)(2,1)S(1)}, u32[]{:S(2)}, u32[]{:S(2)}) collective-permute-start(bf16[1,16,64,128]{3,2,1,0:T(8,128)(2,1)S(1)} %copy-done.48), channel_id=1, source_target_pairs={{0,4},{4,0},{8,12},{12,8},{16,20},{20,16},{24,28},{28,24},{1,5},{5... | collective-permute-start | bytes 786440 | tf_op jit(solution)/shard_map/ppermute | solution.py:418
  403.0 28.5 %collective-permute-start.7 = (bf16[1,16,64,128]{3,2,1,0:T(8,128)(2,1)S(1)}, bf16[1,16,64,128]{3,2,1,0:T(8,128)(2,1)S(1)}, u32[]{:S(2)}, u32[]{:S(2)}) collective-permute-start(bf16[1,16,64,128]{3,2,1,0:T(8,128)(2,1)S(1)} %copy-done.54), channel_id=1, source_target_pairs={{0,16},{4,20},{8,24},{12,28},{16,0},{20,4},{24,8},{28,12},{1,17},{... | collective-permute-start | bytes 786440 | tf_op jit(solution)/shard_map/ppermute | solution.py:418
  404.7 29.1 %collective-permute-start.8 = (bf16[1,16,64,128]{3,2,1,0:T(8,128)(2,1)S(1)}, bf16[1,16,64,128]{3,2,1,0:T(8,128)(2,1)S(1)}, u32[]{:S(2)}, u32[]{:S(2)}) collective-permute-start(bf16[1,16,64,128]{3,2,1,0:T(8,128)(2,1)S(1)} %copy-done.50), channel_id=1, source_target_pairs={{0,20},{4,16},{8,28},{12,24},{16,4},{20,0},{24,12},{28,8},{1,21},{... | collective-permute-start | bytes 786440 | tf_op jit(solution)/shard_map/ppermute | solution.py:418
  (82 other events, 1306.0 us)

commit v2 on v1

v2 whole, which is shorter than its diff:
```python
import functools
import math

import jax
import jax.numpy as jnp
from jax import lax
from jax.experimental import pallas as pl
from jax.experimental.pallas import tpu as pltpu
from jax.sharding import PartitionSpec as P

MIB = 1024 * 1024
VMEM_BYTES = 62 * MIB
PLAN = {'early': 2,
 'order': 2,
 'last': 1,
 'corner': 'last1',
 'near': 'late0',
 'pins': {'pack1': [['early', 5]],
          'last1': [['side', -1], ['early', 4]],
          'dim2b': [['late', 2]],
          'late0': [['late', 6]],
          'dim2a': [['late', 1]],
          'last0': [['early', 7]]},
 'cost': {'pack0': 0.216,
          'pack1': 60,
          'rows': 21.6,
          'mix': 0.96,
          'last0': 0.324,
          'last1': 60,
          'dim1': 0.132,
          'dim2a': 25.92,
          'dim2b': 120,
          'late0': 120,
          'late1': 1.8,
          'late2': 0.162,
          'ffn0': 1.296,
          'ffn1': 3.6,
          'ffn2': 14.4,
          'ffn3': 36.0},
 'groups': [2]}
SPAN = 4.8
NORMAL = (
    0.147212786,
    -0.00633505354,
    0.000398642281,
    -2.65332237e-05,
    1.74432499e-06,
    -1.09393557e-07,
    5.93270033e-09,
    -2.75892574e-10,
    1.73565533e-11,
    -1.17650118e-12,
    3.52373652e-14,
)


def forward_rows(length, mode_count):
    grid_pos = jnp.arange(length, dtype=jnp.int32)[None, :]
    mode_location = jnp.arange(mode_count, dtype=jnp.int32)[:, None]
    phase = (grid_pos * mode_location % length).astype(jnp.float32) * (2.0 * math.pi / length)
    return jnp.concatenate([jnp.cos(phase), -jnp.sin(phase)], axis=0).astype(jnp.bfloat16)


def inverse_rows(length, mode_count):
    mode_location = jnp.arange(mode_count, dtype=jnp.int32)[:, None]
    grid_pos = jnp.arange(length, dtype=jnp.int32)[None, :]
    phase = (grid_pos * mode_location % length).astype(jnp.float32) * (2.0 * math.pi / length)
    factor = jnp.where(mode_location == 0, 1.0, 2.0).astype(jnp.float32) / length
    return jnp.concatenate(
        [factor * jnp.cos(phase), -factor * jnp.sin(phase)], axis=0
    ).astype(jnp.bfloat16)


def mix_kernel(*refs):
    count = len(refs) // 2
    for spec, out in zip(refs[:count], refs[count:]):
        channels = spec.shape[-1]
        for mode in range(spec.shape[1]):
            real = spec[0, mode].astype(jnp.float32).T
            imag = spec[1, mode].astype(jnp.float32).T
            upper = jnp.concatenate([real, -imag], axis=1)
            lower = jnp.concatenate([imag, real], axis=1)
            out[mode, :channels] = upper.astype(jnp.bfloat16)
            out[mode, channels:] = lower.astype(jnp.bfloat16)


def mix_rows(after, *specs):
    _, mode_count, channels, _ = specs[0].shape
    block = min(8, mode_count)
    kernel, token_specs, token = ordered(mix_kernel, after)
    return pl.pallas_call(
        kernel,
        grid=(mode_count // block,),
        in_specs=token_specs
        + [pl.BlockSpec((2, block, channels, channels), lambda g: (0, g, 0, 0))]
        * len(specs),
        out_specs=[pl.BlockSpec((block, 2 * channels, 2 * channels), lambda g: (g, 0, 0))]
        * len(specs),
        out_shape=[hbm(mode_count, 2 * channels, 2 * channels)] * len(specs),
        compiler_params=pltpu.CompilerParams(vmem_limit_bytes=VMEM_BYTES),
        cost_estimate=cost("mix", 0),
        name="mixing_matrices",
    )(*token, *in_hbm(specs))


def hbm(*shape):
    return pltpu.HBM(shape, jnp.bfloat16)


def in_hbm(arrays):
    return [pltpu.with_memory_space_constraint(array, pltpu.HBM) for array in arrays]


def cost(kernel, size):
    micros = PLAN["cost"].get(kernel, 3.0)
    return pl.CostEstimate(
        flops=int(micros * 1.15e9), bytes_accessed=int(size), transcendentals=0
    )


def ordered(kernel, after):
    if after is None:
        return kernel, [], []
    return (
        lambda _, *refs: kernel(*refs),
        [pl.BlockSpec(memory_space=pl.ANY)],
        in_hbm([after]),
    )


def mm(left, right, dims=(1, 0)):
    return lax.dot_general(
        left, right, (((dims[0],), (dims[1],)), ((), ())), preferred_element_type=jnp.float32
    )


def stack_rows(parts):
    if parts[0].shape[0] % 16 == 0:
        return jnp.concatenate(parts, axis=0)
    return jnp.concatenate([p.astype(jnp.float32) for p in parts], axis=0).astype(jnp.bfloat16)


def partners(ways):
    far = list(range(ways // 2, ways))
    near = list(range(1, ways // 2))
    if PLAN["order"] == 1:
        near.reverse()
    if PLAN["order"] == 2:
        far.reverse()
    return [0] + far + near


def pack_kernel(ways, me_ref, x_ref, *refs):
    outs, wide = refs[:ways], refs[ways]
    channels, rows, _, lanes = x_ref.shape
    wide[...] = x_ref[...].astype(jnp.float32).reshape(channels * rows * ways, lanes)
    for out, step in zip(outs, partners(ways)):
        picked = wide[pl.ds(me_ref[0] ^ step, channels * rows, stride=ways), :]
        out[...] = picked.reshape(channels, rows, lanes).astype(jnp.bfloat16)


def pack(kernel_name, field, first, count, ways, me, after):
    channels, rows, _, lanes = field.shape
    depth = min(16, channels)
    token_specs = [pl.BlockSpec(memory_space=pl.ANY)] * len(after)
    token = in_hbm(after)

    def kernel(me_ref, x_ref, *refs):
        pack_kernel(ways, me_ref, x_ref, *refs[len(token) :])

    return pl.pallas_call(
        kernel,
        grid_spec=pltpu.PrefetchScalarGridSpec(
            num_scalar_prefetch=1,
            grid=(count, channels // depth),
            in_specs=[
                pl.BlockSpec((depth, rows, ways, lanes), lambda k, g, me: (g, 0, first + k, 0))
            ]
            + token_specs,
            out_specs=[pl.BlockSpec((None, depth, rows, lanes), lambda k, g, me: (k, g, 0, 0))]
            * ways,
            scratch_shapes=[pltpu.VMEM((depth * rows * ways, lanes), jnp.float32)],
        ),
        out_shape=[hbm(count, channels, rows, lanes)] * ways,
        compiler_params=pltpu.CompilerParams(vmem_limit_bytes=VMEM_BYTES),
        cost_estimate=cost(kernel_name, 0),
        name="pack_columns",
    )(me, *in_hbm([field]), *token)


def side_kernel(ways, me_ref, *refs):
    for x_ref, out_ref in zip(refs[:ways], refs[-ways:]):
        out_ref[...] = x_ref[...]


def rows_first(field, ways, me, after):
    channels, rows, cols, lanes = field.shape
    across = rows // ways

    def rows_of(step):
        return pl.BlockSpec(
            (channels, None, cols, lanes), lambda r, me: (0, (me[1] ^ step) * across + r, 0, 0)
        )

    return pl.pallas_call(
        functools.partial(side_kernel, ways),
        grid_spec=pltpu.PrefetchScalarGridSpec(
            num_scalar_prefetch=1,
            grid=(across,),
            in_specs=[rows_of(step) for step in partners(ways)]
            + [pl.BlockSpec(memory_space=pl.ANY)],
            out_specs=[
                pl.BlockSpec((None, channels, cols, lanes), lambda r, me: (r, 0, 0, 0))
            ]
            * ways,
        ),
        out_shape=[hbm(across, channels, cols, lanes)] * ways,
        compiler_params=pltpu.CompilerParams(vmem_limit_bytes=VMEM_BYTES),
        cost_estimate=cost("rows", 0),
        name="rows_first",
    )(me, *in_hbm([field] * ways + [after]))


def mix_modes(mix_ref, spectra, mixed):
    mode_count, depth, _ = mix_ref.shape
    channels = depth // 2

    def one(mode, _):
        block = spectra[pl.ds(pl.multiple_of(mode * depth, depth), depth), :].astype(jnp.bfloat16)
        result = mm(mix_ref[mode], block)
        for part in range(2):
            mixed[pl.ds(part * mode_count + mode, channels, stride=2 * mode_count), :] = result[
                part * channels : (part + 1) * channels
            ]
        return 0

    lax.fori_loop(0, mode_count, one, 0, unroll=4)


def keep_spectra(spectra, result, channel, mode_count, channels, lanes):
    for at in range(2):
        for part in range(2):
            spectra[pl.ds(part * channels + channel + at, mode_count, stride=2 * channels), :] = (
                result[part * mode_count : (part + 1) * mode_count, at * lanes : (at + 1) * lanes]
            )


def mixed_pair(mixed, channel, coefs):
    start = pl.multiple_of(channel * coefs, 2 * coefs)
    return jnp.concatenate(
        [mixed[pl.ds(start, coefs), :], mixed[pl.ds(start + coefs, coefs), :]], axis=1
    ).astype(jnp.bfloat16)


def lines_kernel(ways, ft_ref, it_ref, mix_ref, *refs):
    pieces, outs = refs[:ways], refs[ways : 2 * ways]
    spectra, mixed, wide = refs[2 * ways :]
    channels, length, lanes = pieces[0].shape
    mode_count = mix_ref.shape[0]
    total = ways * length

    def forward(pair, _):
        channel = 2 * pair
        right = jnp.concatenate(
            [stack_rows([piece[channel + at] for piece in pieces]) for at in range(2)], axis=1
        )
        keep_spectra(spectra, mm(ft_ref[...], right), channel, mode_count, channels, lanes)
        return 0

    lax.fori_loop(0, channels // 2, forward, 0, unroll=4)
    mix_modes(mix_ref, spectra, mixed)

    def inverse(pair, _):
        channel = 2 * pair
        result = mm(it_ref[...], mixed_pair(mixed, channel, 2 * mode_count))
        for at in range(2):
            wide[pl.ds(channel + at, total, stride=channels), :] = result[
                :, at * lanes : (at + 1) * lanes
            ]
        return 0

    lax.fori_loop(0, channels // 2, inverse, 0, unroll=4)
    for step in range(ways):
        part = wide[pl.ds(step * length * channels, length * channels), :]
        outs[step][...] = part.reshape(length, channels, lanes).astype(jnp.bfloat16)


def along_lines(
    kernel_name, pieces, weights, order, begin, count, after=(), held=(), done=None, full=False
):
    ways = len(pieces)
    several, channels, length, lanes = pieces[0].shape
    mode_count = weights.shape[0]
    total = ways * length
    forward = forward_rows(total, mode_count).reshape(2 * mode_count, ways, length)
    forward = jnp.take(forward, order, axis=1).reshape(2 * mode_count, total)
    back = inverse_rows(total, mode_count).T.reshape(ways, length, 2 * mode_count)
    back = jnp.take(back, order, axis=0).reshape(total, 2 * mode_count)
    whole = lambda shape: pl.BlockSpec(shape, lambda g: (0,) * len(shape))
    elsewhere = pl.BlockSpec(memory_space=pl.ANY)
    put, number = (begin, several) if full else (0, count)
    kept = list(done or ()) + list(held)
    moved = 0 if done else ways
    idle = kept + list(after)
    last = len(idle) + 3 + 2 * ways
    return pl.pallas_call(
        lambda *refs: lines_kernel(ways, *refs[len(idle) : last], *refs[-3:]),
        grid=(count,),
        in_specs=[elsewhere] * len(idle)
        + [whole(forward.shape), whole(back.shape), whole(weights.shape)]
        + [pl.BlockSpec((None, channels, length, lanes), lambda g: (begin + g, 0, 0, 0))] * ways,
        out_specs=[
            pl.BlockSpec((None, length, channels, lanes), lambda g: (put + g, 0, 0, 0))
        ]
        * ways
        + [elsewhere] * len(held),
        out_shape=[hbm(number, length, channels, lanes)] * ways
        + [hbm(*array.shape) for array in held],
        input_output_aliases={at: moved + at for at in range(len(kept))},
        scratch_shapes=[
            pltpu.VMEM((2 * channels * mode_count, lanes), jnp.float32),
            pltpu.VMEM((2 * channels * mode_count, lanes), jnp.float32),
            pltpu.VMEM((total * channels, lanes), jnp.float32),
        ],
        compiler_params=pltpu.CompilerParams(vmem_limit_bytes=VMEM_BYTES),
        cost_estimate=cost(kernel_name, 0),
        name="line_branch",
    )(*in_hbm(idle), forward, back, *in_hbm([weights, *pieces]))


def last_kernel(ft_ref, it_ref, mix_ref, x_ref, out_ref, spectra, mixed, wide):
    channels, rows, cols, length = x_ref.shape
    mode_count = mix_ref.shape[0]
    cells = rows * cols

    def forward(pair, _):
        channel = 2 * pair
        right = jnp.concatenate(
            [x_ref[channel + at].reshape(cells, length) for at in range(2)], axis=0
        )
        keep_spectra(
            spectra, mm(ft_ref[...], right, (1, 1)), channel, mode_count, channels, cells
        )
        return 0

    lax.fori_loop(0, channels // 2, forward, 0, unroll=4)
    mix_modes(mix_ref, spectra, mixed)

    def inverse(pair, _):
        channel = 2 * pair
        result = mm(mixed_pair(mixed, channel, 2 * mode_count), it_ref[...], (0, 0))
        for at in range(2):
            wide[pl.ds(channel + at, cells, stride=channels), :] = result[
                at * cells : (at + 1) * cells
            ]
        return 0

    lax.fori_loop(0, channels // 2, inverse, 0, unroll=4)
    out_ref[...] = wide[...].reshape(rows, cols, channels, length).astype(jnp.bfloat16)


def last_branch(kernel_name, field, weights, part, parts, done, after, held=()):
    channels, rows, cols, length = field.shape
    mode_count = weights.shape[0]
    block = max(1, min(rows // parts, 128 // cols))
    steps = rows // block // parts
    forward, back = forward_rows(length, mode_count), inverse_rows(length, mode_count)
    whole = lambda shape: pl.BlockSpec(shape, lambda g: (0,) * len(shape))
    elsewhere = pl.BlockSpec(memory_space=pl.ANY)
    kept = ([] if done is None else [done]) + list(held)
    moved = 1 if done is None else 0
    idle = kept + list(after)
    return pl.pallas_call(
        lambda *refs: last_kernel(*refs[len(idle) : len(idle) + 5], *refs[-3:]),
        grid=(steps,),
        in_specs=[elsewhere] * len(idle)
        + [
            whole(forward.shape),
            whole(back.shape),
            whole(weights.shape),
            pl.BlockSpec(
                (channels, block, cols, length), lambda g: (0, part * steps + g, 0, 0)
            ),
        ],
        out_specs=[
            pl.BlockSpec((block, cols, channels, length), lambda g: (part * steps + g, 0, 0, 0))
        ]
        + [elsewhere] * len(held),
        out_shape=[hbm(rows, cols, channels, length)] + [hbm(*array.shape) for array in held],
        input_output_aliases={at: moved + at for at in range(len(kept))},
        scratch_shapes=[
            pltpu.VMEM((2 * channels * mode_count, block * cols), jnp.float32),
            pltpu.VMEM((2 * channels * mode_count, block * cols), jnp.float32),
            pltpu.VMEM((block * cols * channels, length), jnp.float32),
        ],
        compiler_params=pltpu.CompilerParams(vmem_limit_bytes=VMEM_BYTES),
        cost_estimate=cost(kernel_name, 0),
        name="last_branch",
    )(*in_hbm(idle), forward, back, *in_hbm([weights, field]))


def gelu(x):
    near = jnp.clip(x, -SPAN, SPAN)
    square = near * near - SPAN * SPAN / 2
    ratio = NORMAL[-1] * square + NORMAL[-2]
    for factor in NORMAL[-3::-1]:
        ratio = ratio * square + factor
    return x * (0.5 + near * ratio)


def cell_kernel(ways, col_ways, me_ref, x_ref, win_ref, wout_ref, bin_ref, bout_ref, *refs):
    first, second = refs[:ways], refs[ways : ways + col_ways]
    third = refs[ways + col_ways]
    out_ref, now, wide, before, hidden = refs[-5:]
    channels, rows, _, lanes = x_ref.shape
    steps = partners(ways)

    for place in range(col_ways):

        @pl.when(pl.program_id(0) == place)
        def _():
            now[...] = second[place][...]

    def one(row, _):
        for place in range(0, ways, 2):
            summed = []
            for at in range(2):
                col = me_ref[0] ^ steps[place + at]
                pair = first[place + at][row].astype(jnp.float32)
                pair = (pair + now[row, col].astype(jnp.float32)).astype(jnp.bfloat16)
                total = pair.astype(jnp.float32) + third[row, col].astype(jnp.float32)
                summed.append(total.astype(jnp.bfloat16))
            before[...] = mm(win_ref[...], jnp.concatenate(summed, axis=1))
            for start in range(0, before.shape[0], 32):
                units = pl.ds(start, 32)
                hidden[units] = gelu(before[units] + bin_ref[units]).astype(jnp.bfloat16)
            result = mm(wout_ref[...], hidden[...]) + bout_ref[...]
            for at in range(2):
                col = me_ref[0] ^ steps[place + at]
                wide[pl.ds(col, channels, stride=ways), :] = result[
                    :, at * lanes : (at + 1) * lanes
                ]
        total = wide[...].reshape(channels, ways, lanes) + x_ref[:, row].astype(jnp.float32)
        out_ref[:, row] = total.astype(jnp.bfloat16)
        return 0

    lax.fori_loop(0, rows, one, 0)


def cells(field, first, which, second, third, ffn, chunk, me, done, after):
    channels, rows, cols, lanes = field.shape
    ways, col_ways = len(first), len(second)
    across = rows // col_ways
    steps = partners(col_ways)

    def block(place, me):
        step = steps[0]
        for other in range(1, col_ways):
            step = jnp.where(place == other, steps[other], step)
        return me[1] ^ step

    whole = lambda shape: pl.BlockSpec(shape, lambda *_: (0,) * len(shape))
    tile = pl.BlockSpec(
        (channels, across, ways, lanes), lambda p, me: (0, block(p, me), chunk, 0)
    )
    in_specs = [tile] + [whole(w.shape) for w in ffn]
    in_specs += [
        pl.BlockSpec((None, across, channels, lanes), lambda p, me: (which, block(p, me), 0, 0))
    ] * ways
    in_specs += [
        pl.BlockSpec((across, ways, channels, lanes), lambda p, me: (0, chunk, 0, 0))
    ] * col_ways
    in_specs.append(
        pl.BlockSpec((across, ways, channels, lanes), lambda p, me: (block(p, me), chunk, 0, 0))
    )
    operands = [me, *in_hbm([field]), *ffn, *in_hbm([*first, *second, third])]
    aliases = {}
    if done is not None:
        aliases = {len(operands): 0}
    for array in (done, after):
        if array is not None:
            in_specs.append(pl.BlockSpec(memory_space=pl.ANY))
            operands += in_hbm([array])
    return pl.pallas_call(
        functools.partial(cell_kernel, ways, col_ways),
        grid_spec=pltpu.PrefetchScalarGridSpec(
            num_scalar_prefetch=1,
            grid=(col_ways,),
            in_specs=in_specs,
            out_specs=tile,
            scratch_shapes=[
                pltpu.VMEM((across, ways, channels, lanes), jnp.bfloat16),
                pltpu.VMEM((channels * ways, lanes), jnp.float32),
                pltpu.VMEM((ffn[0].shape[0], 2 * lanes), jnp.float32),
                pltpu.VMEM((ffn[0].shape[0], 2 * lanes), jnp.bfloat16),
            ],
        ),
        out_shape=hbm(*field.shape),
        input_output_aliases=aliases,
        compiler_params=pltpu.CompilerParams(vmem_limit_bytes=VMEM_BYTES),
        cost_estimate=cost(f"ffn{chunk}", 0),
        name="feed_forward",
    )(*operands)


def exchange(pieces, axis, skip=None, only=None):
    ways = len(pieces)
    got = list(pieces)
    for place, step in enumerate(partners(ways)):
        if step and place != skip and only in (None, place):
            pairs = [(at, at ^ step) for at in range(ways)]
            got[place] = lax.ppermute(pieces[place], axis, pairs)
    return got


def body(field, spec_first, spec_second, spec_third, ffn_in, ffn_out, bias_in, bias_out):
    channels, rows, cols, lanes = field.shape
    ways, col_ways = lax.axis_size("row"), lax.axis_size("col")
    row_me, col_me = lax.axis_index("row"), lax.axis_index("col")
    me = jnp.stack([row_me, col_me]).astype(jnp.int32)
    row_order = row_me ^ jnp.array(partners(ways))
    col_order = col_me ^ jnp.array(partners(col_ways))
    chunks = cols // ways
    across = rows // col_ways
    ffn = (ffn_in.T, ffn_out.T, bias_in[:, None], bias_out[:, None])

    early_count = max(1, min(PLAN["early"], chunks - 1))
    rest = chunks - early_count
    nearest = ways // 2 + 1
    seen = {}

    def pins(kernel):
        return [seen[name][place] for name, place in PLAN["pins"].get(kernel, ())]

    early = pack("pack0", field, 0, early_count, ways, me, [])
    seen["early"] = early_in = exchange(early, "row")
    late = pack("pack1", field, early_count, rest, ways, me, [early[0]] + pins("pack1"))
    seen["late"] = late_in = exchange(late, "row")
    corner = 2
    side = list(rows_first(field, col_ways, me, late[0]))
    seen["side"] = side_in = exchange(side, "col", skip=corner)
    first_mix, second_mix, third_mix = mix_rows(side[0], spec_first, spec_second, spec_third)

    def last(part, done, after):
        name = f"last{part}"
        held = [side[corner]] if PLAN["corner"] == name else []
        got = last_branch(name, field, third_mix, part, 2, done, after + pins(name), held)
        if held:
            side[corner] = got[1]
        return got[0]

    third = last(0, None, [])
    if PLAN["last"] == 0:
        third = last(1, third, [])
    side_in[corner] = exchange(side, "col", only=corner)[corner]
    parts = along_lines(
        "dim1", early_in, first_mix, row_order, 0, early_count, after=[third] + pins("dim1")
    )
    token = parts[0]
    if PLAN["last"] == 1:
        third = last(1, third, [token])
        token = third
    cut = across // 2
    second = along_lines(
        "dim2a", side_in, second_mix, col_order, 0, cut, [token] + pins("dim2a"), full=True
    )
    token = second[0]
    if PLAN["last"] == 2:
        third = last(1, third, [token])
        token = third
    second = along_lines(
        "dim2b",
        side_in,
        second_mix,
        col_order,
        cut,
        across - cut,
        [token] + pins("dim2b"),
        done=second,
        full=True,
    )
    token = second[0]
    seen["second"] = second_in = exchange(second, "col")
    if PLAN["last"] == 3:
        third = last(1, third, [token])
        token = third
    late_parts, near, begin = [], parts[nearest:], 0
    groups = PLAN["groups"] if sum(PLAN["groups"]) == rest else [1] * rest
    for at, count in enumerate(groups):
        name = f"late{at}"
        held = near if PLAN["near"] == name else []
        got = along_lines(
            name, late_in, first_mix, row_order, begin, count, [token] + pins(name), held=held
        )
        begin += count
        late_parts.append((got[:ways], count))
        near = got[ways:] if held else near
        token = got[0]
    if PLAN["last"] == 4:
        third = last(1, third, [token])
        token = third
    seen["back"] = back = exchange(parts[:nearest] + near, "row")
    first = [(back, which) for which in range(early_count)]
    for got, count in late_parts:
        back = exchange(got, "row")
        first += [(back, which) for which in range(count)]

    result = None
    for chunk, (branch, which) in enumerate(first):
        result = cells(
            field, branch, which, second_in, third, ffn, chunk, me, result, token
        )
        token = None
    return result


def solution(mesh):
    return jax.shard_map(
        body,
        mesh=mesh,
        in_specs=(P("grp", "row", "col", None), P(), P(), P(), P(), P(), P(), P()),
        out_specs=P("grp", "row", "col", None),
        check_vma=False,
    )
```

time: 475 us -> 519 us (1.093)
  Pallas kernels: 203 us -> 299 us
  local copies, waits for them, and re-layouts: 63.5 us -> 10.8 us
  waiting for transfers between devices: 117 us -> 98.4 us
  starting transfers between devices: 88.6 us -> 105 us
    pallas_call x11, Pallas kernels: 192 us -> 278 us  [the longest x4 142 us: cells(): pl.pallas_call(functools.partial(cell_kernel, ways, col_ways), grid_spec=...]
    unnamed x155 -> x34, local copies, waits for them, and re-layouts: 61.9 us -> 5.56 us
    ppermute x35 -> x34, starting transfers between devices: 76.8 us -> 105 us  [exchange(): got[place] = lax.ppermute(pieces[place], axis, pairs)]
    ppermute x35 -> x34, waiting for transfers between devices: 117 us -> 98.4 us  [exchange(): got[place] = lax.ppermute(pieces[place], axis, pairs)]
    all_to_all x2 -> x0, starting transfers between devices: 11.8 us -> none  [the longest x1 5.92 us: body(): second = lax.all_to_all(second, 'col', split_axis=0, concat_axis=0)]
    pallas_call x2, Pallas kernels: 8.73 us -> 16.3 us  [pack(): pl.pallas_call(kernel, grid_spec=pltpu.PrefetchScalarGridSpec(num_scalar_...]
  transfers between devices with their start and end apart: 37 -> 34, of which waited for: 5 -> 8; matrix products, arithmetic and copies ran while one was open for 1% -> 2% of each run, Pallas kernels for 37% -> 42%
where the time goes in v2:
time: 519 us
  Pallas kernels  299 us (58%)
  starting transfers between devices  105 us (20%)
  waiting for transfers between devices  98.4 us (19%)
  local copies, waits for them, and re-layouts  10.8 us (2%)
    pallas_call x4, Pallas kernels, cells(): pl.pallas_call(functools.partial(cell_kernel, ways, col_ways), grid_spec=...  142 us
    ppermute x34, starting transfers between devices, exchange(): got[place] = lax.ppermute(pieces[place], axis, pairs)  105 us
    ppermute x34, waiting for transfers between devices, exchange(): got[place] = lax.ppermute(pieces[place], axis, pairs)  98.4 us
    pallas_call x4, Pallas kernels, along_lines(): pl.pallas_call(lambda *refs: lines_kernel(ways, *refs[len(idle):last], *r...  83 us
    pallas_call x2, Pallas kernels, last_branch(): pl.pallas_call(lambda *refs: last_kernel(*refs[len(idle):len(idle) + 5],...  44.8 us
    pallas_call x2, Pallas kernels, pack(): pl.pallas_call(kernel, grid_spec=pltpu.PrefetchScalarGridSpec(num_scalar_...  16.3 us
  transfers between devices with their start and end apart: 34, of which 8 were waited for; matrix products, arithmetic and copies ran while one was open for 2% of the time, Pallas kernels for 42%

profile of v2, /device:TPU:0, one launch (start us, length us, event | category | flops | bytes accessed | tf_op | source)
XLA Modules:
  0.0 518.5 jit_solution(7841931046020552468)
XLA Ops:
  0.6 8.2 %pack_columns.2 = (bf16[2,64,16,128]{3,2,1,0:T(8,128)(2,1)}, bf16[2,64,16,128]{3,2,1,0:T(8,128)(2,1)}, bf16[2,64,16,128]{3,2,1,0:T(8,128)(2,1)}, bf16[2,64,16,12...) custom-call(s32[2]{0:T(128)} %pad_add_fusion.me_ref, ...), custom_call_target="tpu_custom_call" | custom-call | flops 248400000 | tf_op jit(solution)/shard_map/pack_columns/pallas_call | solution.py:171
  9.3 2.7 collective-permute-start
  12.0 2.6 collective-permute-start.5
  16.6 8.1 %pack_columns.3 = (bf16[2,64,16,128]{3,2,1,0:T(8,128)(2,1)}, bf16[2,64,16,128]{3,2,1,0:T(8,128)(2,1)}, bf16[2,64,16,128]{3,2,1,0:T(8,128)(2,1)}, bf16[2,64,16,12...) custom-call(s32[2]{0:T(128)} %pad_add_fusion.me_ref, ...), custom_call_target="tpu_custom_call" | custom-call | flops 69000003584 | tf_op jit(solution)/shard_map/pack_columns/pallas_call | solution.py:171
  24.7 7.9 %rows_first.1 = (bf16[4,64,32,128]{3,2,1,0:T(8,128)(2,1)}, bf16[4,64,32,128]{3,2,1,0:T(8,128)(2,1)}, bf16[4,64,32,128]{3,2,1,0:T(8,128)(2,1)}, bf16[4,64,32,128]{3,2,1,0:T(8,128)(2,1)}) custom-call(s32[2]{0:T(128)} %pad_add_fusion.me_ref, bf16[64,16,32,128]{3,2,1,0:T(8,128)(2,1)} %x_ref.11, bf16[64,16,32,128]{3,2,1,0:T(8,128)(2,1)} %x_ref.11, ...), custom_call_target="tpu_custom_call" | custom-call | flops 24839999488 | tf_op jit(solution)/shard_map/rows_first/pallas_call | solution.py:205
  38.7 3.3 collective-permute-start.3
  42.0 19.6 %collective-permute-done.5.refs_8_.refs_4_ = bf16[2,64,16,128]{3,2,1,0:T(8,128)(2,1)S(1)} collective-permute-done((bf16[2,64,16,128]{3,2,1,0:T(8,128)(2,1)}, bf16[2,64,16,128]{3,2,1,0:T(8,128)(2,1)S(1)}, u32[]{:S(2)}, u32[]{:S(2)}) %collective-permute-start.5) | collective-permute-done | bytes 524320 | tf_op jit(solution)/shard_map/ppermute | solution.py:512
  61.6 22.2 %collective-permute-start.6 = (bf16[2,64,16,128]{3,2,1,0:T(8,128)(2,1)}, bf16[2,64,16,128]{3,2,1,0:T(8,128)(2,1)}, u32[]{:S(2)}, u32[]{:S(2)}) collective-permute-start(bf16[2,64,16,128]{3,2,1,0:T(8,128)(2,1)} %get-tuple-element.71), channel_id=1, source_target_pairs={{0,8},{4,12},{8,0},{12,4},{16,24},{20,28},{24,16},{28,20},{1,9},{5... | collective-permute-start | bytes 1572872 | tf_op jit(solution)/shard_map/ppermute | solution.py:512
  87.2 5.0 mixing_matrices.1
  92.2 22.4 %last_branch.2.refs_0_ = bf16[16,32,64,128]{3,2,1,0:T(8,128)(2,1)} custom-call(bf16[2,64,16,128]{3,2,1,0:T(8,128)(2,1)} %copy-done.4, bf16[64,128]{1,0:T(8,128)(2,1)} %pad_maximum_fusion.2.refs_1_.refs_5_, bf16[64,128]{1,0:T(8,128)(2,1)} %get-tuple-element.116.refs_2_.refs_6_, bf16[32,128,128]{2,1,0:T(8,128)(2,1)} %get-tuple-element.65.refs_3_.refs_7_, ...), custom_call_target="tpu_custom_call" | custom-call | flops 372600000 | tf_op jit(solution)/shard_map/last_branch/pallas_call | solution.py:373
  114.6 2.5 collective-permute-start.9
  120.7 20.9 %line_branch.4 = (bf16[2,16,64,128]{3,2,1,0:T(8,128)(2,1)}, bf16[2,16,64,128]{3,2,1,0:T(8,128)(2,1)}, bf16[2,16,64,128]{3,2,1,0:T(8,128)(2,1)}, bf16[2,16,64,128...) custom-call(bf16[16,32,64,128]{3,2,1,0:T(8,128)(2,1)} %last_branch.2, ...), custom_call_target="tpu_custom_call" | custom-call | flops 151800000 | tf_op jit(solution)/shard_map/line_branch/pallas_call | solution.py:306
  143.2 22.4 %last_branch.3 = (bf16[16,32,64,128]{3,2,1,0:T(8,128)(2,1)}, bf16[4,64,32,128]{3,2,1,0:T(8,128)(2,1)}) custom-call(bf16[16,32,64,128]{3,2,1,0:T(8,128)(2,1)} %last_branch.2.refs_0_, bf16[4,64,32,128]{3,2,1,0:T(8,128)(2,1)} %get-tuple-element.75.refs_1_, ...), custom_call_target="tpu_custom_call", output_to_operand_aliasing={{0}: (0, {}), {1}: (1, {})} | custom-call | flops 69000003584 | tf_op jit(solution)/shard_map/last_branch/pallas_call | solution.py:373
  167.3 20.7 %line_branch.5 = (bf16[4,32,64,128]{3,2,1,0:T(8,128)(2,1)}, bf16[4,32,64,128]{3,2,1,0:T(8,128)(2,1)}, bf16[4,32,64,128]{3,2,1,0:T(8,128)(2,1)}, bf16[4,32,64,128]{3,2,1,0:T(8,128)(2,1)}) custom-call(bf16[16,32,64,128]{3,2,1,0:T(8,128)(2,1)} %get-tuple-element.78.refs_0_.refs_12_, bf16[2,64,16,128]{3,2,1,0:T(8,128)(2,1)} %collective-permute-done.8.refs_1_.refs_9_, ...), custom_call_target="tpu_custom_call" | custom-call | flops 29808001024 | tf_op jit(solution)/shard_map/line_branch/pallas_call | solution.py:306
  188.0 3.2 copy.45.refs_0_
  193.2 2.5 collective-permute-start.27
  195.7 20.7 %line_branch.6 = (bf16[4,32,64,128]{3,2,1,0:T(8,128)(2,1)}, bf16[4,32,64,128]{3,2,1,0:T(8,128)(2,1)}, bf16[4,32,64,128]{3,2,1,0:T(8,128)(2,1)}, bf16[4,32,64,128]{3,2,1,0:T(8,128)(2,1)}) custom-call(bf16[4,32,64,128]{3,2,1,0:T(8,128)(2,1)} %copy.45.refs_0_, ...), custom_call_target="tpu_custom_call", output_to_operand_aliasing={{0}: (0, {}), {1}: (1, {}), {2}: (2, {}), {3}: (3, {})} | custom-call | flops 138000007168 | tf_op jit(solution)/shard_map/line_branch/pallas_call | solution.py:306
  217.8 15.0 %collective-permute-done.14.refs_12_ = bf16[2,64,16,128]{3,2,1,0:T(8,128)(2,1)} collective-permute-done((bf16[2,64,16,128]{3,2,1,0:T(8,128)(2,1)}, bf16[2,64,16,128]{3,2,1,0:T(8,128)(2,1)}, u32[]{:S(2)}, u32[]{:S(2)}) %collective-permute-start.14) | collective-permute-done | bytes 524320 | tf_op jit(solution)/shard_map/ppermute | solution.py:512
  233.3 10.1 %collective-permute-done.16.refs_15_ = bf16[2,64,16,128]{3,2,1,0:T(8,128)(2,1)} collective-permute-done((bf16[2,64,16,128]{3,2,1,0:T(8,128)(2,1)}, bf16[2,64,16,128]{3,2,1,0:T(8,128)(2,1)}, u32[]{:S(2)}, u32[]{:S(2)}) %collective-permute-start.16) | collective-permute-done | bytes 524320 | tf_op jit(solution)/shard_map/ppermute | solution.py:512
  244.5 20.8 %line_branch.7 = (bf16[2,16,64,128]{3,2,1,0:T(8,128)(2,1)}, bf16[2,16,64,128]{3,2,1,0:T(8,128)(2,1)}, bf16[2,16,64,128]{3,2,1,0:T(8,128)(2,1)}, bf16[2,16,64,128...) custom-call(bf16[2,16,64,128]{3,2,1,0:T(8,128)(2,1)} %get-tuple-elem, ...), custom_call_target="tpu_custom_call", output_to_operand_aliasing={{8}: (0, {}), {9}: (1, {}), {10}: (2, {})} | custom-call | flops 138000007168 | tf_op jit(solution)/shard_map/line_branch/pallas_call | solution.py:306
  265.3 9.9 %collective-permute-start.30 = (bf16[2,16,64,128]{3,2,1,0:T(8,128)(2,1)}, bf16[2,16,64,128]{3,2,1,0:T(8,128)(2,1)S(1)}, u32[]{:S(2)}, u32[]{:S(2)}) collective-permute-start(bf16[2,16,64,128]{3,2,1,0:T(8,128)(2,1)} %get-tuple-element.107), channel_id=1, source_target_pairs={{0,16},{4,20},{8,24},{12,28},{16,0},{20,4},{24,8},{28,12},{1,17},{... | collective-permute-start | bytes 1572872 | tf_op jit(solution)/shard_map/ppermute | solution.py:512
  275.2 12.6 %collective-permute-done.29.refs_3_ = bf16[2,16,64,128]{3,2,1,0:T(8,128)(2,1)S(1)} collective-permute-done((bf16[2,16,64,128]{3,2,1,0:T(8,128)(2,1)}, bf16[2,16,64,128]{3,2,1,0:T(8,128)(2,1)S(1)}, u32[]{:S(2)}, u32[]{:S(2)}) %collective-permute-start.29) | collective-permute-done | bytes 524320 | tf_op jit(solution)/shard_map/ppermute | solution.py:512
  288.7 10.8 %collective-permute-done.30.refs_4_ = bf16[2,16,64,128]{3,2,1,0:T(8,128)(2,1)S(1)} collective-permute-done((bf16[2,16,64,128]{3,2,1,0:T(8,128)(2,1)}, bf16[2,16,64,128]{3,2,1,0:T(8,128)(2,1)S(1)}, u32[]{:S(2)}, u32[]{:S(2)}) %collective-permute-start.30) | collective-permute-done | bytes 524320 | tf_op jit(solution)/shard_map/ppermute | solution.py:512
  300.5 14.3 %collective-permute-done.32.refs_6_ = bf16[2,16,64,128]{3,2,1,0:T(8,128)(2,1)} collective-permute-done((bf16[2,16,64,128]{3,2,1,0:T(8,128)(2,1)}, bf16[2,16,64,128]{3,2,1,0:T(8,128)(2,1)}, u32[]{:S(2)}, u32[]{:S(2)}) %collective-permute-start.32) | collective-permute-done | bytes 524320 | tf_op jit(solution)/shard_map/ppermute | solution.py:512
  314.7 9.7 %collective-permute-done.33.refs_7_ = bf16[2,16,64,128]{3,2,1,0:T(8,128)(2,1)} collective-permute-done((bf16[2,16,64,128]{3,2,1,0:T(8,128)(2,1)}, bf16[2,16,64,128]{3,2,1,0:T(8,128)(2,1)}, u32[]{:S(2)}, u32[]{:S(2)}) %collective-permute-start.33) | collective-permute-done | bytes 524320 | tf_op jit(solution)/shard_map/ppermute | solution.py:512
  327.3 6.3 %collective-permute-done.17.refs_1_ = bf16[2,16,64,128]{3,2,1,0:T(8,128)(2,1)} collective-permute-done((bf16[2,16,64,128]{3,2,1,0:T(8,128)(2,1)}, bf16[2,16,64,128]{3,2,1,0:T(8,128)(2,1)}, u32[]{:S(2)}, u32[]{:S(2)}) %collective-permute-start.17) | collective-permute-done | bytes 524320 | tf_op jit(solution)/shard_map/ppermute | solution.py:512
  333.6 17.7 %collective-permute-start.19 = (bf16[2,16,64,128]{3,2,1,0:T(8,128)(2,1)}, bf16[2,16,64,128]{3,2,1,0:T(8,128)(2,1)}, u32[]{:S(2)}, u32[]{:S(2)}) collective-permute-start(bf16[2,16,64,128]{3,2,1,0:T(8,128)(2,1)} %get-tuple-element.96), channel_id=1, source_target_pairs={{0,20},{4,16},{8,28},{12,24},{16,4},{20,0},{24,12},{28,8},{1,21},{... | collective-permute-start | bytes 1572872 | tf_op jit(solution)/shard_map/ppermute | solution.py:512
  351.3 22.7 %collective-permute-start.20 = (bf16[2,16,64,128]{3,2,1,0:T(8,128)(2,1)}, bf16[2,16,64,128]{3,2,1,0:T(8,128)(2,1)}, u32[]{:S(2)}, u32[]{:S(2)}) collective-permute-start(bf16[2,16,64,128]{3,2,1,0:T(8,128)(2,1)} %get-tuple-element.97), channel_id=1, source_target_pairs={{0,16},{4,20},{8,24},{12,28},{16,0},{20,4},{24,8},{28,12},{1,17},{... | collective-permute-start | bytes 1572872 | tf_op jit(solution)/shard_map/ppermute | solution.py:512
  375.9 35.6 %feed_forward.4.refs_13_ = bf16[64,16,32,128]{3,2,1,0:T(8,128)(2,1)} custom-call(s32[2]{0:T(128)} %pad_add_fusion.me_ref, bf16[64,16,32,128]{3,2,1,0:T(8,128)(2,1)} %x_ref.11, bf16[256,64]{1,0:T(8,128)(2,1)} %bitcast.18, bf16[64,256]{1,0:T(8,128)(2,1)} %bitcast.24, f32[256,1]{1,0:T(8,128)} %copy.41.bin_ref, f32[64,1]{1,0:T(8,128)} %copy.42.bout_ref, ...), custom_call_target="tpu_custom_call" | custom-call | flops 1490400000 | tf_op jit(solution)/shard_map/feed_forward/pallas_call | solution.py:484
  411.5 35.6 %feed_forward.5.refs_13_ = bf16[64,16,32,128]{3,2,1,0:T(8,128)(2,1)} custom-call(s32[2]{0:T(128)} %pad_add_fusion.me_ref, bf16[64,16,32,128]{3,2,1,0:T(8,128)(2,1)} %x_ref.11, bf16[256,64]{1,0:T(8,128)(2,1)} %bitcast.19, bf16[64,256]{1,0:T(8,128)(2,1)} %bitcast.25, f32[256,1]{1,0:T(8,128)} %copy.41.bin_ref, ...), custom_call_target="tpu_custom_call", output_to_operand_aliasing={{}: (19, {})} | custom-call | flops 4140000000 | tf_op jit(solution)/shard_map/feed_forward/pallas_call | solution.py:484
  447.1 35.6 %feed_forward.6.refs_13_ = bf16[64,16,32,128]{3,2,1,0:T(8,128)(2,1)} custom-call(s32[2]{0:T(128)} %pad_add_fusion.me_ref, bf16[64,16,32,128]{3,2,1,0:T(8,128)(2,1)} %x_ref.11, bf16[256,64]{1,0:T(8,128)(2,1)} %bitcast.20, bf16[64,256]{1,0:T(8,128)(2,1)} %bitcast.26, f32[256,1]{1,0:T(8,128)} %copy.41.bin_ref, ...), custom_call_target="tpu_custom_call", output_to_operand_aliasing={{}: (19, {})} | custom-call | flops 16560000000 | tf_op jit(solution)/shard_map/feed_forward/pallas_call | solution.py:484
  482.7 35.6 %feed_forward.7 = bf16[64,16,32,128]{3,2,1,0:T(8,128)(2,1)} custom-call(s32[2]{0:T(128)} %pad_add_fusion.me_ref, bf16[64,16,32,128]{3,2,1,0:T(8,128)(2,1)} %x_ref.11, bf16[256,64]{1,0:T(8,128)(2,1)} %bitcast.21, bf16[64,256]{1,0:T(8,128)(2,1)} %bitcast.27, f32[256,1]{1,0:T(8,128)} %copy.41.bin_ref, ...), custom_call_target="tpu_custom_call", output_to_operand_aliasing={{}: (19, {})} | custom-call | flops 41400000512 | tf_op jit(solution)/shard_map/feed_forward/pallas_call | solution.py:484
  (114 shorter events, 31.1 us)
Async XLA Ops:
  9.3 29.4 %collective-permute-start = (bf16[2,64,16,128]{3,2,1,0:T(8,128)(2,1)}, bf16[2,64,16,128]{3,2,1,0:T(8,128)(2,1)S(1)}, u32[]{:S(2)}, u32[]{:S(2)}) collective-permute-start(bf16[2,64,16,128]{3,2,1,0:T(8,128)(2,1)} %get-tuple-element.60), channel_id=1, source_target_pairs={{0,12},{4,8},{8,4},{12,0},{16,28},{20,24},{24,20},{28,16},{1,13},{... | collective-permute-start | bytes 1572872 | tf_op jit(solution)/shard_map/ppermute | solution.py:512
  12.0 49.6 %collective-permute-start.5 = (bf16[2,64,16,128]{3,2,1,0:T(8,128)(2,1)}, bf16[2,64,16,128]{3,2,1,0:T(8,128)(2,1)S(1)}, u32[]{:S(2)}, u32[]{:S(2)}) collective-permute-start(bf16[2,64,16,128]{3,2,1,0:T(8,128)(2,1)} %get-tuple-element.70), channel_id=1, source_target_pairs={{0,16},{4,20},{8,24},{12,28},{16,0},{20,4},{24,8},{28,12},{1,17},{... | collective-permute-start | bytes 1572872 | tf_op jit(solution)/shard_map/ppermute | solution.py:512
  14.6 47.1 %collective-permute-start.2 = (bf16[2,64,16,128]{3,2,1,0:T(8,128)(2,1)}, bf16[2,64,16,128]{3,2,1,0:T(8,128)(2,1)}, u32[]{:S(2)}, u32[]{:S(2)}) collective-permute-start(bf16[2,64,16,128]{3,2,1,0:T(8,128)(2,1)} %get-tuple-element.67), channel_id=1, source_target_pairs={{0,28},{4,24},{8,20},{12,16},{16,12},{20,8},{24,4},{28,0},{1,29},{... | collective-permute-start | bytes 1572872 | tf_op jit(solution)/shard_map/ppermute | solution.py:512
  32.6 109.0 %collective-permute-start.10 = (bf16[4,64,32,128]{3,2,1,0:T(8,128)(2,1)}, bf16[4,64,32,128]{3,2,1,0:T(8,128)(2,1)}, u32[]{:S(2)}, u32[]{:S(2)}) collective-permute-start(bf16[4,64,32,128]{3,2,1,0:T(8,128)(2,1)} %get-tuple-element.75.refs_1_), channel_id=1, source_target_pairs={{0,2},{1,3},{2,0},{3,1},{4,6},{5,7},{6,4},{7,5},{8,10},{9,11},{10,... | collective-permute-start | bytes 6291464 | tf_op jit(solution)/shard_map/ppermute | solution.py:512
  34.1 107.6 %collective-permute-start.7 = (bf16[4,64,32,128]{3,2,1,0:T(8,128)(2,1)}, bf16[4,64,32,128]{3,2,1,0:T(8,128)(2,1)}, u32[]{:S(2)}, u32[]{:S(2)}) collective-permute-start(bf16[4,64,32,128]{3,2,1,0:T(8,128)(2,1)} %get-tuple-element.77), channel_id=1, source_target_pairs={{0,1},{1,0},{2,3},{3,2},{4,5},{5,4},{6,7},{7,6},{8,9},{9,8},{10,11... | collective-permute-start | bytes 6291464 | tf_op jit(solution)/shard_map/ppermute | solution.py:512
  38.7 75.9 %collective-permute-start.3 = (bf16[2,64,16,128]{3,2,1,0:T(8,128)(2,1)}, bf16[2,64,16,128]{3,2,1,0:T(8,128)(2,1)S(1)}, u32[]{:S(2)}, u32[]{:S(2)}) collective-permute-start(bf16[2,64,16,128]{3,2,1,0:T(8,128)(2,1)} %get-tuple-element.68), channel_id=1, source_target_pairs={{0,24},{4,28},{8,16},{12,20},{16,8},{20,12},{24,0},{28,4},{1,25},{... | collective-permute-start | bytes 1572872 | tf_op jit(solution)/shard_map/ppermute | solution.py:512
  61.6 55.5 %collective-permute-start.4 = (bf16[2,64,16,128]{3,2,1,0:T(8,128)(2,1)}, bf16[2,64,16,128]{3,2,1,0:T(8,128)(2,1)}, u32[]{:S(2)}, u32[]{:S(2)}) collective-permute-start(bf16[2,64,16,128]{3,2,1,0:T(8,128)(2,1)} %get-tuple-element.69), channel_id=1, source_target_pairs={{0,20},{4,16},{8,28},{12,24},{16,4},{20,0},{24,12},{28,8},{1,21},{... | collective-permute-start | bytes 1572872 | tf_op jit(solution)/shard_map/ppermute | solution.py:512
  61.6 57.7 %collective-permute-start.6 = (bf16[2,64,16,128]{3,2,1,0:T(8,128)(2,1)}, bf16[2,64,16,128]{3,2,1,0:T(8,128)(2,1)}, u32[]{:S(2)}, u32[]{:S(2)}) collective-permute-start(bf16[2,64,16,128]{3,2,1,0:T(8,128)(2,1)} %get-tuple-element.71), channel_id=1, source_target_pairs={{0,8},{4,12},{8,0},{12,4},{16,24},{20,28},{24,16},{28,20},{1,9},{5... | collective-permute-start | bytes 1572872 | tf_op jit(solution)/shard_map/ppermute | solution.py:512
  114.6 52.5 %collective-permute-start.9 = (bf16[4,64,32,128]{3,2,1,0:T(8,128)(2,1)}, bf16[4,64,32,128]{3,2,1,0:T(8,128)(2,1)}, u32[]{:S(2)}, u32[]{:S(2)}) collective-permute-start(bf16[4,64,32,128]{3,2,1,0:T(8,128)(2,1)} %get-tuple-element.81), channel_id=1, source_target_pairs={{0,3},{1,2},{2,1},{3,0},{4,7},{5,6},{6,5},{7,4},{8,11},{9,10},{10,... | collective-permute-start | bytes 6291464 | tf_op jit(solution)/shard_map/ppermute | solution.py:512
  117.1 48.5 %collective-permute-start.8 = (bf16[2,64,16,128]{3,2,1,0:T(8,128)(2,1)}, bf16[2,64,16,128]{3,2,1,0:T(8,128)(2,1)}, u32[]{:S(2)}, u32[]{:S(2)}) collective-permute-start(bf16[2,64,16,128]{3,2,1,0:T(8,128)(2,1)} %get-tuple-element.79), channel_id=1, source_target_pairs={{0,28},{4,24},{8,20},{12,16},{16,12},{20,8},{24,4},{28,0},{1,29},{... | collective-permute-start | bytes 1572872 | tf_op jit(solution)/shard_map/ppermute | solution.py:512
  119.4 71.8 %collective-permute-start.11 = (bf16[2,64,16,128]{3,2,1,0:T(8,128)(2,1)S(1)}, bf16[2,64,16,128]{3,2,1,0:T(8,128)(2,1)}, u32[]{:S(2)}, u32[]{:S(2)}) collective-permute-start(bf16[2,64,16,128]{3,2,1,0:T(8,128)(2,1)S(1)} %copy-done.14), channel_id=1, source_target_pairs={{0,24},{4,28},{8,16},{12,20},{16,8},{20,12},{24,0},{28,4},{1,25},{... | collective-permute-start | bytes 1572872 | tf_op jit(solution)/shard_map/ppermute | solution.py:512
  141.6 50.8 %collective-permute-start.12 = (bf16[2,64,16,128]{3,2,1,0:T(8,128)(2,1)S(1)}, bf16[2,64,16,128]{3,2,1,0:T(8,128)(2,1)S(1)}, u32[]{:S(2)}, u32[]{:S(2)}) collective-permute-start(bf16[2,64,16,128]{3,2,1,0:T(8,128)(2,1)S(1)} %copy-done.13), channel_id=1, source_target_pairs={{0,8},{4,12},{8,0},{12,4},{16,24},{20,28},{24,16},{28,20},{1,9},{5... | collective-permute-start | bytes 1572872 | tf_op jit(solution)/shard_map/ppermute | solution.py:512
  141.7 74.7 %collective-permute-start.13 = (bf16[2,64,16,128]{3,2,1,0:T(8,128)(2,1)}, bf16[2,64,16,128]{3,2,1,0:T(8,128)(2,1)}, u32[]{:S(2)}, u32[]{:S(2)}) collective-permute-start(bf16[2,64,16,128]{3,2,1,0:T(8,128)(2,1)} %get-tuple-element.89), channel_id=1, source_target_pairs={{0,20},{4,16},{8,28},{12,24},{16,4},{20,0},{24,12},{28,8},{1,21},{... | collective-permute-start | bytes 1572872 | tf_op jit(solution)/shard_map/ppermute | solution.py:512
  165.6 67.2 %collective-permute-start.14 = (bf16[2,64,16,128]{3,2,1,0:T(8,128)(2,1)}, bf16[2,64,16,128]{3,2,1,0:T(8,128)(2,1)}, u32[]{:S(2)}, u32[]{:S(2)}) collective-permute-start(bf16[2,64,16,128]{3,2,1,0:T(8,128)(2,1)} %get-tuple-element.90), channel_id=1, source_target_pairs={{0,16},{4,20},{8,24},{12,28},{16,0},{20,4},{24,8},{28,12},{1,17},{... | collective-permute-start | bytes 1572872 | tf_op jit(solution)/shard_map/ppermute | solution.py:512
  167.1 65.7 %collective-permute-start.15 = (bf16[2,64,16,128]{3,2,1,0:T(8,128)(2,1)}, bf16[2,64,16,128]{3,2,1,0:T(8,128)(2,1)}, u32[]{:S(2)}, u32[]{:S(2)}) collective-permute-start(bf16[2,64,16,128]{3,2,1,0:T(8,128)(2,1)} %get-tuple-element.91), channel_id=1, source_target_pairs={{0,4},{4,0},{8,12},{12,8},{16,20},{20,16},{24,28},{28,24},{1,5},{5... | collective-permute-start | bytes 1572872 | tf_op jit(solution)/shard_map/ppermute | solution.py:512
  191.1 52.2 %collective-permute-start.16 = (bf16[2,64,16,128]{3,2,1,0:T(8,128)(2,1)}, bf16[2,64,16,128]{3,2,1,0:T(8,128)(2,1)}, u32[]{:S(2)}, u32[]{:S(2)}) collective-permute-start(bf16[2,64,16,128]{3,2,1,0:T(8,128)(2,1)} %get-tuple-element.92), channel_id=1, source_target_pairs={{0,12},{4,8},{8,4},{12,0},{16,28},{20,24},{24,20},{28,16},{1,13},{... | collective-permute-start | bytes 1572872 | tf_op jit(solution)/shard_map/ppermute | solution.py:512
  193.2 50.7 %collective-permute-start.27 = (bf16[2,16,64,128]{3,2,1,0:T(8,128)(2,1)}, bf16[2,16,64,128]{3,2,1,0:T(8,128)(2,1)S(1)}, u32[]{:S(2)}, u32[]{:S(2)}) collective-permute-start(bf16[2,16,64,128]{3,2,1,0:T(8,128)(2,1)} %get-tuple-element.104), channel_id=1, source_target_pairs={{0,28},{4,24},{8,20},{12,16},{16,12},{20,8},{24,4},{28,0},{1,29},{... | collective-permute-start | bytes 1572872 | tf_op jit(solution)/shard_map/ppermute | solution.py:512
  216.4 48.8 %collective-permute-start.28 = (bf16[2,16,64,128]{3,2,1,0:T(8,128)(2,1)}, bf16[2,16,64,128]{3,2,1,0:T(8,128)(2,1)S(1)}, u32[]{:S(2)}, u32[]{:S(2)}) collective-permute-start(bf16[2,16,64,128]{3,2,1,0:T(8,128)(2,1)} %get-tuple-element.105), channel_id=1, source_target_pairs={{0,24},{4,28},{8,16},{12,20},{16,8},{20,12},{24,0},{28,4},{1,25},{... | collective-permute-start | bytes 1572872 | tf_op jit(solution)/shard_map/ppermute | solution.py:512
  232.8 54.9 %collective-permute-start.29 = (bf16[2,16,64,128]{3,2,1,0:T(8,128)(2,1)}, bf16[2,16,64,128]{3,2,1,0:T(8,128)(2,1)S(1)}, u32[]{:S(2)}, u32[]{:S(2)}) collective-permute-start(bf16[2,16,64,128]{3,2,1,0:T(8,128)(2,1)} %get-tuple-element.106), channel_id=1, source_target_pairs={{0,20},{4,16},{8,28},{12,24},{16,4},{20,0},{24,12},{28,8},{1,21},{... | collective-permute-start | bytes 1572872 | tf_op jit(solution)/shard_map/ppermute | solution.py:512
  232.8 141.2 %collective-permute-start.24 = (bf16[4,32,64,128]{3,2,1,0:T(8,128)(2,1)}, bf16[4,32,64,128]{3,2,1,0:T(8,128)(2,1)}, u32[]{:S(2)}, u32[]{:S(2)}) collective-permute-start(bf16[4,32,64,128]{3,2,1,0:T(8,128)(2,1)} %get-tuple-element.101), channel_id=1, source_target_pairs={{0,3},{1,2},{2,1},{3,0},{4,7},{5,6},{6,5},{7,4},{8,11},{9,10},{10,... | collective-permute-start | bytes 6291464 | tf_op jit(solution)/shard_map/ppermute | solution.py:512
  243.4 130.6 %collective-permute-start.25 = (bf16[4,32,64,128]{3,2,1,0:T(8,128)(2,1)}, bf16[4,32,64,128]{3,2,1,0:T(8,128)(2,1)}, u32[]{:S(2)}, u32[]{:S(2)}) collective-permute-start(bf16[4,32,64,128]{3,2,1,0:T(8,128)(2,1)} %get-tuple-element.102), channel_id=1, source_target_pairs={{0,2},{1,3},{2,0},{3,1},{4,6},{5,7},{6,4},{7,5},{8,10},{9,11},{10,... | collective-permute-start | bytes 6291464 | tf_op jit(solution)/shard_map/ppermute | solution.py:512
  243.9 130.2 %collective-permute-start.26 = (bf16[4,32,64,128]{3,2,1,0:T(8,128)(2,1)}, bf16[4,32,64,128]{3,2,1,0:T(8,128)(2,1)}, u32[]{:S(2)}, u32[]{:S(2)}) collective-permute-start(bf16[4,32,64,128]{3,2,1,0:T(8,128)(2,1)} %get-tuple-element.103), channel_id=1, source_target_pairs={{0,1},{1,0},{2,3},{3,2},{4,5},{5,4},{6,7},{7,6},{8,9},{9,8},{10,11... | collective-permute-start | bytes 6291464 | tf_op jit(solution)/shard_map/ppermute | solution.py:512
  265.3 34.3 %collective-permute-start.30 = (bf16[2,16,64,128]{3,2,1,0:T(8,128)(2,1)}, bf16[2,16,64,128]{3,2,1,0:T(8,128)(2,1)S(1)}, u32[]{:S(2)}, u32[]{:S(2)}) collective-permute-start(bf16[2,16,64,128]{3,2,1,0:T(8,128)(2,1)} %get-tuple-element.107), channel_id=1, source_target_pairs={{0,16},{4,20},{8,24},{12,28},{16,0},{20,4},{24,8},{28,12},{1,17},{... | collective-permute-start | bytes 1572872 | tf_op jit(solution)/shard_map/ppermute | solution.py:512
  299.6 15.2 %collective-permute-start.32 = (bf16[2,16,64,128]{3,2,1,0:T(8,128)(2,1)}, bf16[2,16,64,128]{3,2,1,0:T(8,128)(2,1)}, u32[]{:S(2)}, u32[]{:S(2)}) collective-permute-start(bf16[2,16,64,128]{3,2,1,0:T(8,128)(2,1)} %get-tuple-element.109), channel_id=1, source_target_pairs={{0,8},{4,12},{8,0},{12,4},{16,24},{20,28},{24,16},{28,20},{1,9},{5... | collective-permute-start | bytes 1572872 | tf_op jit(solution)/shard_map/ppermute | solution.py:512
  299.6 24.8 %collective-permute-start.33 = (bf16[2,16,64,128]{3,2,1,0:T(8,128)(2,1)}, bf16[2,16,64,128]{3,2,1,0:T(8,128)(2,1)}, u32[]{:S(2)}, u32[]{:S(2)}) collective-permute-start(bf16[2,16,64,128]{3,2,1,0:T(8,128)(2,1)} %get-tuple-element.110), channel_id=1, source_target_pairs={{0,12},{4,8},{8,4},{12,0},{16,28},{20,24},{24,20},{28,16},{1,13},{... | collective-permute-start | bytes 1572872 | tf_op jit(solution)/shard_map/ppermute | solution.py:512
  314.7 18.8 %collective-permute-start.17 = (bf16[2,16,64,128]{3,2,1,0:T(8,128)(2,1)}, bf16[2,16,64,128]{3,2,1,0:T(8,128)(2,1)}, u32[]{:S(2)}, u32[]{:S(2)}) collective-permute-start(bf16[2,16,64,128]{3,2,1,0:T(8,128)(2,1)} %get-tuple-element.94), channel_id=1, source_target_pairs={{0,28},{4,24},{8,20},{12,16},{16,12},{20,8},{24,4},{28,0},{1,29},{... | collective-permute-start | bytes 1572872 | tf_op jit(solution)/shard_map/ppermute | solution.py:512
  324.4 26.9 %collective-permute-start.18 = (bf16[2,16,64,128]{3,2,1,0:T(8,128)(2,1)}, bf16[2,16,64,128]{3,2,1,0:T(8,128)(2,1)}, u32[]{:S(2)}, u32[]{:S(2)}) collective-permute-start(bf16[2,16,64,128]{3,2,1,0:T(8,128)(2,1)} %get-tuple-element.95), channel_id=1, source_target_pairs={{0,24},{4,28},{8,16},{12,20},{16,8},{20,12},{24,0},{28,4},{1,25},{... | collective-permute-start | bytes 1572872 | tf_op jit(solution)/shard_map/ppermute | solution.py:512
  333.6 113.5 %collective-permute-start.19 = (bf16[2,16,64,128]{3,2,1,0:T(8,128)(2,1)}, bf16[2,16,64,128]{3,2,1,0:T(8,128)(2,1)}, u32[]{:S(2)}, u32[]{:S(2)}) collective-permute-start(bf16[2,16,64,128]{3,2,1,0:T(8,128)(2,1)} %get-tuple-element.96), channel_id=1, source_target_pairs={{0,20},{4,16},{8,28},{12,24},{16,4},{20,0},{24,12},{28,8},{1,21},{... | collective-permute-start | bytes 1572872 | tf_op jit(solution)/shard_map/ppermute | solution.py:512
  351.3 95.8 %collective-permute-start.20 = (bf16[2,16,64,128]{3,2,1,0:T(8,128)(2,1)}, bf16[2,16,64,128]{3,2,1,0:T(8,128)(2,1)}, u32[]{:S(2)}, u32[]{:S(2)}) collective-permute-start(bf16[2,16,64,128]{3,2,1,0:T(8,128)(2,1)} %get-tuple-element.97), channel_id=1, source_target_pairs={{0,16},{4,20},{8,24},{12,28},{16,0},{20,4},{24,8},{28,12},{1,17},{... | collective-permute-start | bytes 1572872 | tf_op jit(solution)/shard_map/ppermute | solution.py:512
  374.0 73.1 %collective-permute-start.21 = (bf16[2,16,64,128]{3,2,1,0:T(8,128)(2,1)}, bf16[2,16,64,128]{3,2,1,0:T(8,128)(2,1)}, u32[]{:S(2)}, u32[]{:S(2)}) collective-permute-start(bf16[2,16,64,128]{3,2,1,0:T(8,128)(2,1)} %get-tuple-element.98), channel_id=1, source_target_pairs={{0,4},{4,0},{8,12},{12,8},{16,20},{20,16},{24,28},{28,24},{1,5},{5... | collective-permute-start | bytes 1572872 | tf_op jit(solution)/shard_map/ppermute | solution.py:512
  374.0 73.1 %collective-permute-start.22 = (bf16[2,16,64,128]{3,2,1,0:T(8,128)(2,1)}, bf16[2,16,64,128]{3,2,1,0:T(8,128)(2,1)}, u32[]{:S(2)}, u32[]{:S(2)}) collective-permute-start(bf16[2,16,64,128]{3,2,1,0:T(8,128)(2,1)} %get-tuple-element.99), channel_id=1, source_target_pairs={{0,8},{4,12},{8,0},{12,4},{16,24},{20,28},{24,16},{28,20},{1,9},{5... | collective-permute-start | bytes 1572872 | tf_op jit(solution)/shard_map/ppermute | solution.py:512
  374.1 73.0 %collective-permute-start.23 = (bf16[2,16,64,128]{3,2,1,0:T(8,128)(2,1)}, bf16[2,16,64,128]{3,2,1,0:T(8,128)(2,1)}, u32[]{:S(2)}, u32[]{:S(2)}) collective-permute-start(bf16[2,16,64,128]{3,2,1,0:T(8,128)(2,1)} %get-tuple-element.100), channel_id=1, source_target_pairs={{0,12},{4,8},{8,4},{12,0},{16,28},{20,24},{24,20},{28,16},{1,13},{... | collective-permute-start | bytes 1572872 | tf_op jit(solution)/shard_map/ppermute | solution.py:512
  (18 other events, 727.0 us)

commit v3 on v2

--- a/solution.py
+++ b/solution.py
@@ -10,48 +10,15 @@
 
 MIB = 1024 * 1024
 VMEM_BYTES = 62 * MIB
-PLAN = {'early': 2,
- 'order': 2,
- 'last': 1,
- 'corner': 'last1',
- 'near': 'late0',
- 'pins': {'pack1': [['early', 5]],
-          'last1': [['side', -1], ['early', 4]],
-          'dim2b': [['late', 2]],
-          'late0': [['late', 6]],
-          'dim2a': [['late', 1]],
-          'last0': [['early', 7]]},
- 'cost': {'pack0': 0.216,
-          'pack1': 60,
-          'rows': 21.6,
-          'mix': 0.96,
-          'last0': 0.324,
-          'last1': 60,
-          'dim1': 0.132,
-          'dim2a': 25.92,
-          'dim2b': 120,
-          'late0': 120,
-          'late1': 1.8,
-          'late2': 0.162,
-          'ffn0': 1.296,
-          'ffn1': 3.6,
-          'ffn2': 14.4,
-          'ffn3': 36.0},
- 'groups': [2]}
-SPAN = 4.8
-NORMAL = (
-    0.147212786,
-    -0.00633505354,
-    0.000398642281,
-    -2.65332237e-05,
-    1.74432499e-06,
-    -1.09393557e-07,
-    5.93270033e-09,
-    -2.75892574e-10,
-    1.73565533e-11,
-    -1.17650118e-12,
-    3.52373652e-14,
-)
+PLAN = {
+    "early": 2,
+    "groups": [1, 1],
+    "last": 0,
+    "corner": "",
+    "pins": {"last1": [("side", -1)]},
+    "cost": {"pack0": 8.0, "pack1": 8.0, "rows": 7.6, "mix": 5.0, "last0": 22.0, "last1": 22.0, "dim1": 20.0, "dim2a": 20.0, "dim2b": 20.0, "late0": 10.0, "late1": 10.0, "ffn0": 21.0, "ffn1": 21.0, "ffn2": 21.0, "ffn3": 21.0},
+}
+HALF_ROOT = math.sqrt(0.5)
 
 
 def forward_rows(length, mode_count):
@@ -140,52 +107,30 @@
     return jnp.concatenate([p.astype(jnp.float32) for p in parts], axis=0).astype(jnp.bfloat16)
 
 
-def partners(ways):
-    far = list(range(ways // 2, ways))
-    near = list(range(1, ways // 2))
-    if PLAN["order"] == 1:
-        near.reverse()
-    if PLAN["order"] == 2:
-        far.reverse()
-    return [0] + far + near
-
-
-def pack_kernel(ways, me_ref, x_ref, *refs):
-    outs, wide = refs[:ways], refs[ways]
-    channels, rows, _, lanes = x_ref.shape
+def pack_kernel(x_ref, *refs):
+    out_ref, wide = refs[-2:]
+    channels, rows, ways, lanes = x_ref.shape
     wide[...] = x_ref[...].astype(jnp.float32).reshape(channels * rows * ways, lanes)
-    for out, step in zip(outs, partners(ways)):
-        picked = wide[pl.ds(me_ref[0] ^ step, channels * rows, stride=ways), :]
-        out[...] = picked.reshape(channels, rows, lanes).astype(jnp.bfloat16)
-
-
-def pack(kernel_name, field, first, count, ways, me, after):
+    for way in range(ways):
+        picked = wide[pl.ds(way, channels * rows, stride=ways), :]
+        out_ref[way] = picked.reshape(channels, rows, lanes).astype(jnp.bfloat16)
+
+
+def pack(kernel_name, field, first, count, ways, after):
     channels, rows, _, lanes = field.shape
     depth = min(16, channels)
-    token_specs = [pl.BlockSpec(memory_space=pl.ANY)] * len(after)
-    token = in_hbm(after)
-
-    def kernel(me_ref, x_ref, *refs):
-        pack_kernel(ways, me_ref, x_ref, *refs[len(token) :])
-
     return pl.pallas_call(
-        kernel,
-        grid_spec=pltpu.PrefetchScalarGridSpec(
-            num_scalar_prefetch=1,
-            grid=(count, channels // depth),
-            in_specs=[
-                pl.BlockSpec((depth, rows, ways, lanes), lambda k, g, me: (g, 0, first + k, 0))
-            ]
-            + token_specs,
-            out_specs=[pl.BlockSpec((None, depth, rows, lanes), lambda k, g, me: (k, g, 0, 0))]
-            * ways,
-            scratch_shapes=[pltpu.VMEM((depth * rows * ways, lanes), jnp.float32)],
-        ),
-        out_shape=[hbm(count, channels, rows, lanes)] * ways,
+        pack_kernel,
+        grid=(count, channels // depth),
+        in_specs=[pl.BlockSpec((depth, rows, ways, lanes), lambda k, g: (g, 0, first + k, 0))]
+        + [pl.BlockSpec(memory_space=pl.ANY)] * len(after),
+        out_specs=pl.BlockSpec((ways, None, depth, rows, lanes), lambda k, g: (0, k, g, 0, 0)),
+        out_shape=hbm(ways, count, channels, rows, lanes),
+        scratch_shapes=[pltpu.VMEM((depth * rows * ways, lanes), jnp.float32)],
         compiler_params=pltpu.CompilerParams(vmem_limit_bytes=VMEM_BYTES),
         cost_estimate=cost(kernel_name, 0),
         name="pack_columns",
-    )(me, *in_hbm([field]), *token)
+    )(*in_hbm([field, *after]))
 
 
 def side_kernel(ways, me_ref, *refs):
@@ -207,7 +152,7 @@
         grid_spec=pltpu.PrefetchScalarGridSpec(
             num_scalar_prefetch=1,
             grid=(across,),
-            in_specs=[rows_of(step) for step in partners(ways)]
+            in_specs=[rows_of(step) for step in range(ways)]
             + [pl.BlockSpec(memory_space=pl.ANY)],
             out_specs=[
                 pl.BlockSpec((None, channels, cols, lanes), lambda r, me: (r, 0, 0, 0))
@@ -253,8 +198,12 @@
 
 
 def lines_kernel(ways, ft_ref, it_ref, mix_ref, *refs):
-    pieces, outs = refs[:ways], refs[ways : 2 * ways]
-    spectra, mixed, wide = refs[2 * ways :]
+    refs, (spectra, mixed, wide) = refs[:-3], refs[-3:]
+    count = len(refs) // 2
+    pieces, outs = refs[:count], refs[count:]
+    if count < ways:
+        pieces = [pieces[0].at[way] for way in range(ways)]
+        outs = [outs[0].at[way] for way in range(ways)]
     channels, length, lanes = pieces[0].shape
     mode_count = mix_ref.shape[0]
     total = ways * length
@@ -285,38 +234,45 @@
         outs[step][...] = part.reshape(length, channels, lanes).astype(jnp.bfloat16)
 
 
-def along_lines(
-    kernel_name, pieces, weights, order, begin, count, after=(), held=(), done=None, full=False
-):
-    ways = len(pieces)
-    several, channels, length, lanes = pieces[0].shape
+def along_lines(kernel_name, pieces, weights, me, begin, count, after, done=None):
+    stacked = not isinstance(pieces, list)
+    if stacked:
+        ways, several, channels, length, lanes = pieces.shape
+        pieces = [pieces]
+    else:
+        ways = len(pieces)
+        several, channels, length, lanes = pieces[0].shape
     mode_count = weights.shape[0]
     total = ways * length
-    forward = forward_rows(total, mode_count).reshape(2 * mode_count, ways, length)
-    forward = jnp.take(forward, order, axis=1).reshape(2 * mode_count, total)
-    back = inverse_rows(total, mode_count).T.reshape(ways, length, 2 * mode_count)
-    back = jnp.take(back, order, axis=0).reshape(total, 2 * mode_count)
+    forward = forward_rows(total, mode_count)
+    back = inverse_rows(total, mode_count).T
+    if stacked:
+        in_spec = pl.BlockSpec(
+            (ways, None, channels, length, lanes), lambda g: (0, begin + g, 0, 0, 0)
+        )
+        out_spec = pl.BlockSpec((ways, None, length, channels, lanes), lambda g: (0, g, 0, 0, 0))
+        out_shape = hbm(ways, count, length, channels, lanes)
+    else:
+        order = me ^ jnp.arange(ways)
+        forward = forward.reshape(2 * mode_count, ways, length)
+        forward = jnp.take(forward, order, axis=1).reshape(2 * mode_count, total)
+        back = back.reshape(ways, length, 2 * mode_count)
+        back = jnp.take(back, order, axis=0).reshape(total, 2 * mode_count)
+        in_spec = pl.BlockSpec((None, channels, length, lanes), lambda g: (begin + g, 0, 0, 0))
+        out_spec = pl.BlockSpec((None, length, channels, lanes), lambda g: (begin + g, 0, 0, 0))
+        out_shape = hbm(several, length, channels, lanes)
     whole = lambda shape: pl.BlockSpec(shape, lambda g: (0,) * len(shape))
-    elsewhere = pl.BlockSpec(memory_space=pl.ANY)
-    put, number = (begin, several) if full else (0, count)
-    kept = list(done or ()) + list(held)
-    moved = 0 if done else ways
+    kept = list(done or ())
     idle = kept + list(after)
-    last = len(idle) + 3 + 2 * ways
     return pl.pallas_call(
-        lambda *refs: lines_kernel(ways, *refs[len(idle) : last], *refs[-3:]),
+        lambda *refs: lines_kernel(ways, *refs[len(idle) :]),
         grid=(count,),
-        in_specs=[elsewhere] * len(idle)
+        in_specs=[pl.BlockSpec(memory_space=pl.ANY)] * len(idle)
         + [whole(forward.shape), whole(back.shape), whole(weights.shape)]
-        + [pl.BlockSpec((None, channels, length, lanes), lambda g: (begin + g, 0, 0, 0))] * ways,
-        out_specs=[
-            pl.BlockSpec((None, length, channels, lanes), lambda g: (put + g, 0, 0, 0))
-        ]
-        * ways
-        + [elsewhere] * len(held),
-        out_shape=[hbm(number, length, channels, lanes)] * ways
-        + [hbm(*array.shape) for array in held],
-        input_output_aliases={at: moved + at for at in range(len(kept))},
+        + [in_spec] * len(pieces),
+        out_specs=[out_spec] * len(pieces),
+        out_shape=[out_shape] * len(pieces),
+        input_output_aliases={at: at for at in range(len(kept))},
         scratch_shapes=[
             pltpu.VMEM((2 * channels * mode_count, lanes), jnp.float32),
             pltpu.VMEM((2 * channels * mode_count, lanes), jnp.float32),
@@ -399,81 +355,64 @@
     )(*in_hbm(idle), forward, back, *in_hbm([weights, field]))
 
 
-def gelu(x):
-    near = jnp.clip(x, -SPAN, SPAN)
-    square = near * near - SPAN * SPAN / 2
-    ratio = NORMAL[-1] * square + NORMAL[-2]
-    for factor in NORMAL[-3::-1]:
-        ratio = ratio * square + factor
-    return x * (0.5 + near * ratio)
-
-
-def cell_kernel(ways, col_ways, me_ref, x_ref, win_ref, wout_ref, bin_ref, bout_ref, *refs):
-    first, second = refs[:ways], refs[ways : ways + col_ways]
-    third = refs[ways + col_ways]
-    out_ref, now, wide, before, hidden = refs[-5:]
-    channels, rows, _, lanes = x_ref.shape
-    steps = partners(ways)
-
-    for place in range(col_ways):
-
-        @pl.when(pl.program_id(0) == place)
+def cell_kernel(col_ways, me_ref, x_ref, win_ref, wout_ref, bin_ref, bout_ref, *refs):
+    first_ref, second, third_ref = refs[0], refs[1 : 1 + col_ways], refs[1 + col_ways]
+    out_ref, now, wide = refs[-3:]
+    channels, _, ways, lanes = x_ref.shape
+
+    for step in range(col_ways):
+
+        @pl.when(pl.program_id(0) == step)
         def _():
-            now[...] = second[place][...]
-
-    def one(row, _):
-        for place in range(0, ways, 2):
-            summed = []
-            for at in range(2):
-                col = me_ref[0] ^ steps[place + at]
-                pair = first[place + at][row].astype(jnp.float32)
-                pair = (pair + now[row, col].astype(jnp.float32)).astype(jnp.bfloat16)
-                total = pair.astype(jnp.float32) + third[row, col].astype(jnp.float32)
-                summed.append(total.astype(jnp.bfloat16))
-            before[...] = mm(win_ref[...], jnp.concatenate(summed, axis=1))
-            for start in range(0, before.shape[0], 32):
-                units = pl.ds(start, 32)
-                hidden[units] = gelu(before[units] + bin_ref[units]).astype(jnp.bfloat16)
-            result = mm(wout_ref[...], hidden[...]) + bout_ref[...]
-            for at in range(2):
-                col = me_ref[0] ^ steps[place + at]
-                wide[pl.ds(col, channels, stride=ways), :] = result[
-                    :, at * lanes : (at + 1) * lanes
-                ]
-        total = wide[...].reshape(channels, ways, lanes) + x_ref[:, row].astype(jnp.float32)
-        out_ref[:, row] = total.astype(jnp.bfloat16)
-        return 0
-
-    lax.fori_loop(0, rows, one, 0)
+            now[...] = second[step][...]
+
+    for col in range(0, ways, 2):
+        summed = []
+        for at in range(2):
+            pair = first_ref[col + at].astype(jnp.float32) + now[col + at].astype(jnp.float32)
+            pair = pair.astype(jnp.bfloat16).astype(jnp.float32)
+            total = pair + third_ref[col + at].astype(jnp.float32)
+            summed.append(total.astype(jnp.bfloat16))
+        pre = mm(win_ref[...], jnp.concatenate(summed, axis=1)) + bin_ref[...]
+        hidden = (0.5 * pre * (1.0 + lax.erf(pre * HALF_ROOT))).astype(jnp.bfloat16)
+        result = mm(wout_ref[...], hidden) + bout_ref[...]
+        for at in range(2):
+            wide[pl.ds(col + at, channels, stride=ways), :] = result[
+                :, at * lanes : (at + 1) * lanes
+            ]
+    total = wide[...].reshape(channels, ways, lanes) + x_ref[:, 0].astype(jnp.float32)
+    out_ref[:, 0] = total.astype(jnp.bfloat16)
 
 
 def cells(field, first, which, second, third, ffn, chunk, me, done, after):
     channels, rows, cols, lanes = field.shape
-    ways, col_ways = len(first), len(second)
+    ways, col_ways = first.shape[0], len(second)
     across = rows // col_ways
-    steps = partners(col_ways)
-
-    def block(place, me):
-        step = steps[0]
-        for other in range(1, col_ways):
-            step = jnp.where(place == other, steps[other], step)
-        return me[1] ^ step
+
+    def row(step, at, me):
+        return (me[1] ^ step) * across + at
+
+    def own_row(which):
+        def index(step, at, me):
+            now = jnp.where(step == which, at, jnp.where(step < which, 0, across - 1))
+            return now, chunk, 0, 0
+
+        return pl.BlockSpec((None, ways, channels, lanes), index)
 
     whole = lambda shape: pl.BlockSpec(shape, lambda *_: (0,) * len(shape))
-    tile = pl.BlockSpec(
-        (channels, across, ways, lanes), lambda p, me: (0, block(p, me), chunk, 0)
-    )
+    tile = pl.BlockSpec((channels, 1, ways, lanes), lambda s, a, me: (0, row(s, a, me), chunk, 0))
     in_specs = [tile] + [whole(w.shape) for w in ffn]
-    in_specs += [
-        pl.BlockSpec((None, across, channels, lanes), lambda p, me: (which, block(p, me), 0, 0))
-    ] * ways
-    in_specs += [
-        pl.BlockSpec((across, ways, channels, lanes), lambda p, me: (0, chunk, 0, 0))
-    ] * col_ways
     in_specs.append(
-        pl.BlockSpec((across, ways, channels, lanes), lambda p, me: (block(p, me), chunk, 0, 0))
-    )
-    operands = [me, *in_hbm([field]), *ffn, *in_hbm([*first, *second, third])]
+        pl.BlockSpec(
+            (ways, None, None, channels, lanes),
+            lambda s, a, me: (0, which, row(s, a, me), 0, 0),
+        )
+    )
+    in_specs += [own_row(step) for step in range(col_ways)]
+    in_specs.append(
+        pl.BlockSpec((None, ways, channels, lanes), lambda s, a, me: (row(s, a, me), chunk, 0, 0))
+    )
+    operands = [me, *in_hbm([field]), *ffn, *in_hbm([first, *second, third])]
     aliases = {}
     if done is not None:
         aliases = {len(operands): 0}
@@ -482,17 +421,15 @@
             in_specs.append(pl.BlockSpec(memory_space=pl.ANY))
             operands += in_hbm([array])
     return pl.pallas_call(
-        functools.partial(cell_kernel, ways, col_ways),
+        functools.partial(cell_kernel, col_ways),
         grid_spec=pltpu.PrefetchScalarGridSpec(
             num_scalar_prefetch=1,
-            grid=(col_ways,),
+            grid=(col_ways, across),
             in_specs=in_specs,
             out_specs=tile,
             scratch_shapes=[
-                pltpu.VMEM((across, ways, channels, lanes), jnp.bfloat16),
+                pltpu.VMEM((ways, channels, lanes), jnp.bfloat16),
                 pltpu.VMEM((channels * ways, lanes), jnp.float32),
-                pltpu.VMEM((ffn[0].shape[0], 2 * lanes), jnp.float32),
-                pltpu.VMEM((ffn[0].shape[0], 2 * lanes), jnp.bfloat16),
             ],
         ),
         out_shape=hbm(*field.shape),
@@ -503,14 +440,20 @@
     )(*operands)
 
 
-def exchange(pieces, axis, skip=None, only=None):
-    ways = len(pieces)
-    got = list(pieces)
-    for place, step in enumerate(partners(ways)):
-        if step and place != skip and only in (None, place):
-            pairs = [(at, at ^ step) for at in range(ways)]
-            got[place] = lax.ppermute(pieces[place], axis, pairs)
-    return got
+def swap(piece, axis, step):
+    ways = lax.axis_size(axis)
+    return lax.ppermute(piece, axis, [(at, at ^ step) for at in range(ways)])
+
+
+def exchange(pieces, axis, skip=None):
+    return [
+        swap(piece, axis, step) if step not in (0, skip) else piece
+        for step, piece in enumerate(pieces)
+    ]
+
+
+def trade(stack):
+    return lax.all_to_all(stack, "row", split_axis=0, concat_axis=0)
 
 
 def body(field, spec_first, spec_second, spec_third, ffn_in, ffn_out, bias_in, bias_out):
@@ -518,26 +461,24 @@
     ways, col_ways = lax.axis_size("row"), lax.axis_size("col")
     row_me, col_me = lax.axis_index("row"), lax.axis_index("col")
     me = jnp.stack([row_me, col_me]).astype(jnp.int32)
-    row_order = row_me ^ jnp.array(partners(ways))
-    col_order = col_me ^ jnp.array(partners(col_ways))
     chunks = cols // ways
     across = rows // col_ways
     ffn = (ffn_in.T, ffn_out.T, bias_in[:, None], bias_out[:, None])
 
     early_count = max(1, min(PLAN["early"], chunks - 1))
     rest = chunks - early_count
-    nearest = ways // 2 + 1
     seen = {}
 
     def pins(kernel):
         return [seen[name][place] for name, place in PLAN["pins"].get(kernel, ())]
 
-    early = pack("pack0", field, 0, early_count, ways, me, [])
-    seen["early"] = early_in = exchange(early, "row")
-    late = pack("pack1", field, early_count, rest, ways, me, [early[0]] + pins("pack1"))
-    seen["late"] = late_in = exchange(late, "row")
-    corner = 2
-    side = list(rows_first(field, col_ways, me, late[0]))
+    early = pack("pack0", field, 0, early_count, ways, [])
+    early_in = trade(early)
+    late = pack("pack1", field, early_count, rest, ways, [early])
+    late_in = trade(late)
+    seen["early"], seen["late"] = [early_in], [late_in]
+    corner = 3
+    side = list(rows_first(field, col_ways, me, early))
     seen["side"] = side_in = exchange(side, "col", skip=corner)
     first_mix, second_mix, third_mix = mix_rows(side[0], spec_first, spec_second, spec_third)
 
@@ -552,17 +493,18 @@
     third = last(0, None, [])
     if PLAN["last"] == 0:
         third = last(1, third, [])
-    side_in[corner] = exchange(side, "col", only=corner)[corner]
+    side_in[corner] = swap(side[corner], "col", corner)
     parts = along_lines(
-        "dim1", early_in, first_mix, row_order, 0, early_count, after=[third] + pins("dim1")
-    )
-    token = parts[0]
+        "dim1", early_in, first_mix, None, 0, early_count, [third] + pins("dim1")
+    )[0]
+    back = [(trade(parts), early_count)]
+    token = parts
     if PLAN["last"] == 1:
         third = last(1, third, [token])
         token = third
     cut = across // 2
     second = along_lines(
-        "dim2a", side_in, second_mix, col_order, 0, cut, [token] + pins("dim2a"), full=True
+        "dim2a", side_in, second_mix, col_me, 0, cut, [token] + pins("dim2a")
     )
     token = second[0]
     if PLAN["last"] == 2:
@@ -572,45 +514,37 @@
         "dim2b",
         side_in,
         second_mix,
-        col_order,
+        col_me,
         cut,
         across - cut,
         [token] + pins("dim2b"),
         done=second,
-        full=True,
     )
     token = second[0]
-    seen["second"] = second_in = exchange(second, "col")
+    second_in = exchange(second, "col")
+    seen["second"] = second_in
     if PLAN["last"] == 3:
         third = last(1, third, [token])
         token = third
-    late_parts, near, begin = [], parts[nearest:], 0
     groups = PLAN["groups"] if sum(PLAN["groups"]) == rest else [1] * rest
+    begin = 0
     for at, count in enumerate(groups):
         name = f"late{at}"
-        held = near if PLAN["near"] == name else []
-        got = along_lines(
-            name, late_in, first_mix, row_order, begin, count, [token] + pins(name), held=held
-        )
+        parts = along_lines(name, late_in, first_mix, None, begin, count, [token] + pins(name))[0]
+        back.append((trade(parts), count))
         begin += count
-        late_parts.append((got[:ways], count))
-        near = got[ways:] if held else near
-        token = got[0]
+        token = parts
     if PLAN["last"] == 4:
         third = last(1, third, [token])
         token = third
-    seen["back"] = back = exchange(parts[:nearest] + near, "row")
-    first = [(back, which) for which in range(early_count)]
-    for got, count in late_parts:
-        back = exchange(got, "row")
-        first += [(back, which) for which in range(count)]
-
-    result = None
-    for chunk, (branch, which) in enumerate(first):
-        result = cells(
-            field, branch, which, second_in, third, ffn, chunk, me, result, token
-        )
-        token = None
+
+    result, chunk = None, 0
+    for branch, count in back:
+        for which in range(count):
+            result = cells(
+                field, branch, which, second_in, third, ffn, chunk, me, result, token
+            )
+            chunk, token = chunk + 1, None
     return result
 
 

time: 519 us -> 451 us (0.87)
  starting transfers between devices: 105 us -> 31.9 us
  waiting for transfers between devices: 98.4 us -> 163 us
  Pallas kernels: 299 us -> 244 us
    all_to_all x0 -> x5, waiting for transfers between devices: none -> 134 us  [trade(): return lax.all_to_all(stack, 'row', split_axis=0, concat_axis=0)]
    ppermute x34 -> x6, starting transfers between devices: 105 us -> 6.99 us  [swap(): return lax.ppermute(piece, axis, [(at, at ^ step) for at in range(ways)])]
    ppermute x34 -> x6, waiting for transfers between devices: 98.4 us -> 29.3 us  [swap(): return lax.ppermute(piece, axis, [(at, at ^ step) for at in range(ways)])]
    pallas_call x10 -> x11, Pallas kernels: 242 us -> 187 us  [the longest x4 86.5 us: cells(): pl.pallas_call(functools.partial(cell_kernel, col_ways), grid_spec=pltpu....]
    all_to_all x0 -> x5, starting transfers between devices: none -> 24.9 us  [trade(): return lax.all_to_all(stack, 'row', split_axis=0, concat_axis=0)]
  transfers between devices with their start and end apart: 34 -> 11, of which waited for: 8 -> 5; matrix products, arithmetic and copies ran while one was open for 2% -> 2% of each run, Pallas kernels for 42% -> 48%
where the time goes in v3:
time: 451 us; the launch traced here: 450 us
  Pallas kernels  244 us (54%)
  waiting for transfers between devices  163 us (36%)
  starting transfers between devices  31.9 us (7%)
  local copies, waits for them, and re-layouts  8.65 us (2%)
    all_to_all x5, waiting for transfers between devices, trade(): return lax.all_to_all(stack, 'row', split_axis=0, concat_axis=0)  134 us
    pallas_call x4, Pallas kernels, cells(): pl.pallas_call(functools.partial(cell_kernel, col_ways), grid_spec=pltpu....  86.5 us
    pallas_call x5, Pallas kernels, along_lines(): pl.pallas_call(lambda *refs: lines_kernel(ways, *refs[len(idle):]), grid=...  85.9 us
    pallas_call x2, Pallas kernels, last_branch(): pl.pallas_call(lambda *refs: last_kernel(*refs[len(idle):len(idle) + 5],...  44.7 us
    ppermute x6, waiting for transfers between devices, swap(): return lax.ppermute(piece, axis, [(at, at ^ step) for at in range(ways)])  29.3 us
    all_to_all x5, starting transfers between devices, trade(): return lax.all_to_all(stack, 'row', split_axis=0, concat_axis=0)  24.9 us
    pallas_call x2, Pallas kernels, pack(): pl.pallas_call(pack_kernel, grid=(count, channels // depth), in_specs=[pl...  14.7 us
  transfers between devices with their start and end apart: 11, of which 5 were waited for; matrix products, arithmetic and copies ran while one was open for 2% of the time, Pallas kernels for 48%

profile of v3, /device:TPU:0, one launch (start us, length us, event | category | flops | bytes accessed | tf_op | source)
XLA Modules:
  0.0 450.3 jit_solution(2409392286008784497)
XLA Ops:
  0.0 7.4 %pack_columns.2.refs_4_.refs_0_ = bf16[8,2,64,16,128]{4,3,2,1,0:T(8,128)(2,1)} custom-call(bf16[64,16,32,128]{3,2,1,0:T(8,128)(2,1)} %x_ref.11), custom_call_target="tpu_custom_call" | custom-call | flops 9200000000 | tf_op jit(solution)/shard_map/pack_columns/pallas_call | solution.py:122
  7.4 6.3 %all-to-all-start = ((bf16[8,2,64,16,128]{4,3,2,1,0:T(8,128)(2,1)}), bf16[8,2,64,16,128]{4,3,2,1,0:T(8,128)(2,1)}, u32[]{:S(2)}, u32[]{:S(2)}) async-start(bf16[8,2,64,16,128]{4,3,2,1,0:T(8,128)(2,1)} %pack_columns.2.refs_4_.refs_0_), calls=%async_computation | async-start | bytes 8388608 | tf_op jit(solution)/shard_map/all_to_all | solution.py:456
  14.3 7.8 %rows_first.1 = (bf16[4,64,32,128]{3,2,1,0:T(8,128)(2,1)}, bf16[4,64,32,128]{3,2,1,0:T(8,128)(2,1)}, bf16[4,64,32,128]{3,2,1,0:T(8,128)(2,1)}, bf16[4,64,32,128]{3,2,1,0:T(8,128)(2,1)}) custom-call(s32[2]{0:T(128)} %pad_add_fusion.me_ref, bf16[64,16,32,128]{3,2,1,0:T(8,128)(2,1)} %x_ref.11, bf16[64,16,32,128]{3,2,1,0:T(8,128)(2,1)} %x_ref.11, ...), custom_call_target="tpu_custom_call" | custom-call | flops 8739999744 | tf_op jit(solution)/shard_map/rows_first/pallas_call | solution.py:150
  22.1 2.4 collective-permute-start.2
  27.4 7.4 %pack_columns.3 = bf16[8,2,64,16,128]{4,3,2,1,0:T(8,128)(2,1)} custom-call(bf16[64,16,32,128]{3,2,1,0:T(8,128)(2,1)} %x_ref.11, bf16[8,2,64,16,128]{4,3,2,1,0:T(8,128)(2,1)} %pack_columns.2.refs_4_.refs_0_), custom_call_target="tpu_custom_call" | custom-call | flops 9200000000 | tf_op jit(solution)/shard_map/pack_columns/pallas_call | solution.py:122
  34.8 73.0 %all-to-all-done.refs_4_ = bf16[8,2,64,16,128]{4,3,2,1,0:T(8,128)(2,1)} async-done(((bf16[8,2,64,16,128]{4,3,2,1,0:T(8,128)(2,1)}), bf16[8,2,64,16,128]{4,3,2,1,0:T(8,128)(2,1)}, u32[]{:S(2)}, u32[]{:S(2)}) %all-to-all-start) | async-done | bytes 4194336 | tf_op jit(solution)/shard_map/all_to_all | solution.py:456
  107.8 4.6 %all-to-all-start.1 = ((bf16[8,2,64,16,128]{4,3,2,1,0:T(8,128)(2,1)}), bf16[8,2,64,16,128]{4,3,2,1,0:T(8,128)(2,1)}, u32[]{:S(2)}, u32[]{:S(2)}) async-start(bf16[8,2,64,16,128]{4,3,2,1,0:T(8,128)(2,1)} %pack_columns.3), calls=%async_computation.1 | async-start | bytes 8388608 | tf_op jit(solution)/shard_map/all_to_all | solution.py:456
  112.4 4.9 %mixing_matrices.1 = (bf16[32,128,128]{2,1,0:T(8,128)(2,1)}, bf16[32,128,128]{2,1,0:T(8,128)(2,1)}, bf16[32,128,128]{2,1,0:T(8,128)(2,1)}) custom-call(bf16[4,64,32,128]{3,2,1,0:T(8,128)(2,1)} %get-tuple-element.22._.refs_4_.refs_8_, bf16[2,32,64,64]{3,2,1,0:T(8,128)(2,1)} %refs_0_.3, bf16[2,32,64,64]{3,2,1,0:T(8,128)(2,1)} %refs_1_.3, ...), custom_call_target="tpu_custom_call" | custom-call | flops 5750000128 | tf_op jit(solution)/shard_map/mixing_matrices/pallas_call | solution.py:58
  117.3 22.3 %last_branch.2.refs_0_ = bf16[16,32,64,128]{3,2,1,0:T(8,128)(2,1)} custom-call(bf16[64,128]{1,0:T(8,128)(2,1)} %copy.49.refs_0_.refs_2_.refs_1_, bf16[64,128]{1,0:T(8,128)(2,1)} %copy.50.refs_1_.refs_3_, bf16[32,128,128]{2,1,0:T(8,128)(2,1)} %get-tuple-element.23.refs_2_.refs_4_, bf16[64,16,32,128]{3,2,1,0:T(8,128)(2,1)} %x_ref.11), custom_call_target="tpu_custom_call" | custom-call | flops 25300000768 | tf_op jit(solution)/shard_map/last_branch/pallas_call | solution.py:329
  139.6 22.4 %last_branch.3.refs_0_.refs_5_ = bf16[16,32,64,128]{3,2,1,0:T(8,128)(2,1)} custom-call(bf16[16,32,64,128]{3,2,1,0:T(8,128)(2,1)} %last_branch.2.refs_0_, bf16[4,64,32,128]{3,2,1,0:T(8,128)(2,1)} %get-tuple-element.24.refs_1_, bf16[64,128]{1,0:T(8,128)(2,1)} %copy.49.refs_0_.refs_2_.refs_1_, ...), custom_call_target="tpu_custom_call", output_to_operand_aliasing={{}: (0, {})} | custom-call | flops 25300000768 | tf_op jit(solution)/shard_map/last_branch/pallas_call | solution.py:329
  162.0 20.5 %line_branch.5.refs_0_ = bf16[8,2,16,64,128]{4,3,2,1,0:T(8,128)(2,1)} custom-call(bf16[16,32,64,128]{3,2,1,0:T(8,128)(2,1)} %last_branch.3.refs_0_.refs_5_, bf16[64,128]{1,0:T(8,128)(2,1)} %copy.49.refs_0_.refs_2_.refs_1_, bf16[128,64]{1,0:T(8,128)(2,1)} %bitcast.13, bf16[32,128,128]{2,1,0:T(8,128)(2,1)} %get-tuple-element.25.refs_3_, ...), custom_call_target="tpu_custom_call" | custom-call | flops 23000000512 | tf_op jit(solution)/shard_map/line_branch/pallas_call | solution.py:267
  182.6 23.9 %all-to-all-done.1.refs_4_ = bf16[8,2,64,16,128]{4,3,2,1,0:T(8,128)(2,1)} async-done(((bf16[8,2,64,16,128]{4,3,2,1,0:T(8,128)(2,1)}), bf16[8,2,64,16,128]{4,3,2,1,0:T(8,128)(2,1)}, u32[]{:S(2)}, u32[]{:S(2)}) %all-to-all-start.1) | async-done | bytes 4194336 | tf_op jit(solution)/shard_map/all_to_all | solution.py:456
  206.4 4.6 %all-to-all-start.4 = ((bf16[8,2,16,64,128]{4,3,2,1,0:T(8,128)(2,1)}), bf16[8,2,16,64,128]{4,3,2,1,0:T(8,128)(2,1)}, u32[]{:S(2)}, u32[]{:S(2)}) async-start(bf16[8,2,16,64,128]{4,3,2,1,0:T(8,128)(2,1)} %line_branch.5.refs_0_), calls=%async_computation.4 | async-start | bytes 8388608 | tf_op jit(solution)/shard_map/all_to_all | solution.py:456
  212.7 0.7 copy.54.refs_1_.refs_5_
  214.1 20.7 %line_branch.6 = (bf16[4,32,64,128]{3,2,1,0:T(8,128)(2,1)}, bf16[4,32,64,128]{3,2,1,0:T(8,128)(2,1)}, bf16[4,32,64,128]{3,2,1,0:T(8,128)(2,1)}, bf16[4,32,64,128]{3,2,1,0:T(8,128)(2,1)}) custom-call(bf16[8,2,16,64,128]{4,3,2,1,0:T(8,128)(2,1)} %line_branch.5.refs_0_, bf16[64,128]{1,0:T(8,128)(2,1)} %copy.54.refs_1_.refs_5_, bf16[128,64]{1,0:T(8,128)(2,1)} %bitcast.22, ...), custom_call_target="tpu_custom_call" | custom-call | flops 23000000512 | tf_op jit(solution)/shard_map/line_branch/pallas_call | solution.py:267
  234.9 3.1 copy.67.refs_0_
  238.0 20.7 %line_branch.7 = (bf16[4,32,64,128]{3,2,1,0:T(8,128)(2,1)}, bf16[4,32,64,128]{3,2,1,0:T(8,128)(2,1)}, bf16[4,32,64,128]{3,2,1,0:T(8,128)(2,1)}, bf16[4,32,64,128]{3,2,1,0:T(8,128)(2,1)}) custom-call(bf16[4,32,64,128]{3,2,1,0:T(8,128)(2,1)} %copy.67.refs_0_, ...), custom_call_target="tpu_custom_call", output_to_operand_aliasing={{0}: (0, {}), {1}: (1, {}), {2}: (2, {}), {3}: (3, {})} | custom-call | flops 23000000512 | tf_op jit(solution)/shard_map/line_branch/pallas_call | solution.py:267
  258.7 1.5 collective-permute-start.3
  260.2 1.5 collective-permute-start.4
  262.2 12.0 %line_branch.8.refs_0_ = bf16[8,1,16,64,128]{4,3,2,1,0:T(8,128)(2,1)} custom-call(bf16[4,32,64,128]{3,2,1,0:T(8,128)(2,1)} %get-tuple-element.33.refs_0_.refs_1_, bf16[64,128]{1,0:T(8,128)(2,1)} %copy.49.refs_0_.refs_2_.refs_1_, bf16[128,64]{1,0:T(8,128)(2,1)} %bitcast.14, bf16[32,128,128]{2,1,0:T(8,128)(2,1)} %get-tuple-element.25.refs_3_, ...), custom_call_target="tpu_custom_call" | custom-call | flops 11500000256 | tf_op jit(solution)/shard_map/line_branch/pallas_call | solution.py:267
  274.2 30.9 %all-to-all-done.4.refs_0_ = bf16[8,2,16,64,128]{4,3,2,1,0:T(8,128)(2,1)} async-done(((bf16[8,2,16,64,128]{4,3,2,1,0:T(8,128)(2,1)}), bf16[8,2,16,64,128]{4,3,2,1,0:T(8,128)(2,1)}, u32[]{:S(2)}, u32[]{:S(2)}) %all-to-all-start.4) | async-done | bytes 4194336 | tf_op jit(solution)/shard_map/all_to_all | solution.py:456
  305.0 4.5 %all-to-all-start.3 = ((bf16[8,1,16,64,128]{4,3,2,1,0:T(8,128)(2,1)}), bf16[8,1,16,64,128]{4,3,2,1,0:T(8,128)(2,1)}, u32[]{:S(2)}, u32[]{:S(2)}) async-start(bf16[8,1,16,64,128]{4,3,2,1,0:T(8,128)(2,1)} %line_branch.8.refs_0_), calls=%async_computation.3 | async-start | bytes 4194304 | tf_op jit(solution)/shard_map/all_to_all | solution.py:456
  309.6 0.8 copy.64.bin_ref
  310.4 0.7 copy.47
  311.8 11.9 %line_branch.9.refs_6_ = bf16[8,1,16,64,128]{4,3,2,1,0:T(8,128)(2,1)} custom-call(bf16[8,1,16,64,128]{4,3,2,1,0:T(8,128)(2,1)} %line_branch.8.refs_0_, bf16[64,128]{1,0:T(8,128)(2,1)} %copy.49.refs_0_.refs_2_.refs_1_, bf16[128,64]{1,0:T(8,128)(2,1)} %bitcast.15, bf16[32,128,128]{2,1,0:T(8,128)(2,1)} %get-tuple-element.25.refs_3_, ...), custom_call_target="tpu_custom_call" | custom-call | flops 11500000256 | tf_op jit(solution)/shard_map/line_branch/pallas_call | solution.py:267
  323.7 29.3 %collective-permute-done.4.refs_3_ = bf16[4,32,64,128]{3,2,1,0:T(8,128)(2,1)} collective-permute-done((bf16[4,32,64,128]{3,2,1,0:T(8,128)(2,1)}, bf16[4,32,64,128]{3,2,1,0:T(8,128)(2,1)}, u32[]{:S(2)}, u32[]{:S(2)}) %collective-permute-start.4) | collective-permute-done | bytes 2097184 | tf_op jit(solution)/shard_map/ppermute | solution.py:445
  353.1 21.6 %feed_forward.4.refs_6_ = bf16[64,16,32,128]{3,2,1,0:T(8,128)(2,1)} custom-call(s32[2]{0:T(128)} %pad_add_fusion.me_ref, bf16[64,16,32,128]{3,2,1,0:T(8,128)(2,1)} %x_ref.11, bf16[256,64]{1,0:T(8,128)(2,1)} %bitcast.18, bf16[64,256]{1,0:T(8,128)(2,1)} %bitcast.26, f32[256,1]{1,0:T(8,128)} %copy.64.bin_ref, f32[64,1]{1,0:T(8,128)} %copy.65.bout_ref, ...), custom_call_target="tpu_custom_call" | custom-call | flops 24149999616 | tf_op jit(solution)/shard_map/feed_forward/pallas_call | solution.py:423
  374.7 4.8 %all-to-all-start.2 = ((bf16[8,1,16,64,128]{4,3,2,1,0:T(8,128)(2,1)}), bf16[8,1,16,64,128]{4,3,2,1,0:T(8,128)(2,1)}, u32[]{:S(2)}, u32[]{:S(2)}) async-start(bf16[8,1,16,64,128]{4,3,2,1,0:T(8,128)(2,1)} %line_branch.9.refs_6_), calls=%async_computation.2 | async-start | bytes 4194304 | tf_op jit(solution)/shard_map/all_to_all | solution.py:456
  379.5 21.6 %feed_forward.5.refs_6_ = bf16[64,16,32,128]{3,2,1,0:T(8,128)(2,1)} custom-call(s32[2]{0:T(128)} %pad_add_fusion.me_ref, bf16[64,16,32,128]{3,2,1,0:T(8,128)(2,1)} %x_ref.11, bf16[256,64]{1,0:T(8,128)(2,1)} %bitcast.19, bf16[64,256]{1,0:T(8,128)(2,1)} %bitcast.27, f32[256,1]{1,0:T(8,128)} %copy.64.bin_ref, ...), custom_call_target="tpu_custom_call", output_to_operand_aliasing={{}: (12, {})} | custom-call | flops 24149999616 | tf_op jit(solution)/shard_map/feed_forward/pallas_call | solution.py:423
  401.1 21.6 %feed_forward.6.refs_6_ = bf16[64,16,32,128]{3,2,1,0:T(8,128)(2,1)} custom-call(s32[2]{0:T(128)} %pad_add_fusion.me_ref, bf16[64,16,32,128]{3,2,1,0:T(8,128)(2,1)} %x_ref.11, bf16[256,64]{1,0:T(8,128)(2,1)} %bitcast.20, bf16[64,256]{1,0:T(8,128)(2,1)} %bitcast.28, f32[256,1]{1,0:T(8,128)} %copy.64.bin_ref, ...), custom_call_target="tpu_custom_call", output_to_operand_aliasing={{}: (12, {})} | custom-call | flops 24149999616 | tf_op jit(solution)/shard_map/feed_forward/pallas_call | solution.py:423
  422.7 5.9 %all-to-all-done.2.refs_0_ = bf16[8,1,16,64,128]{4,3,2,1,0:T(8,128)(2,1)} async-done(((bf16[8,1,16,64,128]{4,3,2,1,0:T(8,128)(2,1)}), bf16[8,1,16,64,128]{4,3,2,1,0:T(8,128)(2,1)}, u32[]{:S(2)}, u32[]{:S(2)}) %all-to-all-start.2) | async-done | bytes 2097184 | tf_op jit(solution)/shard_map/all_to_all | solution.py:456
  428.6 21.6 %feed_forward.7 = bf16[64,16,32,128]{3,2,1,0:T(8,128)(2,1)} custom-call(s32[2]{0:T(128)} %pad_add_fusion.me_ref, bf16[64,16,32,128]{3,2,1,0:T(8,128)(2,1)} %x_ref.11, bf16[256,64]{1,0:T(8,128)(2,1)} %bitcast.21, bf16[64,256]{1,0:T(8,128)(2,1)} %bitcast.29, f32[256,1]{1,0:T(8,128)} %copy.64.bin_ref, ...), custom_call_target="tpu_custom_call", output_to_operand_aliasing={{}: (12, {})} | custom-call | flops 24149999616 | tf_op jit(solution)/shard_map/feed_forward/pallas_call | solution.py:423
  (39 shorter events, 7.0 us)
Async XLA Ops:
  7.4 100.4 %all-to-all-start = ((bf16[8,2,64,16,128]{4,3,2,1,0:T(8,128)(2,1)}), bf16[8,2,64,16,128]{4,3,2,1,0:T(8,128)(2,1)}, u32[]{:S(2)}, u32[]{:S(2)}) async-start(bf16[8,2,64,16,128]{4,3,2,1,0:T(8,128)(2,1)} %pack_columns.2.refs_4_.refs_0_), calls=%async_computation | async-start | bytes 8388608 | tf_op jit(solution)/shard_map/all_to_all | solution.py:456
  22.1 192.1 %collective-permute-start.2 = (bf16[4,64,32,128]{3,2,1,0:T(8,128)(2,1)}, bf16[4,64,32,128]{3,2,1,0:T(8,128)(2,1)}, u32[]{:S(2)}, u32[]{:S(2)}) collective-permute-start(bf16[4,64,32,128]{3,2,1,0:T(8,128)(2,1)} %get-tuple-element.24.refs_1_), channel_id=1, source_target_pairs={{0,3},{1,2},{2,1},{3,0},{4,7},{5,6},{6,5},{7,4},{8,11},{9,10},{10,... | collective-permute-start | bytes 6291464 | tf_op jit(solution)/shard_map/ppermute | solution.py:445
  24.5 189.6 %collective-permute-start = (bf16[4,64,32,128]{3,2,1,0:T(8,128)(2,1)}, bf16[4,64,32,128]{3,2,1,0:T(8,128)(2,1)}, u32[]{:S(2)}, u32[]{:S(2)}) collective-permute-start(bf16[4,64,32,128]{3,2,1,0:T(8,128)(2,1)} %get-tuple-element.27), channel_id=1, source_target_pairs={{0,1},{1,0},{2,3},{3,2},{4,5},{5,4},{6,7},{7,6},{8,9},{9,8},{10,11... | collective-permute-start | bytes 6291464 | tf_op jit(solution)/shard_map/ppermute | solution.py:445
  25.0 189.1 %collective-permute-start.1 = (bf16[4,64,32,128]{3,2,1,0:T(8,128)(2,1)}, bf16[4,64,32,128]{3,2,1,0:T(8,128)(2,1)}, u32[]{:S(2)}, u32[]{:S(2)}) collective-permute-start(bf16[4,64,32,128]{3,2,1,0:T(8,128)(2,1)} %get-tuple-element.28), channel_id=1, source_target_pairs={{0,2},{1,3},{2,0},{3,1},{4,6},{5,7},{6,4},{7,5},{8,10},{9,11},{10,... | collective-permute-start | bytes 6291464 | tf_op jit(solution)/shard_map/ppermute | solution.py:445
  26.1 8.7 %copy-start = (bf16[64,128]{0,1:T(8,128)(2,1)}, bf16[64,128]{0,1:T(8,128)(2,1)S(1)}, u32[]{:S(2)}) copy-start(bf16[64,128]{0,1:T(8,128)(2,1)S(1)} %get-tuple-element.44) | copy-start | bytes 49156
  107.8 98.6 %all-to-all-start.1 = ((bf16[8,2,64,16,128]{4,3,2,1,0:T(8,128)(2,1)}), bf16[8,2,64,16,128]{4,3,2,1,0:T(8,128)(2,1)}, u32[]{:S(2)}, u32[]{:S(2)}) async-start(bf16[8,2,64,16,128]{4,3,2,1,0:T(8,128)(2,1)} %pack_columns.3), calls=%async_computation.1 | async-start | bytes 8388608 | tf_op jit(solution)/shard_map/all_to_all | solution.py:456
  182.6 28.5 %copy-start.1 = (bf16[64,128]{0,1:T(8,128)(2,1)S(1)}, bf16[64,128]{0,1:T(8,128)(2,1)}, u32[]{:S(2)}) copy-start(bf16[64,128]{0,1:T(8,128)(2,1)} %copy-done) | copy-start | bytes 49156
  206.4 98.6 %all-to-all-start.4 = ((bf16[8,2,16,64,128]{4,3,2,1,0:T(8,128)(2,1)}), bf16[8,2,16,64,128]{4,3,2,1,0:T(8,128)(2,1)}, u32[]{:S(2)}, u32[]{:S(2)}) async-start(bf16[8,2,16,64,128]{4,3,2,1,0:T(8,128)(2,1)} %line_branch.5.refs_0_), calls=%async_computation.4 | async-start | bytes 8388608 | tf_op jit(solution)/shard_map/all_to_all | solution.py:456
  258.7 65.0 %collective-permute-start.3 = (bf16[4,32,64,128]{3,2,1,0:T(8,128)(2,1)}, bf16[4,32,64,128]{3,2,1,0:T(8,128)(2,1)}, u32[]{:S(2)}, u32[]{:S(2)}) collective-permute-start(bf16[4,32,64,128]{3,2,1,0:T(8,128)(2,1)} %get-tuple-element.34), channel_id=1, source_target_pairs={{0,1},{1,0},{2,3},{3,2},{4,5},{5,4},{6,7},{7,6},{8,9},{9,8},{10,11... | collective-permute-start | bytes 6291464 | tf_op jit(solution)/shard_map/ppermute | solution.py:445
  260.2 92.9 %collective-permute-start.4 = (bf16[4,32,64,128]{3,2,1,0:T(8,128)(2,1)}, bf16[4,32,64,128]{3,2,1,0:T(8,128)(2,1)}, u32[]{:S(2)}, u32[]{:S(2)}) collective-permute-start(bf16[4,32,64,128]{3,2,1,0:T(8,128)(2,1)} %get-tuple-element.35), channel_id=1, source_target_pairs={{0,2},{1,3},{2,0},{3,1},{4,6},{5,7},{6,4},{7,5},{8,10},{9,11},{10,... | collective-permute-start | bytes 6291464 | tf_op jit(solution)/shard_map/ppermute | solution.py:445
  261.7 91.3 %collective-permute-start.5 = (bf16[4,32,64,128]{3,2,1,0:T(8,128)(2,1)}, bf16[4,32,64,128]{3,2,1,0:T(8,128)(2,1)}, u32[]{:S(2)}, u32[]{:S(2)}) collective-permute-start(bf16[4,32,64,128]{3,2,1,0:T(8,128)(2,1)} %get-tuple-element.36), channel_id=1, source_target_pairs={{0,3},{1,2},{2,1},{3,0},{4,7},{5,6},{6,5},{7,4},{8,11},{9,10},{10,... | collective-permute-start | bytes 6291464 | tf_op jit(solution)/shard_map/ppermute | solution.py:445
  274.2 35.4 %copy-start.3 = (f32[256]{0:T(256)S(1)}, f32[256]{0:T(256)}, u32[]{:S(2)}) copy-start(f32[256]{0:T(256)} %param.18) | copy-start | bytes 3076
  274.2 36.2 %copy-start.2 = (bf16[64,256]{1,0:T(8,128)(2,1)S(1)}, bf16[64,256]{1,0:T(8,128)(2,1)}, u32[]{:S(2)}) copy-start(bf16[64,256]{1,0:T(8,128)(2,1)} %param.16) | copy-start | bytes 98308
  274.2 36.9 %copy-start.4 = (f32[64]{0:T(128)S(1)}, f32[64]{0:T(128)}, u32[]{:S(2)}) copy-start(f32[64]{0:T(128)} %param.19) | copy-start | bytes 772
  305.0 69.6 %all-to-all-start.3 = ((bf16[8,1,16,64,128]{4,3,2,1,0:T(8,128)(2,1)}), bf16[8,1,16,64,128]{4,3,2,1,0:T(8,128)(2,1)}, u32[]{:S(2)}, u32[]{:S(2)}) async-start(bf16[8,1,16,64,128]{4,3,2,1,0:T(8,128)(2,1)} %line_branch.8.refs_0_), calls=%async_computation.3 | async-start | bytes 4194304 | tf_op jit(solution)/shard_map/all_to_all | solution.py:456
  374.7 54.0 %all-to-all-start.2 = ((bf16[8,1,16,64,128]{4,3,2,1,0:T(8,128)(2,1)}), bf16[8,1,16,64,128]{4,3,2,1,0:T(8,128)(2,1)}, u32[]{:S(2)}, u32[]{:S(2)}) async-start(bf16[8,1,16,64,128]{4,3,2,1,0:T(8,128)(2,1)} %line_branch.9.refs_6_), calls=%async_computation.2 | async-start | bytes 4194304 | tf_op jit(solution)/shard_map/all_to_all | solution.py:456

commit v4 on v3

--- a/solution.py
+++ b/solution.py
@@ -11,12 +11,12 @@
 MIB = 1024 * 1024
 VMEM_BYTES = 62 * MIB
 PLAN = {
-    "early": 2,
-    "groups": [1, 1],
+    "early": 1,
+    "groups": [2, 1],
     "last": 0,
     "corner": "",
     "pins": {"last1": [("side", -1)]},
-    "cost": {"pack0": 8.0, "pack1": 8.0, "rows": 7.6, "mix": 5.0, "last0": 22.0, "last1": 22.0, "dim1": 20.0, "dim2a": 20.0, "dim2b": 20.0, "late0": 10.0, "late1": 10.0, "ffn0": 21.0, "ffn1": 21.0, "ffn2": 21.0, "ffn3": 21.0},
+    "cost": {"pack0": 4.0, "pack1": 11.0, "rows": 7.6, "mix": 5.0, "last0": 22.0, "last1": 22.0, "dim1": 10.0, "dim2a": 20.0, "dim2b": 20.0, "late0": 20.0, "late1": 10.0, "ffn0": 21.0, "ffn1": 21.0, "ffn2": 21.0, "ffn3": 21.0},
 }
 HALF_ROOT = math.sqrt(0.5)
 
@@ -234,7 +234,7 @@
         outs[step][...] = part.reshape(length, channels, lanes).astype(jnp.bfloat16)
 
 
-def along_lines(kernel_name, pieces, weights, me, begin, count, after, done=None):
+def along_lines(kernel_name, pieces, weights, me, begin, count, after, done=None, held=()):
     stacked = not isinstance(pieces, list)
     if stacked:
         ways, several, channels, length, lanes = pieces.shape
@@ -262,17 +262,20 @@
         out_spec = pl.BlockSpec((None, length, channels, lanes), lambda g: (begin + g, 0, 0, 0))
         out_shape = hbm(several, length, channels, lanes)
     whole = lambda shape: pl.BlockSpec(shape, lambda g: (0,) * len(shape))
-    kept = list(done or ())
+    kept = list(done or ()) + list(held)
+    moved = 0 if done else len(pieces)
     idle = kept + list(after)
+    last = len(idle) + 3 + 2 * len(pieces)
+    elsewhere = pl.BlockSpec(memory_space=pl.ANY)
     return pl.pallas_call(
-        lambda *refs: lines_kernel(ways, *refs[len(idle) :]),
+        lambda *refs: lines_kernel(ways, *refs[len(idle) : last], *refs[-3:]),
         grid=(count,),
-        in_specs=[pl.BlockSpec(memory_space=pl.ANY)] * len(idle)
+        in_specs=[elsewhere] * len(idle)
         + [whole(forward.shape), whole(back.shape), whole(weights.shape)]
         + [in_spec] * len(pieces),
-        out_specs=[out_spec] * len(pieces),
-        out_shape=[out_shape] * len(pieces),
-        input_output_aliases={at: at for at in range(len(kept))},
+        out_specs=[out_spec] * len(pieces) + [elsewhere] * len(held),
+        out_shape=[out_shape] * len(pieces) + [hbm(*array.shape) for array in held],
+        input_output_aliases={at: moved + at for at in range(len(kept))},
         scratch_shapes=[
             pltpu.VMEM((2 * channels * mode_count, lanes), jnp.float32),
             pltpu.VMEM((2 * channels * mode_count, lanes), jnp.float32),
@@ -497,7 +500,6 @@
     parts = along_lines(
         "dim1", early_in, first_mix, None, 0, early_count, [third] + pins("dim1")
     )[0]
-    back = [(trade(parts), early_count)]
     token = parts
     if PLAN["last"] == 1:
         third = last(1, third, [token])
@@ -519,7 +521,10 @@
         across - cut,
         [token] + pins("dim2b"),
         done=second,
-    )
+        held=[parts],
+    )
+    second, parts = second[:-1], second[-1]
+    back = [(trade(parts), early_count)]
     token = second[0]
     second_in = exchange(second, "col")
     seen["second"] = second_in

time: 451 us -> 454 us (level)
    ppermute x6, waiting for transfers between devices: 29.3 us -> 76.4 us  [swap(): return lax.ppermute(piece, axis, [(at, at ^ step) for at in range(ways)])]
    all_to_all x5, waiting for transfers between devices: 134 us -> 89.3 us  [trade(): return lax.all_to_all(stack, 'row', split_axis=0, concat_axis=0)]
  transfers between devices with their start and end apart: 11 -> 11, of which waited for: 5 -> 6; matrix products, arithmetic and copies ran while one was open for 2% -> 2% of each run, Pallas kernels for 48% -> 48%
where the time goes in v4:
time: 454 us; the launch traced here: 453 us
  Pallas kernels  244 us (54%)
  waiting for transfers between devices  166 us (37%)
  starting transfers between devices  32 us (7%)
  local copies, waits for them, and re-layouts  8.63 us (2%)
    all_to_all x5, waiting for transfers between devices, trade(): return lax.all_to_all(stack, 'row', split_axis=0, concat_axis=0)  89.3 us
    pallas_call x4, Pallas kernels, cells(): pl.pallas_call(functools.partial(cell_kernel, col_ways), grid_spec=pltpu....  86.5 us
    pallas_call x5, Pallas kernels, along_lines(): pl.pallas_call(lambda *refs: lines_kernel(ways, *refs[len(idle):last], *r...  85.7 us
    ppermute x6, waiting for transfers between devices, swap(): return lax.ppermute(piece, axis, [(at, at ^ step) for at in range(ways)])  76.4 us
    pallas_call x2, Pallas kernels, last_branch(): pl.pallas_call(lambda *refs: last_kernel(*refs[len(idle):len(idle) + 5],...  44.7 us
    all_to_all x5, starting transfers between devices, trade(): return lax.all_to_all(stack, 'row', split_axis=0, concat_axis=0)  24.9 us
    pallas_call x2, Pallas kernels, pack(): pl.pallas_call(pack_kernel, grid=(count, channels // depth), in_specs=[pl...  14.6 us
  transfers between devices with their start and end apart: 11, of which 6 were waited for; matrix products, arithmetic and copies ran while one was open for 2% of the time, Pallas kernels for 48%

profile of v4, /device:TPU:0, one launch (start us, length us, event | category | flops | bytes accessed | tf_op | source)
XLA Modules:
  0.0 453.0 jit_solution(17966244323839721047)
XLA Ops:
  0.0 4.2 pack_columns.2.refs_4_.refs_0_
  4.2 6.3 %all-to-all-start = ((bf16[8,1,64,16,128]{4,3,2,1,0:T(8,128)(2,1)}), bf16[8,1,64,16,128]{4,3,2,1,0:T(8,128)(2,1)}, u32[]{:S(2)}, u32[]{:S(2)}) async-start(bf16[8,1,64,16,128]{4,3,2,1,0:T(8,128)(2,1)} %pack_columns.2.refs_4_.refs_0_), calls=%async_computation | async-start | bytes 4194304 | tf_op jit(solution)/shard_map/all_to_all | solution.py:459
  11.2 7.8 %rows_first.1 = (bf16[4,64,32,128]{3,2,1,0:T(8,128)(2,1)}, bf16[4,64,32,128]{3,2,1,0:T(8,128)(2,1)}, bf16[4,64,32,128]{3,2,1,0:T(8,128)(2,1)}, bf16[4,64,32,128]{3,2,1,0:T(8,128)(2,1)}) custom-call(s32[2]{0:T(128)} %pad_add_fusion.me_ref, bf16[64,16,32,128]{3,2,1,0:T(8,128)(2,1)} %x_ref.11, bf16[64,16,32,128]{3,2,1,0:T(8,128)(2,1)} %x_ref.11, ...), custom_call_target="tpu_custom_call" | custom-call | flops 8739999744 | tf_op jit(solution)/shard_map/rows_first/pallas_call | solution.py:150
  19.0 2.4 collective-permute-start.2
  24.3 5.0 %mixing_matrices.1 = (bf16[32,128,128]{2,1,0:T(8,128)(2,1)}, bf16[32,128,128]{2,1,0:T(8,128)(2,1)}, bf16[32,128,128]{2,1,0:T(8,128)(2,1)}) custom-call(bf16[4,64,32,128]{3,2,1,0:T(8,128)(2,1)} %get-tuple-element.23._.refs_4_.refs_9_, bf16[2,32,64,64]{3,2,1,0:T(8,128)(2,1)} %refs_0_.3, bf16[2,32,64,64]{3,2,1,0:T(8,128)(2,1)} %refs_1_.3, ...), custom_call_target="tpu_custom_call" | custom-call | flops 5750000128 | tf_op jit(solution)/shard_map/mixing_matrices/pallas_call | solution.py:58
  29.3 10.4 %pack_columns.3 = bf16[8,3,64,16,128]{4,3,2,1,0:T(8,128)(2,1)} custom-call(bf16[64,16,32,128]{3,2,1,0:T(8,128)(2,1)} %x_ref.11, bf16[8,1,64,16,128]{4,3,2,1,0:T(8,128)(2,1)} %pack_columns.2.refs_4_.refs_0_), custom_call_target="tpu_custom_call" | custom-call | flops 12650000384 | tf_op jit(solution)/shard_map/pack_columns/pallas_call | solution.py:122
  39.7 20.0 %all-to-all-done.refs_4_ = bf16[8,1,64,16,128]{4,3,2,1,0:T(8,128)(2,1)} async-done(((bf16[8,1,64,16,128]{4,3,2,1,0:T(8,128)(2,1)}), bf16[8,1,64,16,128]{4,3,2,1,0:T(8,128)(2,1)}, u32[]{:S(2)}, u32[]{:S(2)}) %all-to-all-start) | async-done | bytes 2097184 | tf_op jit(solution)/shard_map/all_to_all | solution.py:459
  59.7 4.7 %all-to-all-start.1 = ((bf16[8,3,64,16,128]{4,3,2,1,0:T(8,128)(2,1)}), bf16[8,3,64,16,128]{4,3,2,1,0:T(8,128)(2,1)}, u32[]{:S(2)}, u32[]{:S(2)}) async-start(bf16[8,3,64,16,128]{4,3,2,1,0:T(8,128)(2,1)} %pack_columns.3), calls=%async_computation.1 | async-start | bytes 12582912 | tf_op jit(solution)/shard_map/all_to_all | solution.py:459
  64.5 22.3 %last_branch.2.refs_0_ = bf16[16,32,64,128]{3,2,1,0:T(8,128)(2,1)} custom-call(bf16[64,128]{1,0:T(8,128)(2,1)} %copy.50.refs_0_.refs_2_.refs_1_, bf16[64,128]{1,0:T(8,128)(2,1)} %copy.51.refs_1_.refs_3_, bf16[32,128,128]{2,1,0:T(8,128)(2,1)} %get-tuple-element.24.refs_2_.refs_4_, bf16[64,16,32,128]{3,2,1,0:T(8,128)(2,1)} %x_ref.11), custom_call_target="tpu_custom_call" | custom-call | flops 25300000768 | tf_op jit(solution)/shard_map/last_branch/pallas_call | solution.py:332
  86.8 22.4 %last_branch.3.refs_0_.refs_5_ = bf16[16,32,64,128]{3,2,1,0:T(8,128)(2,1)} custom-call(bf16[16,32,64,128]{3,2,1,0:T(8,128)(2,1)} %last_branch.2.refs_0_, bf16[4,64,32,128]{3,2,1,0:T(8,128)(2,1)} %get-tuple-element.25.refs_1_, bf16[64,128]{1,0:T(8,128)(2,1)} %copy.50.refs_0_.refs_2_.refs_1_, ...), custom_call_target="tpu_custom_call", output_to_operand_aliasing={{}: (0, {})} | custom-call | flops 25300000768 | tf_op jit(solution)/shard_map/last_branch/pallas_call | solution.py:332
  112.3 11.9 %line_branch.5.refs_0_.refs_4_ = bf16[8,1,16,64,128]{4,3,2,1,0:T(8,128)(2,1)} custom-call(bf16[16,32,64,128]{3,2,1,0:T(8,128)(2,1)} %last_branch.3.refs_0_.refs_5_, bf16[64,128]{1,0:T(8,128)(2,1)} %copy.50.refs_0_.refs_2_.refs_1_, bf16[128,64]{1,0:T(8,128)(2,1)} %bitcast.14, bf16[32,128,128]{2,1,0:T(8,128)(2,1)} %get-tuple-element.26.refs_3_, ...), custom_call_target="tpu_custom_call" | custom-call | flops 11500000256 | tf_op jit(solution)/shard_map/line_branch/pallas_call | solution.py:270
  124.2 20.7 %line_branch.6 = (bf16[4,32,64,128]{3,2,1,0:T(8,128)(2,1)}, bf16[4,32,64,128]{3,2,1,0:T(8,128)(2,1)}, bf16[4,32,64,128]{3,2,1,0:T(8,128)(2,1)}, bf16[4,32,64,128]{3,2,1,0:T(8,128)(2,1)}) custom-call(bf16[8,1,16,64,128]{4,3,2,1,0:T(8,128)(2,1)} %line_branch.5.refs_0_.refs_4_, bf16[64,128]{1,0:T(8,128)(2,1)} %copy.55.refs_1_.refs_6_, ...), custom_call_target="tpu_custom_call" | custom-call | flops 23000000512 | tf_op jit(solution)/shard_map/line_branch/pallas_call | solution.py:270
  144.8 3.1 copy.68.refs_0_
  147.9 20.6 %line_branch.7 = (bf16[4,32,64,128]{3,2,1,0:T(8,128)(2,1)}, bf16[4,32,64,128]{3,2,1,0:T(8,128)(2,1)}, bf16[4,32,64,128]{3,2,1,0:T(8,128)(2,1)}, bf16[4,32,64,128...) custom-call(bf16[4,32,64,128]{3,2,1,0:T(8,128)(2,1)} %copy.68.refs_0, ...), custom_call_target="tpu_custom_call", output_to_operand_aliasing={{0}: (0, {}), {1}: (1, {}), {2}: (2, {}), {3}: (3, {}), {4}... | custom-call | flops 23000000512 | tf_op jit(solution)/shard_map/line_branch/pallas_call | solution.py:270
  168.6 34.9 %all-to-all-done.1.refs_4_ = bf16[8,3,64,16,128]{4,3,2,1,0:T(8,128)(2,1)} async-done(((bf16[8,3,64,16,128]{4,3,2,1,0:T(8,128)(2,1)}), bf16[8,3,64,16,128]{4,3,2,1,0:T(8,128)(2,1)}, u32[]{:S(2)}, u32[]{:S(2)}) %all-to-all-start.1) | async-done | bytes 6291488 | tf_op jit(solution)/shard_map/all_to_all | solution.py:459
  203.4 4.4 all-to-all-start.4
  207.8 20.6 %line_branch.8.refs_0_ = bf16[8,2,16,64,128]{4,3,2,1,0:T(8,128)(2,1)} custom-call(bf16[4,32,64,128]{3,2,1,0:T(8,128)(2,1)} %get-tuple-element.34.refs_0_.refs_1_, bf16[64,128]{1,0:T(8,128)(2,1)} %copy.50.refs_0_.refs_2_.refs_1_, bf16[128,64]{1,0:T(8,128)(2,1)} %bitcast.15, bf16[32,128,128]{2,1,0:T(8,128)(2,1)} %get-tuple-element.26.refs_3_, ...), custom_call_target="tpu_custom_call" | custom-call | flops 23000000512 | tf_op jit(solution)/shard_map/line_branch/pallas_call | solution.py:270
  228.4 28.5 %all-to-all-done.4.refs_0_ = bf16[8,1,16,64,128]{4,3,2,1,0:T(8,128)(2,1)} async-done(((bf16[8,1,16,64,128]{4,3,2,1,0:T(8,128)(2,1)}), bf16[8,1,16,64,128]{4,3,2,1,0:T(8,128)(2,1)}, u32[]{:S(2)}, u32[]{:S(2)}) %all-to-all-start.4) | async-done | bytes 2097184 | tf_op jit(solution)/shard_map/all_to_all | solution.py:459
  256.9 4.7 %all-to-all-start.3 = ((bf16[8,2,16,64,128]{4,3,2,1,0:T(8,128)(2,1)}), bf16[8,2,16,64,128]{4,3,2,1,0:T(8,128)(2,1)}, u32[]{:S(2)}, u32[]{:S(2)}) async-start(bf16[8,2,16,64,128]{4,3,2,1,0:T(8,128)(2,1)} %line_branch.8.refs_0_), calls=%async_computation.3 | async-start | bytes 8388608 | tf_op jit(solution)/shard_map/all_to_all | solution.py:459
  261.6 1.6 collective-permute-start.3
  263.2 1.5 collective-permute-start.4
  265.2 0.8 copy.65.bin_ref
  266.0 0.7 copy.48
  267.4 12.0 %line_branch.9.refs_6_ = bf16[8,1,16,64,128]{4,3,2,1,0:T(8,128)(2,1)} custom-call(bf16[8,2,16,64,128]{4,3,2,1,0:T(8,128)(2,1)} %line_branch.8.refs_0_, bf16[64,128]{1,0:T(8,128)(2,1)} %copy.50.refs_0_.refs_2_.refs_1_, bf16[128,64]{1,0:T(8,128)(2,1)} %bitcast.16, bf16[32,128,128]{2,1,0:T(8,128)(2,1)} %get-tuple-element.26.refs_3_, ...), custom_call_target="tpu_custom_call" | custom-call | flops 11500000256 | tf_op jit(solution)/shard_map/line_branch/pallas_call | solution.py:270
  279.4 31.1 %collective-permute-done.3.refs_2_ = bf16[4,32,64,128]{3,2,1,0:T(8,128)(2,1)} collective-permute-done((bf16[4,32,64,128]{3,2,1,0:T(8,128)(2,1)}, bf16[4,32,64,128]{3,2,1,0:T(8,128)(2,1)}, u32[]{:S(2)}, u32[]{:S(2)}) %collective-permute-start.3) | collective-permute-done | bytes 2097184 | tf_op jit(solution)/shard_map/ppermute | solution.py:448
  310.5 45.3 %collective-permute-done.4.refs_3_ = bf16[4,32,64,128]{3,2,1,0:T(8,128)(2,1)} collective-permute-done((bf16[4,32,64,128]{3,2,1,0:T(8,128)(2,1)}, bf16[4,32,64,128]{3,2,1,0:T(8,128)(2,1)}, u32[]{:S(2)}, u32[]{:S(2)}) %collective-permute-start.4) | collective-permute-done | bytes 2097184 | tf_op jit(solution)/shard_map/ppermute | solution.py:448
  355.8 21.6 %feed_forward.4.refs_6_ = bf16[64,16,32,128]{3,2,1,0:T(8,128)(2,1)} custom-call(s32[2]{0:T(128)} %pad_add_fusion.me_ref, bf16[64,16,32,128]{3,2,1,0:T(8,128)(2,1)} %x_ref.11, bf16[256,64]{1,0:T(8,128)(2,1)} %bitcast.18, bf16[64,256]{1,0:T(8,128)(2,1)} %bitcast.26, f32[256,1]{1,0:T(8,128)} %copy.65.bin_ref, f32[64,1]{1,0:T(8,128)} %copy.66.bout_ref, ...), custom_call_target="tpu_custom_call" | custom-call | flops 24149999616 | tf_op jit(solution)/shard_map/feed_forward/pallas_call | solution.py:426
  377.4 4.8 %all-to-all-start.2 = ((bf16[8,1,16,64,128]{4,3,2,1,0:T(8,128)(2,1)}), bf16[8,1,16,64,128]{4,3,2,1,0:T(8,128)(2,1)}, u32[]{:S(2)}, u32[]{:S(2)}) async-start(bf16[8,1,16,64,128]{4,3,2,1,0:T(8,128)(2,1)} %line_branch.9.refs_6_), calls=%async_computation.2 | async-start | bytes 4194304 | tf_op jit(solution)/shard_map/all_to_all | solution.py:459
  382.2 21.6 %feed_forward.5.refs_6_ = bf16[64,16,32,128]{3,2,1,0:T(8,128)(2,1)} custom-call(s32[2]{0:T(128)} %pad_add_fusion.me_ref, bf16[64,16,32,128]{3,2,1,0:T(8,128)(2,1)} %x_ref.11, bf16[256,64]{1,0:T(8,128)(2,1)} %bitcast.19, bf16[64,256]{1,0:T(8,128)(2,1)} %bitcast.27, f32[256,1]{1,0:T(8,128)} %copy.65.bin_ref, ...), custom_call_target="tpu_custom_call", output_to_operand_aliasing={{}: (12, {})} | custom-call | flops 24149999616 | tf_op jit(solution)/shard_map/feed_forward/pallas_call | solution.py:426
  403.8 21.6 %feed_forward.6.refs_6_ = bf16[64,16,32,128]{3,2,1,0:T(8,128)(2,1)} custom-call(s32[2]{0:T(128)} %pad_add_fusion.me_ref, bf16[64,16,32,128]{3,2,1,0:T(8,128)(2,1)} %x_ref.11, bf16[256,64]{1,0:T(8,128)(2,1)} %bitcast.20, bf16[64,256]{1,0:T(8,128)(2,1)} %bitcast.28, f32[256,1]{1,0:T(8,128)} %copy.65.bin_ref, ...), custom_call_target="tpu_custom_call", output_to_operand_aliasing={{}: (12, {})} | custom-call | flops 24149999616 | tf_op jit(solution)/shard_map/feed_forward/pallas_call | solution.py:426
  425.4 5.9 %all-to-all-done.2.refs_0_ = bf16[8,1,16,64,128]{4,3,2,1,0:T(8,128)(2,1)} async-done(((bf16[8,1,16,64,128]{4,3,2,1,0:T(8,128)(2,1)}), bf16[8,1,16,64,128]{4,3,2,1,0:T(8,128)(2,1)}, u32[]{:S(2)}, u32[]{:S(2)}) %all-to-all-start.2) | async-done | bytes 2097184 | tf_op jit(solution)/shard_map/all_to_all | solution.py:459
  431.4 21.6 %feed_forward.7 = bf16[64,16,32,128]{3,2,1,0:T(8,128)(2,1)} custom-call(s32[2]{0:T(128)} %pad_add_fusion.me_ref, bf16[64,16,32,128]{3,2,1,0:T(8,128)(2,1)} %x_ref.11, bf16[256,64]{1,0:T(8,128)(2,1)} %bitcast.21, bf16[64,256]{1,0:T(8,128)(2,1)} %bitcast.29, f32[256,1]{1,0:T(8,128)} %copy.65.bin_ref, ...), custom_call_target="tpu_custom_call", output_to_operand_aliasing={{}: (12, {})} | custom-call | flops 24149999616 | tf_op jit(solution)/shard_map/feed_forward/pallas_call | solution.py:426
  (37 shorter events, 7.7 us)
Async XLA Ops:
  4.2 55.5 %all-to-all-start = ((bf16[8,1,64,16,128]{4,3,2,1,0:T(8,128)(2,1)}), bf16[8,1,64,16,128]{4,3,2,1,0:T(8,128)(2,1)}, u32[]{:S(2)}, u32[]{:S(2)}) async-start(bf16[8,1,64,16,128]{4,3,2,1,0:T(8,128)(2,1)} %pack_columns.2.refs_4_.refs_0_), calls=%async_computation | async-start | bytes 4194304 | tf_op jit(solution)/shard_map/all_to_all | solution.py:459
  19.0 105.2 %collective-permute-start.2 = (bf16[4,64,32,128]{3,2,1,0:T(8,128)(2,1)}, bf16[4,64,32,128]{3,2,1,0:T(8,128)(2,1)}, u32[]{:S(2)}, u32[]{:S(2)}) collective-permute-start(bf16[4,64,32,128]{3,2,1,0:T(8,128)(2,1)} %get-tuple-element.25.refs_1_), channel_id=1, source_target_pairs={{0,3},{1,2},{2,1},{3,0},{4,7},{5,6},{6,5},{7,4},{8,11},{9,10},{10,... | collective-permute-start | bytes 6291464 | tf_op jit(solution)/shard_map/ppermute | solution.py:448
  21.4 102.7 %collective-permute-start = (bf16[4,64,32,128]{3,2,1,0:T(8,128)(2,1)}, bf16[4,64,32,128]{3,2,1,0:T(8,128)(2,1)}, u32[]{:S(2)}, u32[]{:S(2)}) collective-permute-start(bf16[4,64,32,128]{3,2,1,0:T(8,128)(2,1)} %get-tuple-element.28), channel_id=1, source_target_pairs={{0,1},{1,0},{2,3},{3,2},{4,5},{5,4},{6,7},{7,6},{8,9},{9,8},{10,11... | collective-permute-start | bytes 6291464 | tf_op jit(solution)/shard_map/ppermute | solution.py:448
  21.9 102.2 %collective-permute-start.1 = (bf16[4,64,32,128]{3,2,1,0:T(8,128)(2,1)}, bf16[4,64,32,128]{3,2,1,0:T(8,128)(2,1)}, u32[]{:S(2)}, u32[]{:S(2)}) collective-permute-start(bf16[4,64,32,128]{3,2,1,0:T(8,128)(2,1)} %get-tuple-element.29), channel_id=1, source_target_pairs={{0,2},{1,3},{2,0},{3,1},{4,6},{5,7},{6,4},{7,5},{8,10},{9,11},{10,... | collective-permute-start | bytes 6291464 | tf_op jit(solution)/shard_map/ppermute | solution.py:448
  23.0 86.3 %copy-start = (bf16[64,128]{0,1:T(8,128)(2,1)}, bf16[64,128]{0,1:T(8,128)(2,1)S(1)}, u32[]{:S(2)}) copy-start(bf16[64,128]{0,1:T(8,128)(2,1)S(1)} %get-tuple-element.46) | copy-start | bytes 49156
  59.7 143.7 %all-to-all-start.1 = ((bf16[8,3,64,16,128]{4,3,2,1,0:T(8,128)(2,1)}), bf16[8,3,64,16,128]{4,3,2,1,0:T(8,128)(2,1)}, u32[]{:S(2)}, u32[]{:S(2)}) async-start(bf16[8,3,64,16,128]{4,3,2,1,0:T(8,128)(2,1)} %pack_columns.3), calls=%async_computation.1 | async-start | bytes 12582912 | tf_op jit(solution)/shard_map/all_to_all | solution.py:459
  203.4 53.4 %all-to-all-start.4 = ((bf16[8,1,16,64,128]{4,3,2,1,0:T(8,128)(2,1)}), bf16[8,1,16,64,128]{4,3,2,1,0:T(8,128)(2,1)}, u32[]{:S(2)}, u32[]{:S(2)}) async-start(bf16[8,1,16,64,128]{4,3,2,1,0:T(8,128)(2,1)} %get-tuple-element.38), calls=%async_computation.4 | async-start | bytes 4194304 | tf_op jit(solution)/shard_map/all_to_all | solution.py:459
  228.4 36.8 %copy-start.2 = (f32[256]{0:T(256)S(1)}, f32[256]{0:T(256)}, u32[]{:S(2)}) copy-start(f32[256]{0:T(256)} %param.18) | copy-start | bytes 3076
  228.4 37.6 %copy-start.1 = (bf16[64,256]{1,0:T(8,128)(2,1)S(1)}, bf16[64,256]{1,0:T(8,128)(2,1)}, u32[]{:S(2)}) copy-start(bf16[64,256]{1,0:T(8,128)(2,1)} %param.16) | copy-start | bytes 98308
  228.4 38.3 %copy-start.3 = (f32[64]{0:T(128)S(1)}, f32[64]{0:T(128)}, u32[]{:S(2)}) copy-start(f32[64]{0:T(128)} %param.19) | copy-start | bytes 772
  256.9 120.5 %all-to-all-start.3 = ((bf16[8,2,16,64,128]{4,3,2,1,0:T(8,128)(2,1)}), bf16[8,2,16,64,128]{4,3,2,1,0:T(8,128)(2,1)}, u32[]{:S(2)}, u32[]{:S(2)}) async-start(bf16[8,2,16,64,128]{4,3,2,1,0:T(8,128)(2,1)} %line_branch.8.refs_0_), calls=%async_computation.3 | async-start | bytes 8388608 | tf_op jit(solution)/shard_map/all_to_all | solution.py:459
  261.6 48.9 %collective-permute-start.3 = (bf16[4,32,64,128]{3,2,1,0:T(8,128)(2,1)}, bf16[4,32,64,128]{3,2,1,0:T(8,128)(2,1)}, u32[]{:S(2)}, u32[]{:S(2)}) collective-permute-start(bf16[4,32,64,128]{3,2,1,0:T(8,128)(2,1)} %get-tuple-element.35), channel_id=1, source_target_pairs={{0,1},{1,0},{2,3},{3,2},{4,5},{5,4},{6,7},{7,6},{8,9},{9,8},{10,11... | collective-permute-start | bytes 6291464 | tf_op jit(solution)/shard_map/ppermute | solution.py:448
  263.2 92.6 %collective-permute-start.4 = (bf16[4,32,64,128]{3,2,1,0:T(8,128)(2,1)}, bf16[4,32,64,128]{3,2,1,0:T(8,128)(2,1)}, u32[]{:S(2)}, u32[]{:S(2)}) collective-permute-start(bf16[4,32,64,128]{3,2,1,0:T(8,128)(2,1)} %get-tuple-element.36), channel_id=1, source_target_pairs={{0,2},{1,3},{2,0},{3,1},{4,6},{5,7},{6,4},{7,5},{8,10},{9,11},{10,... | collective-permute-start | bytes 6291464 | tf_op jit(solution)/shard_map/ppermute | solution.py:448
  264.7 91.1 %collective-permute-start.5 = (bf16[4,32,64,128]{3,2,1,0:T(8,128)(2,1)}, bf16[4,32,64,128]{3,2,1,0:T(8,128)(2,1)}, u32[]{:S(2)}, u32[]{:S(2)}) collective-permute-start(bf16[4,32,64,128]{3,2,1,0:T(8,128)(2,1)} %get-tuple-element.37), channel_id=1, source_target_pairs={{0,3},{1,2},{2,1},{3,0},{4,7},{5,6},{6,5},{7,4},{8,11},{9,10},{10,... | collective-permute-start | bytes 6291464 | tf_op jit(solution)/shard_map/ppermute | solution.py:448
  377.4 54.0 %all-to-all-start.2 = ((bf16[8,1,16,64,128]{4,3,2,1,0:T(8,128)(2,1)}), bf16[8,1,16,64,128]{4,3,2,1,0:T(8,128)(2,1)}, u32[]{:S(2)}, u32[]{:S(2)}) async-start(bf16[8,1,16,64,128]{4,3,2,1,0:T(8,128)(2,1)} %line_branch.9.refs_6_), calls=%async_computation.2 | async-start | bytes 4194304 | tf_op jit(solution)/shard_map/all_to_all | solution.py:459

commit v5 on v4

--- a/solution.py
+++ b/solution.py
@@ -11,12 +11,12 @@
 MIB = 1024 * 1024
 VMEM_BYTES = 62 * MIB
 PLAN = {
-    "early": 1,
-    "groups": [2, 1],
+    "early": 2,
+    "groups": [1, 1],
     "last": 0,
     "corner": "",
-    "pins": {"last1": [("side", -1)]},
-    "cost": {"pack0": 4.0, "pack1": 11.0, "rows": 7.6, "mix": 5.0, "last0": 22.0, "last1": 22.0, "dim1": 10.0, "dim2a": 20.0, "dim2b": 20.0, "late0": 20.0, "late1": 10.0, "ffn0": 21.0, "ffn1": 21.0, "ffn2": 21.0, "ffn3": 21.0},
+    "pins": {"late0": [("second", 1), ("second", 2), ("second", 3)]},
+    "cost": {"pack0": 8.0, "pack1": 8.0, "rows": 7.6, "mix": 5.0, "last0": 22.0, "last1": 22.0, "dim1": 20.0, "dim2a": 20.0, "dim2b": 20.0, "late0": 200.0, "late1": 10.0, "ffn0": 21.0, "ffn1": 21.0, "ffn2": 21.0, "ffn3": 21.0},
 }
 HALF_ROOT = math.sqrt(0.5)
 
@@ -477,9 +477,6 @@
 
     early = pack("pack0", field, 0, early_count, ways, [])
     early_in = trade(early)
-    late = pack("pack1", field, early_count, rest, ways, [early])
-    late_in = trade(late)
-    seen["early"], seen["late"] = [early_in], [late_in]
     corner = 3
     side = list(rows_first(field, col_ways, me, early))
     seen["side"] = side_in = exchange(side, "col", skip=corner)
@@ -496,6 +493,7 @@
     third = last(0, None, [])
     if PLAN["last"] == 0:
         third = last(1, third, [])
+    late_in = trade(pack("pack1", field, early_count, rest, ways, [third]))
     side_in[corner] = swap(side[corner], "col", corner)
     parts = along_lines(
         "dim1", early_in, first_mix, None, 0, early_count, [third] + pins("dim1")
@@ -533,12 +531,16 @@
         token = third
     groups = PLAN["groups"] if sum(PLAN["groups"]) == rest else [1] * rest
     begin = 0
+    ready = []
     for at, count in enumerate(groups):
         name = f"late{at}"
-        parts = along_lines(name, late_in, first_mix, None, begin, count, [token] + pins(name))[0]
-        back.append((trade(parts), count))
+        parts, *ready = along_lines(
+            name, late_in, first_mix, None, begin, count, [token] + pins(name), held=ready
+        )
+        ready.append(parts)
         begin += count
         token = parts
+    back += [(trade(parts), count) for parts, count in zip(ready, groups)]
     if PLAN["last"] == 4:
         third = last(1, third, [token])
         token = third

time: 454 us -> 435 us (0.958)
  waiting for transfers between devices: 166 us -> 144 us
    ppermute x6, waiting for transfers between devices: 76.4 us -> 60.7 us  [swap(): return lax.ppermute(piece, axis, [(at, at ^ step) for at in range(ways)])]
    all_to_all x5, waiting for transfers between devices: 89.3 us -> 82.9 us  [trade(): return lax.all_to_all(stack, 'row', split_axis=0, concat_axis=0)]
  transfers between devices with their start and end apart: 11 -> 11, of which waited for: 6 -> 7; matrix products, arithmetic and copies ran while one was open for 2% -> 3% of each run, Pallas kernels for 48% -> 50%
where the time goes in v5:
time: 435 us; the launch traced here: 434 us
  Pallas kernels  244 us (56%)
  waiting for transfers between devices  144 us (33%)
  starting transfers between devices  31.5 us (7%)
  local copies, waits for them, and re-layouts  11.8 us (3%)
    pallas_call x4, Pallas kernels, cells(): pl.pallas_call(functools.partial(cell_kernel, col_ways), grid_spec=pltpu....  86.5 us
    pallas_call x5, Pallas kernels, along_lines(): pl.pallas_call(lambda *refs: lines_kernel(ways, *refs[len(idle):last], *r...  85.7 us
    all_to_all x5, waiting for transfers between devices, trade(): return lax.all_to_all(stack, 'row', split_axis=0, concat_axis=0)  82.9 us
    ppermute x6, waiting for transfers between devices, swap(): return lax.ppermute(piece, axis, [(at, at ^ step) for at in range(ways)])  60.7 us
    pallas_call x2, Pallas kernels, last_branch(): pl.pallas_call(lambda *refs: last_kernel(*refs[len(idle):len(idle) + 5],...  44.7 us
    all_to_all x5, starting transfers between devices, trade(): return lax.all_to_all(stack, 'row', split_axis=0, concat_axis=0)  24.5 us
    pallas_call x2, Pallas kernels, pack(): pl.pallas_call(pack_kernel, grid=(count, channels // depth), in_specs=[pl...  14.8 us
  transfers between devices with their start and end apart: 11, of which 7 were waited for; matrix products, arithmetic and copies ran while one was open for 3% of the time, Pallas kernels for 50%

profile of v5, /device:TPU:0, one launch (start us, length us, event | category | flops | bytes accessed | tf_op | source)
XLA Modules:
  0.0 433.5 jit_solution(6555244728819550976)
XLA Ops:
  0.0 7.4 %pack_columns.2.refs_4_ = bf16[8,2,64,16,128]{4,3,2,1,0:T(8,128)(2,1)} custom-call(bf16[64,16,32,128]{3,2,1,0:T(8,128)(2,1)} %x_ref.11), custom_call_target="tpu_custom_call" | custom-call | flops 9200000000 | tf_op jit(solution)/shard_map/pack_columns/pallas_call | solution.py:122
  7.4 6.3 %all-to-all-start = ((bf16[8,2,64,16,128]{4,3,2,1,0:T(8,128)(2,1)}), bf16[8,2,64,16,128]{4,3,2,1,0:T(8,128)(2,1)}, u32[]{:S(2)}, u32[]{:S(2)}) async-start(bf16[8,2,64,16,128]{4,3,2,1,0:T(8,128)(2,1)} %pack_columns.2.refs_4_), calls=%async_computation | async-start | bytes 8388608 | tf_op jit(solution)/shard_map/all_to_all | solution.py:459
  14.3 7.7 %rows_first.1 = (bf16[4,64,32,128]{3,2,1,0:T(8,128)(2,1)}, bf16[4,64,32,128]{3,2,1,0:T(8,128)(2,1)}, bf16[4,64,32,128]{3,2,1,0:T(8,128)(2,1)}, bf16[4,64,32,128]{3,2,1,0:T(8,128)(2,1)}) custom-call(s32[2]{0:T(128)} %pad_add_fusion.me_ref, bf16[64,16,32,128]{3,2,1,0:T(8,128)(2,1)} %x_ref.11, bf16[64,16,32,128]{3,2,1,0:T(8,128)(2,1)} %x_ref.11, ...), custom_call_target="tpu_custom_call" | custom-call | flops 8739999744 | tf_op jit(solution)/shard_map/rows_first/pallas_call | solution.py:150
  23.5 1.5 collective-permute-start.1
  30.4 5.0 %mixing_matrices.1 = (bf16[32,128,128]{2,1,0:T(8,128)(2,1)}, bf16[32,128,128]{2,1,0:T(8,128)(2,1)}, bf16[32,128,128]{2,1,0:T(8,128)(2,1)}) custom-call(bf16[4,64,32,128]{3,2,1,0:T(8,128)(2,1)} %get-tuple-element.25._.refs_4_.refs_9_, bf16[2,32,64,64]{3,2,1,0:T(8,128)(2,1)} %refs_0_.3, bf16[2,32,64,64]{3,2,1,0:T(8,128)(2,1)} %refs_1_.3, ...), custom_call_target="tpu_custom_call" | custom-call | flops 5750000128 | tf_op jit(solution)/shard_map/mixing_matrices/pallas_call | solution.py:58
  35.4 22.3 %last_branch.2.refs_0_ = bf16[16,32,64,128]{3,2,1,0:T(8,128)(2,1)} custom-call(bf16[64,128]{1,0:T(8,128)(2,1)} %copy.51.refs_0_.refs_1_.refs_4_.refs_2_, bf16[64,128]{1,0:T(8,128)(2,1)} %copy.52.refs_1_.refs_2_, bf16[32,128,128]{2,1,0:T(8,128)(2,1)} %get-tuple-element.26.refs_2_.refs_3_, bf16[64,16,32,128]{3,2,1,0:T(8,128)(2,1)} %x_ref.11), custom_call_target="tpu_custom_call" | custom-call | flops 25300000768 | tf_op jit(solution)/shard_map/last_branch/pallas_call | solution.py:332
  57.8 22.4 %last_branch.3.refs_0_.refs_5_ = bf16[16,32,64,128]{3,2,1,0:T(8,128)(2,1)} custom-call(bf16[16,32,64,128]{3,2,1,0:T(8,128)(2,1)} %last_branch.2.refs_0_, bf16[64,128]{1,0:T(8,128)(2,1)} %copy.51.refs_0_.refs_1_.refs_4_.refs_2_, bf16[64,128]{1,0:T(8,128)(2,1)} %copy.52.refs_1_.refs_2_, ...), custom_call_target="tpu_custom_call", output_to_operand_aliasing={{}: (0, {})} | custom-call | flops 25300000768 | tf_op jit(solution)/shard_map/last_branch/pallas_call | solution.py:332
  80.2 7.4 %pack_columns.3 = bf16[8,2,64,16,128]{4,3,2,1,0:T(8,128)(2,1)} custom-call(bf16[64,16,32,128]{3,2,1,0:T(8,128)(2,1)} %x_ref.11, bf16[16,32,64,128]{3,2,1,0:T(8,128)(2,1)} %last_branch.3.refs_0_.refs_5_), custom_call_target="tpu_custom_call" | custom-call | flops 9200000000 | tf_op jit(solution)/shard_map/pack_columns/pallas_call | solution.py:122
  87.6 20.2 %all-to-all-done.refs_4_ = bf16[8,2,64,16,128]{4,3,2,1,0:T(8,128)(2,1)} async-done(((bf16[8,2,64,16,128]{4,3,2,1,0:T(8,128)(2,1)}), bf16[8,2,64,16,128]{4,3,2,1,0:T(8,128)(2,1)}, u32[]{:S(2)}, u32[]{:S(2)}) %all-to-all-start) | async-done | bytes 4194336 | tf_op jit(solution)/shard_map/all_to_all | solution.py:459
  107.8 4.6 %all-to-all-start.1 = ((bf16[8,2,64,16,128]{4,3,2,1,0:T(8,128)(2,1)}), bf16[8,2,64,16,128]{4,3,2,1,0:T(8,128)(2,1)}, u32[]{:S(2)}, u32[]{:S(2)}) async-start(bf16[8,2,64,16,128]{4,3,2,1,0:T(8,128)(2,1)} %pack_columns.3), calls=%async_computation.1 | async-start | bytes 8388608 | tf_op jit(solution)/shard_map/all_to_all | solution.py:459
  112.4 20.6 %line_branch.5.refs_0_.refs_4_ = bf16[8,2,16,64,128]{4,3,2,1,0:T(8,128)(2,1)} custom-call(bf16[16,32,64,128]{3,2,1,0:T(8,128)(2,1)} %last_branch.3.refs_0_.refs_5_, bf16[64,128]{1,0:T(8,128)(2,1)} %copy.51.refs_0_.refs_1_.refs_4_.refs_2_, bf16[128,64]{1,0:T(8,128)(2,1)} %bitcast.14, bf16[32,128,128]{2,1,0:T(8,128)(2,1)} %get-tuple-element.27.refs_3_.refs_6_.refs_4_, ...), custom_call_target="tpu_custom_call" | custom-call | flops 23000000512 | tf_op jit(solution)/shard_map/line_branch/pallas_call | solution.py:270
  132.9 20.7 %line_branch.6 = (bf16[4,32,64,128]{3,2,1,0:T(8,128)(2,1)}, bf16[4,32,64,128]{3,2,1,0:T(8,128)(2,1)}, bf16[4,32,64,128]{3,2,1,0:T(8,128)(2,1)}, bf16[4,32,64,128]{3,2,1,0:T(8,128)(2,1)}) custom-call(bf16[8,2,16,64,128]{4,3,2,1,0:T(8,128)(2,1)} %line_branch.5.refs_0_.refs_4_, bf16[64,128]{1,0:T(8,128)(2,1)} %copy.56.refs_1_.refs_6_, ...), custom_call_target="tpu_custom_call" | custom-call | flops 23000000512 | tf_op jit(solution)/shard_map/line_branch/pallas_call | solution.py:270
  153.6 3.1 copy.69.refs_0_
  156.7 20.6 %line_branch.7 = (bf16[4,32,64,128]{3,2,1,0:T(8,128)(2,1)}, bf16[4,32,64,128]{3,2,1,0:T(8,128)(2,1)}, bf16[4,32,64,128]{3,2,1,0:T(8,128)(2,1)}, bf16[4,32,64,128...) custom-call(bf16[4,32,64,128]{3,2,1,0:T(8,128)(2,1)} %copy.69.refs_0, ...), custom_call_target="tpu_custom_call", output_to_operand_aliasing={{0}: (0, {}), {1}: (1, {}), {2}: (2, {}), {3}: (3, {}), {4}... | custom-call | flops 23000000512 | tf_op jit(solution)/shard_map/line_branch/pallas_call | solution.py:270
  177.3 1.5 collective-permute-start.3
  178.8 1.5 collective-permute-start.4
  180.8 25.5 %all-to-all-done.1.refs_7_.refs_5_ = bf16[8,2,64,16,128]{4,3,2,1,0:T(8,128)(2,1)} async-done(((bf16[8,2,64,16,128]{4,3,2,1,0:T(8,128)(2,1)}), bf16[8,2,64,16,128]{4,3,2,1,0:T(8,128)(2,1)}, u32[]{:S(2)}, u32[]{:S(2)}) %all-to-all-start.1) | async-done | bytes 4194336 | tf_op jit(solution)/shard_map/all_to_all | solution.py:459
  206.4 4.6 %all-to-all-start.4 = ((bf16[8,2,16,64,128]{4,3,2,1,0:T(8,128)(2,1)}), bf16[8,2,16,64,128]{4,3,2,1,0:T(8,128)(2,1)}, u32[]{:S(2)}, u32[]{:S(2)}) async-start(bf16[8,2,16,64,128]{4,3,2,1,0:T(8,128)(2,1)} %get-tuple-element.42), calls=%async_computation.4 | async-start | bytes 8388608 | tf_op jit(solution)/shard_map/all_to_all | solution.py:459
  211.0 15.1 %collective-permute-done.3.refs_1_.refs_2_ = bf16[4,32,64,128]{3,2,1,0:T(8,128)(2,1)} collective-permute-done((bf16[4,32,64,128]{3,2,1,0:T(8,128)(2,1)}, bf16[4,32,64,128]{3,2,1,0:T(8,128)(2,1)}, u32[]{:S(2)}, u32[]{:S(2)}) %collective-permute-start.3) | collective-permute-done | bytes 2097184 | tf_op jit(solution)/shard_map/ppermute | solution.py:448
  226.1 45.6 %collective-permute-done.4.refs_2_.refs_3_ = bf16[4,32,64,128]{3,2,1,0:T(8,128)(2,1)} collective-permute-done((bf16[4,32,64,128]{3,2,1,0:T(8,128)(2,1)}, bf16[4,32,64,128]{3,2,1,0:T(8,128)(2,1)}, u32[]{:S(2)}, u32[]{:S(2)}) %collective-permute-start.4) | collective-permute-done | bytes 2097184 | tf_op jit(solution)/shard_map/ppermute | solution.py:448
  271.7 11.9 %line_branch.8.refs_1_ = bf16[8,1,16,64,128]{4,3,2,1,0:T(8,128)(2,1)} custom-call(bf16[4,32,64,128]{3,2,1,0:T(8,128)(2,1)} %get-tuple-element.36.refs_0_.refs_1_, bf16[4,32,64,128]{3,2,1,0:T(8,128)(2,1)} %collective-permute-done.3.refs_1_.refs_2_, bf16[4,32,64,128]{3,2,1,0:T(8,128)(2,1)} %collective-permute-done.4.refs_2_.refs_3_, ...), custom_call_target="tpu_custom_call" | custom-call | flops 230000001024 | tf_op jit(solution)/shard_map/line_branch/pallas_call | solution.py:270
  283.6 3.1 copy.74.refs_0_
  286.8 11.9 %line_branch.9 = (bf16[8,1,16,64,128]{4,3,2,1,0:T(8,128)(2,1)}, bf16[8,1,16,64,128]{4,3,2,1,0:T(8,128)(2,1)}) custom-call(bf16[8,1,16,64,128]{4,3,2,1,0:T(8,128)(2,1)} %copy.74.refs_0_, bf16[8,1,16,64,128]{4,3,2,1,0:T(8,128)(2,1)} %line_branch.8.refs_1_, bf16[64,128]{1,0:T(8,128)(2,1)} %copy.51.refs_0_.refs_1_.refs_4_.refs_2_, ...), custom_call_target="tpu_custom_call", output_to_operand_aliasing={{1}: (0, {})} | custom-call | flops 11500000256 | tf_op jit(solution)/shard_map/line_branch/pallas_call | solution.py:270
  298.7 6.3 %all-to-all-done.4.refs_0_ = bf16[8,2,16,64,128]{4,3,2,1,0:T(8,128)(2,1)} async-done(((bf16[8,2,16,64,128]{4,3,2,1,0:T(8,128)(2,1)}), bf16[8,2,16,64,128]{4,3,2,1,0:T(8,128)(2,1)}, u32[]{:S(2)}, u32[]{:S(2)}) %all-to-all-start.4) | async-done | bytes 4194336 | tf_op jit(solution)/shard_map/all_to_all | solution.py:459
  305.0 4.7 %all-to-all-start.3 = ((bf16[8,1,16,64,128]{4,3,2,1,0:T(8,128)(2,1)}), bf16[8,1,16,64,128]{4,3,2,1,0:T(8,128)(2,1)}, u32[]{:S(2)}, u32[]{:S(2)}) async-start(bf16[8,1,16,64,128]{4,3,2,1,0:T(8,128)(2,1)} %get-tuple-element.41), calls=%async_computation.3 | async-start | bytes 4194304 | tf_op jit(solution)/shard_map/all_to_all | solution.py:459
  311.9 21.6 %feed_forward.4.refs_6_ = bf16[64,16,32,128]{3,2,1,0:T(8,128)(2,1)} custom-call(s32[2]{0:T(128)} %pad_add_fusion.me_ref, bf16[64,16,32,128]{3,2,1,0:T(8,128)(2,1)} %x_ref.11, bf16[256,64]{1,0:T(8,128)(2,1)} %bitcast.18, bf16[64,256]{1,0:T(8,128)(2,1)} %bitcast.26, f32[256,1]{1,0:T(8,128)} %copy.66.bin_ref, f32[64,1]{1,0:T(8,128)} %copy.67.bout_ref, ...), custom_call_target="tpu_custom_call" | custom-call | flops 24149999616 | tf_op jit(solution)/shard_map/feed_forward/pallas_call | solution.py:426
  333.5 25.0 %all-to-all-done.3.refs_0_ = bf16[8,1,16,64,128]{4,3,2,1,0:T(8,128)(2,1)} async-done(((bf16[8,1,16,64,128]{4,3,2,1,0:T(8,128)(2,1)}), bf16[8,1,16,64,128]{4,3,2,1,0:T(8,128)(2,1)}, u32[]{:S(2)}, u32[]{:S(2)}) %all-to-all-start.3) | async-done | bytes 2097184 | tf_op jit(solution)/shard_map/all_to_all | solution.py:459
  358.5 4.3 %all-to-all-start.2 = ((bf16[8,1,16,64,128]{4,3,2,1,0:T(8,128)(2,1)}), bf16[8,1,16,64,128]{4,3,2,1,0:T(8,128)(2,1)}, u32[]{:S(2)}, u32[]{:S(2)}) async-start(bf16[8,1,16,64,128]{4,3,2,1,0:T(8,128)(2,1)} %get-tuple-element.40.refs_6_), calls=%async_computation.2 | async-start | bytes 4194304 | tf_op jit(solution)/shard_map/all_to_all | solution.py:459
  362.9 21.6 %feed_forward.5.refs_6_ = bf16[64,16,32,128]{3,2,1,0:T(8,128)(2,1)} custom-call(s32[2]{0:T(128)} %pad_add_fusion.me_ref, bf16[64,16,32,128]{3,2,1,0:T(8,128)(2,1)} %x_ref.11, bf16[256,64]{1,0:T(8,128)(2,1)} %bitcast.19, bf16[64,256]{1,0:T(8,128)(2,1)} %bitcast.27, f32[256,1]{1,0:T(8,128)} %copy.66.bin_ref, ...), custom_call_target="tpu_custom_call", output_to_operand_aliasing={{}: (12, {})} | custom-call | flops 24149999616 | tf_op jit(solution)/shard_map/feed_forward/pallas_call | solution.py:426
  384.5 21.6 %feed_forward.6.refs_6_ = bf16[64,16,32,128]{3,2,1,0:T(8,128)(2,1)} custom-call(s32[2]{0:T(128)} %pad_add_fusion.me_ref, bf16[64,16,32,128]{3,2,1,0:T(8,128)(2,1)} %x_ref.11, bf16[256,64]{1,0:T(8,128)(2,1)} %bitcast.20, bf16[64,256]{1,0:T(8,128)(2,1)} %bitcast.28, f32[256,1]{1,0:T(8,128)} %copy.66.bin_ref, ...), custom_call_target="tpu_custom_call", output_to_operand_aliasing={{}: (12, {})} | custom-call | flops 24149999616 | tf_op jit(solution)/shard_map/feed_forward/pallas_call | solution.py:426
  406.1 5.8 %all-to-all-done.2.refs_0_ = bf16[8,1,16,64,128]{4,3,2,1,0:T(8,128)(2,1)} async-done(((bf16[8,1,16,64,128]{4,3,2,1,0:T(8,128)(2,1)}), bf16[8,1,16,64,128]{4,3,2,1,0:T(8,128)(2,1)}, u32[]{:S(2)}, u32[]{:S(2)}) %all-to-all-start.2) | async-done | bytes 2097184 | tf_op jit(solution)/shard_map/all_to_all | solution.py:459
  411.9 21.6 %feed_forward.7 = bf16[64,16,32,128]{3,2,1,0:T(8,128)(2,1)} custom-call(s32[2]{0:T(128)} %pad_add_fusion.me_ref, bf16[64,16,32,128]{3,2,1,0:T(8,128)(2,1)} %x_ref.11, bf16[256,64]{1,0:T(8,128)(2,1)} %bitcast.21, bf16[64,256]{1,0:T(8,128)(2,1)} %bitcast.29, f32[256,1]{1,0:T(8,128)} %copy.66.bin_ref, ...), custom_call_target="tpu_custom_call", output_to_operand_aliasing={{}: (12, {})} | custom-call | flops 24149999616 | tf_op jit(solution)/shard_map/feed_forward/pallas_call | solution.py:426
  (38 shorter events, 10.2 us)
Async XLA Ops:
  7.4 100.4 %all-to-all-start = ((bf16[8,2,64,16,128]{4,3,2,1,0:T(8,128)(2,1)}), bf16[8,2,64,16,128]{4,3,2,1,0:T(8,128)(2,1)}, u32[]{:S(2)}, u32[]{:S(2)}) async-start(bf16[8,2,64,16,128]{4,3,2,1,0:T(8,128)(2,1)} %pack_columns.2.refs_4_), calls=%async_computation | async-start | bytes 8388608 | tf_op jit(solution)/shard_map/all_to_all | solution.py:459
  22.0 110.9 %collective-permute-start = (bf16[4,64,32,128]{3,2,1,0:T(8,128)(2,1)}, bf16[4,64,32,128]{3,2,1,0:T(8,128)(2,1)}, u32[]{:S(2)}, u32[]{:S(2)}) collective-permute-start(bf16[4,64,32,128]{3,2,1,0:T(8,128)(2,1)} %get-tuple-element.29), channel_id=1, source_target_pairs={{0,1},{1,0},{2,3},{3,2},{4,5},{5,4},{6,7},{7,6},{8,9},{9,8},{10,11... | collective-permute-start | bytes 6291464 | tf_op jit(solution)/shard_map/ppermute | solution.py:448
  23.5 109.4 %collective-permute-start.1 = (bf16[4,64,32,128]{3,2,1,0:T(8,128)(2,1)}, bf16[4,64,32,128]{3,2,1,0:T(8,128)(2,1)}, u32[]{:S(2)}, u32[]{:S(2)}) collective-permute-start(bf16[4,64,32,128]{3,2,1,0:T(8,128)(2,1)} %get-tuple-element.30), channel_id=1, source_target_pairs={{0,2},{1,3},{2,0},{3,1},{4,6},{5,7},{6,4},{7,5},{8,10},{9,11},{10,... | collective-permute-start | bytes 6291464 | tf_op jit(solution)/shard_map/ppermute | solution.py:448
  25.0 107.9 %collective-permute-start.2 = (bf16[4,64,32,128]{3,2,1,0:T(8,128)(2,1)}, bf16[4,64,32,128]{3,2,1,0:T(8,128)(2,1)}, u32[]{:S(2)}, u32[]{:S(2)}) collective-permute-start(bf16[4,64,32,128]{3,2,1,0:T(8,128)(2,1)} %get-tuple-element.31), channel_id=1, source_target_pairs={{0,3},{1,2},{2,1},{3,0},{4,7},{5,6},{6,5},{7,4},{8,11},{9,10},{10,... | collective-permute-start | bytes 6291464 | tf_op jit(solution)/shard_map/ppermute | solution.py:448
  26.0 9.4 %copy-start = (bf16[64,128]{0,1:T(8,128)(2,1)}, bf16[64,128]{0,1:T(8,128)(2,1)S(1)}, u32[]{:S(2)}) copy-start(bf16[64,128]{0,1:T(8,128)(2,1)S(1)} %get-tuple-element.50) | copy-start | bytes 49156
  107.8 98.6 %all-to-all-start.1 = ((bf16[8,2,64,16,128]{4,3,2,1,0:T(8,128)(2,1)}), bf16[8,2,64,16,128]{4,3,2,1,0:T(8,128)(2,1)}, u32[]{:S(2)}, u32[]{:S(2)}) async-start(bf16[8,2,64,16,128]{4,3,2,1,0:T(8,128)(2,1)} %pack_columns.3), calls=%async_computation.1 | async-start | bytes 8388608 | tf_op jit(solution)/shard_map/all_to_all | solution.py:459
  177.3 48.8 %collective-permute-start.3 = (bf16[4,32,64,128]{3,2,1,0:T(8,128)(2,1)}, bf16[4,32,64,128]{3,2,1,0:T(8,128)(2,1)}, u32[]{:S(2)}, u32[]{:S(2)}) collective-permute-start(bf16[4,32,64,128]{3,2,1,0:T(8,128)(2,1)} %get-tuple-element.37), channel_id=1, source_target_pairs={{0,1},{1,0},{2,3},{3,2},{4,5},{5,4},{6,7},{7,6},{8,9},{9,8},{10,11... | collective-permute-start | bytes 6291464 | tf_op jit(solution)/shard_map/ppermute | solution.py:448
  178.8 92.9 %collective-permute-start.4 = (bf16[4,32,64,128]{3,2,1,0:T(8,128)(2,1)}, bf16[4,32,64,128]{3,2,1,0:T(8,128)(2,1)}, u32[]{:S(2)}, u32[]{:S(2)}) collective-permute-start(bf16[4,32,64,128]{3,2,1,0:T(8,128)(2,1)} %get-tuple-element.38), channel_id=1, source_target_pairs={{0,2},{1,3},{2,0},{3,1},{4,6},{5,7},{6,4},{7,5},{8,10},{9,11},{10,... | collective-permute-start | bytes 6291464 | tf_op jit(solution)/shard_map/ppermute | solution.py:448
  180.3 91.3 %collective-permute-start.5 = (bf16[4,32,64,128]{3,2,1,0:T(8,128)(2,1)}, bf16[4,32,64,128]{3,2,1,0:T(8,128)(2,1)}, u32[]{:S(2)}, u32[]{:S(2)}) collective-permute-start(bf16[4,32,64,128]{3,2,1,0:T(8,128)(2,1)} %get-tuple-element.39), channel_id=1, source_target_pairs={{0,3},{1,2},{2,1},{3,0},{4,7},{5,6},{6,5},{7,4},{8,11},{9,10},{10,... | collective-permute-start | bytes 6291464 | tf_op jit(solution)/shard_map/ppermute | solution.py:448
  206.4 98.6 %all-to-all-start.4 = ((bf16[8,2,16,64,128]{4,3,2,1,0:T(8,128)(2,1)}), bf16[8,2,16,64,128]{4,3,2,1,0:T(8,128)(2,1)}, u32[]{:S(2)}, u32[]{:S(2)}) async-start(bf16[8,2,16,64,128]{4,3,2,1,0:T(8,128)(2,1)} %get-tuple-element.42), calls=%async_computation.4 | async-start | bytes 8388608 | tf_op jit(solution)/shard_map/all_to_all | solution.py:459
  305.0 4.7 %copy-start.2 = (f32[256]{0:T(256)S(1)}, f32[256]{0:T(256)}, u32[]{:S(2)}) copy-start(f32[256]{0:T(256)} %param.18) | copy-start | bytes 3076
  305.0 5.5 %copy-start.1 = (bf16[64,256]{1,0:T(8,128)(2,1)S(1)}, bf16[64,256]{1,0:T(8,128)(2,1)}, u32[]{:S(2)}) copy-start(bf16[64,256]{1,0:T(8,128)(2,1)} %param.16) | copy-start | bytes 98308
  305.0 6.2 %copy-start.3 = (f32[64]{0:T(128)S(1)}, f32[64]{0:T(128)}, u32[]{:S(2)}) copy-start(f32[64]{0:T(128)} %param.19) | copy-start | bytes 772
  305.0 53.5 %all-to-all-start.3 = ((bf16[8,1,16,64,128]{4,3,2,1,0:T(8,128)(2,1)}), bf16[8,1,16,64,128]{4,3,2,1,0:T(8,128)(2,1)}, u32[]{:S(2)}, u32[]{:S(2)}) async-start(bf16[8,1,16,64,128]{4,3,2,1,0:T(8,128)(2,1)} %get-tuple-element.41), calls=%async_computation.3 | async-start | bytes 4194304 | tf_op jit(solution)/shard_map/all_to_all | solution.py:459
  358.5 53.4 %all-to-all-start.2 = ((bf16[8,1,16,64,128]{4,3,2,1,0:T(8,128)(2,1)}), bf16[8,1,16,64,128]{4,3,2,1,0:T(8,128)(2,1)}, u32[]{:S(2)}, u32[]{:S(2)}) async-start(bf16[8,1,16,64,128]{4,3,2,1,0:T(8,128)(2,1)} %get-tuple-element.40.refs_6_), calls=%async_computation.2 | async-start | bytes 4194304 | tf_op jit(solution)/shard_map/all_to_all | solution.py:459

commit v6 on v5

--- a/solution.py
+++ b/solution.py
@@ -10,13 +10,23 @@
 
 MIB = 1024 * 1024
 VMEM_BYTES = 62 * MIB
-PLAN = {
-    "early": 2,
-    "groups": [1, 1],
-    "last": 0,
-    "corner": "",
-    "pins": {"late0": [("second", 1), ("second", 2), ("second", 3)]},
-    "cost": {"pack0": 8.0, "pack1": 8.0, "rows": 7.6, "mix": 5.0, "last0": 22.0, "last1": 22.0, "dim1": 20.0, "dim2a": 20.0, "dim2b": 20.0, "late0": 200.0, "late1": 10.0, "ffn0": 21.0, "ffn1": 21.0, "ffn2": 21.0, "ffn3": 21.0},
+COSTS = {
+    "pack0": 8.0,
+    "pack1": 8.0,
+    "rows": 7.6,
+    "mix": 5.0,
+    "last0": 22.0,
+    "last1": 22.0,
+    "dim1": 20.0,
+    "dim2a": 20.0,
+    "dim2b": 20.0,
+    "late0": 200.0,
+    "late1": 10.0,
+    "ffn0": 2.0,
+    "ffn1": 2.0,
+    "ffn2": 60.0,
+    "ffn3": 60.0,
+    "ffn4": 11.0,
 }
 HALF_ROOT = math.sqrt(0.5)
 
@@ -79,7 +89,7 @@
 
 
 def cost(kernel, size):
-    micros = PLAN["cost"].get(kernel, 3.0)
+    micros = COSTS.get(kernel, 3.0)
     return pl.CostEstimate(
         flops=int(micros * 1.15e9), bytes_accessed=int(size), transcendentals=0
     )
@@ -199,11 +209,11 @@
 
 def lines_kernel(ways, ft_ref, it_ref, mix_ref, *refs):
     refs, (spectra, mixed, wide) = refs[:-3], refs[-3:]
-    count = len(refs) // 2
-    pieces, outs = refs[:count], refs[count:]
-    if count < ways:
-        pieces = [pieces[0].at[way] for way in range(ways)]
-        outs = [outs[0].at[way] for way in range(ways)]
+    if len(refs) == 2 * ways:
+        pieces, outs = refs[:ways], [[out] for out in refs[ways:]]
+    else:
+        pieces = [refs[0].at[way] for way in range(ways)]
+        outs = [[out.at[way] for out in refs[1:]] for way in range(ways)]
     channels, length, lanes = pieces[0].shape
     mode_count = mix_ref.shape[0]
     total = ways * length
@@ -230,28 +240,39 @@
 
     lax.fori_loop(0, channels // 2, inverse, 0, unroll=4)
     for step in range(ways):
-        part = wide[pl.ds(step * length * channels, length * channels), :]
-        outs[step][...] = part.reshape(length, channels, lanes).astype(jnp.bfloat16)
-
-
-def along_lines(kernel_name, pieces, weights, me, begin, count, after, done=None, held=()):
+        start = step * length
+        for out in outs[step]:
+            rows = out.shape[0]
+            part = wide[pl.ds(start * channels, rows * channels), :]
+            out[...] = part.reshape(rows, channels, lanes).astype(jnp.bfloat16)
+            start += rows
+
+
+def along_lines(
+    kernel_name, pieces, weights, begin, count, after, me=None, groups=None, outs=None, done=(), held=()
+):
     stacked = not isinstance(pieces, list)
+    mode_count = weights.shape[0]
     if stacked:
         ways, several, channels, length, lanes = pieces.shape
         pieces = [pieces]
     else:
         ways = len(pieces)
         several, channels, length, lanes = pieces[0].shape
-    mode_count = weights.shape[0]
     total = ways * length
     forward = forward_rows(total, mode_count)
     back = inverse_rows(total, mode_count).T
     if stacked:
+        back = back.reshape(ways, groups, length // groups, 2 * mode_count)
+        back = back.swapaxes(1, 2).reshape(total, 2 * mode_count)
         in_spec = pl.BlockSpec(
             (ways, None, channels, length, lanes), lambda g: (0, begin + g, 0, 0, 0)
         )
-        out_spec = pl.BlockSpec((ways, None, length, channels, lanes), lambda g: (0, g, 0, 0, 0))
-        out_shape = hbm(ways, count, length, channels, lanes)
+        out_specs = [
+            pl.BlockSpec((ways, cells, channels, lanes), lambda g, place=place: (0, place + g, 0, 0))
+            for _, cells, place in outs
+        ]
+        out_shape = [hbm(ways, cells, channels, lanes) for cells, _, _ in outs]
     else:
         order = me ^ jnp.arange(ways)
         forward = forward.reshape(2 * mode_count, ways, length)
@@ -259,13 +280,15 @@
         back = back.reshape(ways, length, 2 * mode_count)
         back = jnp.take(back, order, axis=0).reshape(total, 2 * mode_count)
         in_spec = pl.BlockSpec((None, channels, length, lanes), lambda g: (begin + g, 0, 0, 0))
-        out_spec = pl.BlockSpec((None, length, channels, lanes), lambda g: (begin + g, 0, 0, 0))
-        out_shape = hbm(several, length, channels, lanes)
+        out_specs = [
+            pl.BlockSpec((None, length, channels, lanes), lambda g: (begin + g, 0, 0, 0))
+        ] * ways
+        out_shape = [hbm(several, length, channels, lanes)] * ways
     whole = lambda shape: pl.BlockSpec(shape, lambda g: (0,) * len(shape))
-    kept = list(done or ()) + list(held)
-    moved = 0 if done else len(pieces)
-    idle = kept + list(after)
-    last = len(idle) + 3 + 2 * len(pieces)
+    idle = [*done, *held, *after]
+    aliases = {at: at for at in range(len(done))}
+    aliases |= {len(done) + at: len(out_specs) + at for at in range(len(held))}
+    last = len(idle) + 3 + len(pieces) + len(out_specs)
     elsewhere = pl.BlockSpec(memory_space=pl.ANY)
     return pl.pallas_call(
         lambda *refs: lines_kernel(ways, *refs[len(idle) : last], *refs[-3:]),
@@ -273,9 +296,9 @@
         in_specs=[elsewhere] * len(idle)
         + [whole(forward.shape), whole(back.shape), whole(weights.shape)]
         + [in_spec] * len(pieces),
-        out_specs=[out_spec] * len(pieces) + [elsewhere] * len(held),
-        out_shape=[out_shape] * len(pieces) + [hbm(*array.shape) for array in held],
-        input_output_aliases={at: moved + at for at in range(len(kept))},
+        out_specs=out_specs + [elsewhere] * len(held),
+        out_shape=out_shape + [hbm(*array.shape) for array in held],
+        input_output_aliases=aliases,
         scratch_shapes=[
             pltpu.VMEM((2 * channels * mode_count, lanes), jnp.float32),
             pltpu.VMEM((2 * channels * mode_count, lanes), jnp.float32),
@@ -387,18 +410,18 @@
     out_ref[:, 0] = total.astype(jnp.bfloat16)
 
 
-def cells(field, first, which, second, third, ffn, chunk, me, done, after):
+def cells(kernel_name, field, first, base, second, third, ffn, chunk, begin, count, me, done, after):
     channels, rows, cols, lanes = field.shape
     ways, col_ways = first.shape[0], len(second)
     across = rows // col_ways
 
     def row(step, at, me):
-        return (me[1] ^ step) * across + at
+        return (me[1] ^ step) * across + begin + at
 
     def own_row(which):
         def index(step, at, me):
-            now = jnp.where(step == which, at, jnp.where(step < which, 0, across - 1))
-            return now, chunk, 0, 0
+            now = jnp.where(step == which, at, jnp.where(step < which, 0, count - 1))
+            return begin + now, chunk, 0, 0
 
         return pl.BlockSpec((None, ways, channels, lanes), index)
 
@@ -407,8 +430,8 @@
     in_specs = [tile] + [whole(w.shape) for w in ffn]
     in_specs.append(
         pl.BlockSpec(
-            (ways, None, None, channels, lanes),
-            lambda s, a, me: (0, which, row(s, a, me), 0, 0),
+            (ways, None, channels, lanes),
+            lambda s, a, me: (0, base + a * col_ways + (me[1] ^ s), 0, 0),
         )
     )
     in_specs += [own_row(step) for step in range(col_ways)]
@@ -427,7 +450,7 @@
         functools.partial(cell_kernel, col_ways),
         grid_spec=pltpu.PrefetchScalarGridSpec(
             num_scalar_prefetch=1,
-            grid=(col_ways, across),
+            grid=(col_ways, count),
             in_specs=in_specs,
             out_specs=tile,
             scratch_shapes=[
@@ -438,7 +461,7 @@
         out_shape=hbm(*field.shape),
         input_output_aliases=aliases,
         compiler_params=pltpu.CompilerParams(vmem_limit_bytes=VMEM_BYTES),
-        cost_estimate=cost(f"ffn{chunk}", 0),
+        cost_estimate=cost(kernel_name, 0),
         name="feed_forward",
     )(*operands)
 
@@ -448,11 +471,8 @@
     return lax.ppermute(piece, axis, [(at, at ^ step) for at in range(ways)])
 
 
-def exchange(pieces, axis, skip=None):
-    return [
-        swap(piece, axis, step) if step not in (0, skip) else piece
-        for step, piece in enumerate(pieces)
-    ]
+def exchange(pieces, axis):
+    return [swap(piece, axis, step) if step else piece for step, piece in enumerate(pieces)]
 
 
 def trade(stack):
@@ -468,90 +488,76 @@
     across = rows // col_ways
     ffn = (ffn_in.T, ffn_out.T, bias_in[:, None], bias_out[:, None])
 
-    early_count = max(1, min(PLAN["early"], chunks - 1))
+    early_count = max(1, chunks // 2)
     rest = chunks - early_count
-    seen = {}
-
-    def pins(kernel):
-        return [seen[name][place] for name, place in PLAN["pins"].get(kernel, ())]
-
     early = pack("pack0", field, 0, early_count, ways, [])
     early_in = trade(early)
-    corner = 3
-    side = list(rows_first(field, col_ways, me, early))
-    seen["side"] = side_in = exchange(side, "col", skip=corner)
+    side = rows_first(field, col_ways, me, early)
+    side_in = exchange(side, "col")
     first_mix, second_mix, third_mix = mix_rows(side[0], spec_first, spec_second, spec_third)
-
-    def last(part, done, after):
-        name = f"last{part}"
-        held = [side[corner]] if PLAN["corner"] == name else []
-        got = last_branch(name, field, third_mix, part, 2, done, after + pins(name), held)
-        if held:
-            side[corner] = got[1]
-        return got[0]
-
-    third = last(0, None, [])
-    if PLAN["last"] == 0:
-        third = last(1, third, [])
+    (third,) = last_branch("last0", field, third_mix, 0, 2, None, [])
+    (third,) = last_branch("last1", field, third_mix, 1, 2, third, [])
     late_in = trade(pack("pack1", field, early_count, rest, ways, [third]))
-    side_in[corner] = swap(side[corner], "col", corner)
-    parts = along_lines(
-        "dim1", early_in, first_mix, None, 0, early_count, [third] + pins("dim1")
-    )[0]
-    token = parts
-    if PLAN["last"] == 1:
-        third = last(1, third, [token])
-        token = third
+    (parts,) = along_lines(
+        "dim1",
+        early_in,
+        first_mix,
+        0,
+        early_count,
+        [third],
+        groups=col_ways,
+        outs=[(early_count * rows, rows, 0)],
+    )
     cut = across // 2
-    second = along_lines(
-        "dim2a", side_in, second_mix, col_me, 0, cut, [token] + pins("dim2a")
-    )
-    token = second[0]
-    if PLAN["last"] == 2:
-        third = last(1, third, [token])
-        token = third
-    second = along_lines(
-        "dim2b",
-        side_in,
-        second_mix,
-        col_me,
-        cut,
-        across - cut,
-        [token] + pins("dim2b"),
-        done=second,
-        held=[parts],
-    )
-    second, parts = second[:-1], second[-1]
-    back = [(trade(parts), early_count)]
-    token = second[0]
+    second = along_lines("dim2a", side_in, second_mix, 0, cut, [parts], me=col_me)
+    *second, parts = along_lines(
+        "dim2b", side_in, second_mix, cut, across - cut, [], me=col_me, done=second, held=[parts]
+    )
     second_in = exchange(second, "col")
-    seen["second"] = second_in
-    if PLAN["last"] == 3:
-        third = last(1, third, [token])
-        token = third
-    groups = PLAN["groups"] if sum(PLAN["groups"]) == rest else [1] * rest
-    begin = 0
-    ready = []
-    for at, count in enumerate(groups):
-        name = f"late{at}"
-        parts, *ready = along_lines(
-            name, late_in, first_mix, None, begin, count, [token] + pins(name), held=ready
-        )
-        ready.append(parts)
-        begin += count
-        token = parts
-    back += [(trade(parts), count) for parts, count in zip(ready, groups)]
-    if PLAN["last"] == 4:
-        third = last(1, third, [token])
-        token = third
-
-    result, chunk = None, 0
-    for branch, count in back:
-        for which in range(count):
-            result = cells(
-                field, branch, which, second_in, third, ffn, chunk, me, result, token
-            )
-            chunk, token = chunk + 1, None
+    after = [second[0], *second_in[1:]]
+    if rest == 2:
+        half = rows // 2
+        outs = [(rows + half, rows, 0)]
+        (middle,) = along_lines(
+            "late0", late_in, first_mix, 0, 1, after, groups=col_ways, outs=outs
+        )
+        outs = [(rows + half, half, rows // half), (half, half, 0)]
+        middle, end = along_lines(
+            "late1", late_in, first_mix, 1, 1, [], groups=col_ways, outs=outs, done=[middle]
+        )
+        back = [parts, middle, end]
+    else:
+        (late,) = along_lines(
+            "late0", late_in, first_mix, 0, rest, after, groups=col_ways, outs=[(rest * rows, rows, 0)]
+        )
+        back = [parts, late]
+    back = [trade(array) for array in back]
+
+    calls = [(0, chunk * rows, chunk, 0, across) for chunk in range(early_count)]
+    if rest == 2:
+        calls.append((1, 0, early_count, 0, across))
+        calls.append((1, rows, early_count + 1, 0, cut))
+        calls.append((2, 0, early_count + 1, cut, across - cut))
+    else:
+        calls += [(1, at * rows, early_count + at, 0, across) for at in range(rest)]
+    result, token = None, late_in if rest != 2 else end
+    for at, (array, base, chunk, begin, count) in enumerate(calls):
+        result = cells(
+            f"ffn{at}",
+            field,
+            back[array],
+            base,
+            second_in,
+            third,
+            ffn,
+            chunk,
+            begin,
+            count,
+            me,
+            result,
+            token,
+        )
+        token = None
     return result
 
 

time: 435 us -> 433 us (level)
  local copies, waits for them, and re-layouts: 11.8 us -> 5.75 us
    unnamed x11 -> x9, local copies, waits for them, and re-layouts: 6.96 us -> 1.71 us
    pallas_call x4 -> x5, Pallas kernels: 86.5 us -> 89.1 us  [cells(): pl.pallas_call(functools.partial(cell_kernel, col_ways), grid_spec=pltpu....]
  transfers between devices with their start and end apart: 11 -> 11, of which waited for: 7 -> 6; matrix products, arithmetic and copies ran while one was open for 3% -> 2% of each run, Pallas kernels for 50% -> 53%
where the time goes in v6:
time: 433 us; the launch traced here: 431 us
  Pallas kernels  247 us (57%)
  waiting for transfers between devices  144 us (33%)
  starting transfers between devices  30.8 us (7%)
  local copies, waits for them, and re-layouts  5.75 us (1%)
    pallas_call x5, Pallas kernels, cells(): pl.pallas_call(functools.partial(cell_kernel, col_ways), grid_spec=pltpu....  89.1 us
    all_to_all x5, waiting for transfers between devices, trade(): return lax.all_to_all(stack, 'row', split_axis=0, concat_axis=0)  86.7 us
    pallas_call x5, Pallas kernels, along_lines(): pl.pallas_call(lambda *refs: lines_kernel(ways, *refs[len(idle):last], *r...  86 us
    ppermute x6, waiting for transfers between devices, swap(): return lax.ppermute(piece, axis, [(at, at ^ step) for at in range(ways)])  57.8 us
    pallas_call x2, Pallas kernels, last_branch(): pl.pallas_call(lambda *refs: last_kernel(*refs[len(idle):len(idle) + 5],...  44.7 us
    all_to_all x5, starting transfers between devices, trade(): return lax.all_to_all(stack, 'row', split_axis=0, concat_axis=0)  23.8 us
    pallas_call x2, Pallas kernels, pack(): pl.pallas_call(pack_kernel, grid=(count, channels // depth), in_specs=[pl...  14.7 us
  transfers between devices with their start and end apart: 11, of which 6 were waited for; matrix products, arithmetic and copies ran while one was open for 2% of the time, Pallas kernels for 53%

profile of v6, /device:TPU:0, one launch (start us, length us, event | category | flops | bytes accessed | tf_op | source)
XLA Modules:
  0.0 431.4 jit_solution(11776404988815414913)
XLA Ops:
  0.0 7.4 %pack_columns.2.refs_4_ = bf16[8,2,64,16,128]{4,3,2,1,0:T(8,128)(2,1)} custom-call(bf16[64,16,32,128]{3,2,1,0:T(8,128)(2,1)} %x_ref.13), custom_call_target="tpu_custom_call" | custom-call | flops 9200000000 | tf_op jit(solution)/shard_map/pack_columns/pallas_call | solution.py:132
  7.4 6.3 %all-to-all-start = ((bf16[8,2,64,16,128]{4,3,2,1,0:T(8,128)(2,1)}), bf16[8,2,64,16,128]{4,3,2,1,0:T(8,128)(2,1)}, u32[]{:S(2)}, u32[]{:S(2)}) async-start(bf16[8,2,64,16,128]{4,3,2,1,0:T(8,128)(2,1)} %pack_columns.2.refs_4_), calls=%async_computation | async-start | bytes 8388608 | tf_op jit(solution)/shard_map/all_to_all | solution.py:479
  14.3 7.7 %rows_first.1 = (bf16[4,64,32,128]{3,2,1,0:T(8,128)(2,1)}, bf16[4,64,32,128]{3,2,1,0:T(8,128)(2,1)}, bf16[4,64,32,128]{3,2,1,0:T(8,128)(2,1)}, bf16[4,64,32,128]{3,2,1,0:T(8,128)(2,1)}) custom-call(s32[2]{0:T(128)} %pad_add_fusion.me_ref, bf16[64,16,32,128]{3,2,1,0:T(8,128)(2,1)} %x_ref.13, bf16[64,16,32,128]{3,2,1,0:T(8,128)(2,1)} %x_ref.13, ...), custom_call_target="tpu_custom_call" | custom-call | flops 8739999744 | tf_op jit(solution)/shard_map/rows_first/pallas_call | solution.py:160
  22.0 1.5 collective-permute-start
  23.5 1.5 collective-permute-start.1
  30.7 4.9 %mixing_matrices.1 = (bf16[32,128,128]{2,1,0:T(8,128)(2,1)}, bf16[32,128,128]{2,1,0:T(8,128)(2,1)}, bf16[32,128,128]{2,1,0:T(8,128)(2,1)}) custom-call(bf16[4,64,32,128]{3,2,1,0:T(8,128)(2,1)} %get-tuple-element.25._.refs_4_.refs_8_, bf16[2,32,64,64]{3,2,1,0:T(8,128)(2,1)} %refs_0_.3, bf16[2,32,64,64]{3,2,1,0:T(8,128)(2,1)} %refs_1_.3, ...), custom_call_target="tpu_custom_call" | custom-call | flops 5750000128 | tf_op jit(solution)/shard_map/mixing_matrices/pallas_call | solution.py:68
  35.6 22.3 %last_branch.2.refs_0_ = bf16[16,32,64,128]{3,2,1,0:T(8,128)(2,1)} custom-call(bf16[64,128]{1,0:T(8,128)(2,1)} %pad_maximum_fusion.1.refs_0_.refs_1_.refs_4_, bf16[64,128]{1,0:T(8,128)(2,1)} %get-tuple-element.44.refs_1_.refs_2_, bf16[32,128,128]{2,1,0:T(8,128)(2,1)} %get-tuple-element.26.refs_2_.refs_3_, bf16[64,16,32,128]{3,2,1,0:T(8,128)(2,1)} %x_ref.13), custom_call_target="tpu_custom_call" | custom-call | flops 25300000768 | tf_op jit(solution)/shard_map/last_branch/pallas_call | solution.py:355
  57.9 22.4 %last_branch.3.refs_0_.refs_5_ = bf16[16,32,64,128]{3,2,1,0:T(8,128)(2,1)} custom-call(bf16[16,32,64,128]{3,2,1,0:T(8,128)(2,1)} %last_branch.2.refs_0_, bf16[64,128]{1,0:T(8,128)(2,1)} %pad_maximum_fusion.1.refs_0_.refs_1_.refs_4_, bf16[64,128]{1,0:T(8,128)(2,1)} %get-tuple-element.44.refs_1_.refs_2_, ...), custom_call_target="tpu_custom_call", output_to_operand_aliasing={{}: (0, {})} | custom-call | flops 25300000768 | tf_op jit(solution)/shard_map/last_branch/pallas_call | solution.py:355
  80.3 7.4 %pack_columns.3 = bf16[8,2,64,16,128]{4,3,2,1,0:T(8,128)(2,1)} custom-call(bf16[64,16,32,128]{3,2,1,0:T(8,128)(2,1)} %x_ref.13, bf16[16,32,64,128]{3,2,1,0:T(8,128)(2,1)} %last_branch.3.refs_0_.refs_5_), custom_call_target="tpu_custom_call" | custom-call | flops 9200000000 | tf_op jit(solution)/shard_map/pack_columns/pallas_call | solution.py:132
  87.7 20.1 %all-to-all-done.refs_4_ = bf16[8,2,64,16,128]{4,3,2,1,0:T(8,128)(2,1)} async-done(((bf16[8,2,64,16,128]{4,3,2,1,0:T(8,128)(2,1)}), bf16[8,2,64,16,128]{4,3,2,1,0:T(8,128)(2,1)}, u32[]{:S(2)}, u32[]{:S(2)}) %all-to-all-start) | async-done | bytes 4194336 | tf_op jit(solution)/shard_map/all_to_all | solution.py:479
  107.8 4.6 %all-to-all-start.1 = ((bf16[8,2,64,16,128]{4,3,2,1,0:T(8,128)(2,1)}), bf16[8,2,64,16,128]{4,3,2,1,0:T(8,128)(2,1)}, u32[]{:S(2)}, u32[]{:S(2)}) async-start(bf16[8,2,64,16,128]{4,3,2,1,0:T(8,128)(2,1)} %pack_columns.3), calls=%async_computation.1 | async-start | bytes 8388608 | tf_op jit(solution)/shard_map/all_to_all | solution.py:479
  112.4 20.6 %line_branch.5.refs_0_.refs_4_ = bf16[8,32,64,128]{3,2,1,0:T(8,128)(2,1)} custom-call(bf16[16,32,64,128]{3,2,1,0:T(8,128)(2,1)} %last_branch.3.refs_0_.refs_5_, bf16[64,128]{1,0:T(8,128)(2,1)} %pad_maximum_fusion.1.refs_0_.refs_1_.refs_4_, bf16[128,64]{1,0:T(8,128)(2,1)} %bitcast.30, bf16[32,128,128]{2,1,0:T(8,128)(2,1)} %get-tuple-element.27.refs_3_.refs_6_, ...), custom_call_target="tpu_custom_call" | custom-call | flops 23000000512 | tf_op jit(solution)/shard_map/line_branch/pallas_call | solution.py:293
  132.9 20.7 %line_branch.6 = (bf16[4,32,64,128]{3,2,1,0:T(8,128)(2,1)}, bf16[4,32,64,128]{3,2,1,0:T(8,128)(2,1)}, bf16[4,32,64,128]{3,2,1,0:T(8,128)(2,1)}, bf16[4,32,64,128]{3,2,1,0:T(8,128)(2,1)}) custom-call(bf16[8,32,64,128]{3,2,1,0:T(8,128)(2,1)} %line_branch.5.refs_0_.refs_4_, bf16[64,128]{1,0:T(8,128)(2,1)} %copy.32.refs_1_.refs_5_, bf16[128,64]{1,0:T(8,128)(2,1)} %bitcast.33, ...), custom_call_target="tpu_custom_call" | custom-call | flops 23000000512 | tf_op jit(solution)/shard_map/line_branch/pallas_call | solution.py:293
  153.7 20.7 %line_branch.7 = (bf16[4,32,64,128]{3,2,1,0:T(8,128)(2,1)}, bf16[4,32,64,128]{3,2,1,0:T(8,128)(2,1)}, bf16[4,32,64,128]{3,2,1,0:T(8,128)(2,1)}, bf16[4,32,64,128]{3,2,1,0:T(8,128)(2,1)}, bf16[8,32,64,128]{3,2,1,0:T(8,128)(2,1)}) custom-call(bf16[4,32,64,128]{3,2,1,0:T(8,128)(2,1)} %get-tuple-elem, ...), custom_call_target="tpu_custom_call", output_to_operand_aliasing={{0}: (0, {}), {1}: (1, {}), {2}: (2, {}), {3}: (3, {}), {4}... | custom-call | flops 23000000512 | tf_op jit(solution)/shard_map/line_branch/pallas_call | solution.py:293
  174.4 1.5 collective-permute-start.3
  175.9 1.5 collective-permute-start.4
  177.9 28.5 %all-to-all-done.1.refs_7_.refs_4_ = bf16[8,2,64,16,128]{4,3,2,1,0:T(8,128)(2,1)} async-done(((bf16[8,2,64,16,128]{4,3,2,1,0:T(8,128)(2,1)}), bf16[8,2,64,16,128]{4,3,2,1,0:T(8,128)(2,1)}, u32[]{:S(2)}, u32[]{:S(2)}) %all-to-all-start.1) | async-done | bytes 4194336 | tf_op jit(solution)/shard_map/all_to_all | solution.py:479
  206.4 4.6 %all-to-all-start.4 = ((bf16[8,32,64,128]{3,2,1,0:T(8,128)(2,1)}), bf16[8,32,64,128]{3,2,1,0:T(8,128)(2,1)}, u32[]{:S(2)}, u32[]{:S(2)}) async-start(bf16[8,32,64,128]{3,2,1,0:T(8,128)(2,1)} %get-tuple-element.42), calls=%async_computation.4 | async-start | bytes 8388608 | tf_op jit(solution)/shard_map/all_to_all | solution.py:479
  210.9 12.2 %collective-permute-done.3.refs_1_.refs_2_ = bf16[4,32,64,128]{3,2,1,0:T(8,128)(2,1)} collective-permute-done((bf16[4,32,64,128]{3,2,1,0:T(8,128)(2,1)}, bf16[4,32,64,128]{3,2,1,0:T(8,128)(2,1)}, u32[]{:S(2)}, u32[]{:S(2)}) %collective-permute-start.3) | collective-permute-done | bytes 2097184 | tf_op jit(solution)/shard_map/ppermute | solution.py:471
  223.1 45.6 %collective-permute-done.4.refs_2_.refs_3_ = bf16[4,32,64,128]{3,2,1,0:T(8,128)(2,1)} collective-permute-done((bf16[4,32,64,128]{3,2,1,0:T(8,128)(2,1)}, bf16[4,32,64,128]{3,2,1,0:T(8,128)(2,1)}, u32[]{:S(2)}, u32[]{:S(2)}) %collective-permute-start.4) | collective-permute-done | bytes 2097184 | tf_op jit(solution)/shard_map/ppermute | solution.py:471
  268.7 12.0 %line_branch.8.refs_0_ = bf16[8,24,64,128]{3,2,1,0:T(8,128)(2,1)} custom-call(bf16[4,32,64,128]{3,2,1,0:T(8,128)(2,1)} %get-tuple-element.36.refs_0_.refs_1_, bf16[4,32,64,128]{3,2,1,0:T(8,128)(2,1)} %collective-permute-done.3.refs_1_.refs_2_, bf16[4,32,64,128]{3,2,1,0:T(8,128)(2,1)} %collective-permute-done.4.refs_2_.refs_3_, ...), custom_call_target="tpu_custom_call" | custom-call | flops 230000001024 | tf_op jit(solution)/shard_map/line_branch/pallas_call | solution.py:293
  280.7 12.1 %line_branch.9 = (bf16[8,24,64,128]{3,2,1,0:T(8,128)(2,1)}, bf16[8,8,64,128]{3,2,1,0:T(8,128)(2,1)}) custom-call(bf16[8,24,64,128]{3,2,1,0:T(8,128)(2,1)} %line_branch.8.refs_0_, bf16[64,128]{1,0:T(8,128)(2,1)} %pad_maximum_fusion.1.refs_0_.refs_1_.refs_4_, bf16[128,64]{1,0:T(8,128)(2,1)} %bitcast.32, ...), custom_call_target="tpu_custom_call", output_to_operand_aliasing={{0}: (0, {})} | custom-call | flops 11500000256 | tf_op jit(solution)/shard_map/line_branch/pallas_call | solution.py:293
  292.8 12.2 %all-to-all-done.4.refs_0_ = bf16[8,32,64,128]{3,2,1,0:T(8,128)(2,1)} async-done(((bf16[8,32,64,128]{3,2,1,0:T(8,128)(2,1)}), bf16[8,32,64,128]{3,2,1,0:T(8,128)(2,1)}, u32[]{:S(2)}, u32[]{:S(2)}) %all-to-all-start.4) | async-done | bytes 4194336 | tf_op jit(solution)/shard_map/all_to_all | solution.py:479
  305.0 4.8 %all-to-all-start.3 = ((bf16[8,24,64,128]{3,2,1,0:T(8,128)(2,1)}), bf16[8,24,64,128]{3,2,1,0:T(8,128)(2,1)}, u32[]{:S(2)}, u32[]{:S(2)}) async-start(bf16[8,24,64,128]{3,2,1,0:T(8,128)(2,1)} %get-tuple-element.41), calls=%async_computation.3 | async-start | bytes 6291456 | tf_op jit(solution)/shard_map/all_to_all | solution.py:479
  312.0 21.6 %feed_forward.5.refs_6_ = bf16[64,16,32,128]{3,2,1,0:T(8,128)(2,1)} custom-call(s32[2]{0:T(128)} %pad_add_fusion.me_ref, bf16[64,16,32,128]{3,2,1,0:T(8,128)(2,1)} %x_ref.13, bf16[256,64]{1,0:T(8,128)(2,1)} %bitcast.17, bf16[64,256]{1,0:T(8,128)(2,1)} %bitcast.25, f32[256,1]{1,0:T(8,128)} %copy.42.bin_ref, f32[64,1]{1,0:T(8,128)} %copy.43.bout_ref, ...), custom_call_target="tpu_custom_call" | custom-call | flops 2300000000 | tf_op jit(solution)/shard_map/feed_forward/pallas_call | solution.py:449
  333.6 21.6 %feed_forward.6.refs_6_ = bf16[64,16,32,128]{3,2,1,0:T(8,128)(2,1)} custom-call(s32[2]{0:T(128)} %pad_add_fusion.me_ref, bf16[64,16,32,128]{3,2,1,0:T(8,128)(2,1)} %x_ref.13, bf16[256,64]{1,0:T(8,128)(2,1)} %bitcast.18, bf16[64,256]{1,0:T(8,128)(2,1)} %bitcast.26, f32[256,1]{1,0:T(8,128)} %copy.42.bin_ref, ...), custom_call_target="tpu_custom_call", output_to_operand_aliasing={{}: (12, {})} | custom-call | flops 2300000000 | tf_op jit(solution)/shard_map/feed_forward/pallas_call | solution.py:449
  355.2 25.9 %all-to-all-done.3.refs_0_ = bf16[8,24,64,128]{3,2,1,0:T(8,128)(2,1)} async-done(((bf16[8,24,64,128]{3,2,1,0:T(8,128)(2,1)}), bf16[8,24,64,128]{3,2,1,0:T(8,128)(2,1)}, u32[]{:S(2)}, u32[]{:S(2)}) %all-to-all-start.3) | async-done | bytes 3145760 | tf_op jit(solution)/shard_map/all_to_all | solution.py:479
  381.1 3.6 all-to-all-start.2
  384.6 21.6 %feed_forward.7.refs_6_ = bf16[64,16,32,128]{3,2,1,0:T(8,128)(2,1)} custom-call(s32[2]{0:T(128)} %pad_add_fusion.me_ref, bf16[64,16,32,128]{3,2,1,0:T(8,128)(2,1)} %x_ref.13, bf16[256,64]{1,0:T(8,128)(2,1)} %bitcast.19, bf16[64,256]{1,0:T(8,128)(2,1)} %bitcast.27, f32[256,1]{1,0:T(8,128)} %copy.42.bin_ref, ...), custom_call_target="tpu_custom_call", output_to_operand_aliasing={{}: (12, {})} | custom-call | flops 69000003584 | tf_op jit(solution)/shard_map/feed_forward/pallas_call | solution.py:449
  406.3 12.1 %feed_forward.8.refs_6_ = bf16[64,16,32,128]{3,2,1,0:T(8,128)(2,1)} custom-call(s32[2]{0:T(128)} %pad_add_fusion.me_ref, bf16[64,16,32,128]{3,2,1,0:T(8,128)(2,1)} %x_ref.13, bf16[256,64]{1,0:T(8,128)(2,1)} %bitcast.20, bf16[64,256]{1,0:T(8,128)(2,1)} %bitcast.28, f32[256,1]{1,0:T(8,128)} %copy.42.bin_ref, ...), custom_call_target="tpu_custom_call", output_to_operand_aliasing={{}: (12, {})} | custom-call | flops 69000003584 | tf_op jit(solution)/shard_map/feed_forward/pallas_call | solution.py:449
  418.4 1.0 copy-done
  419.4 12.1 %feed_forward.9 = bf16[64,16,32,128]{3,2,1,0:T(8,128)(2,1)} custom-call(s32[2]{0:T(128)} %pad_add_fusion.me_ref, bf16[64,16,32,128]{3,2,1,0:T(8,128)(2,1)} %x_ref.13, bf16[256,64]{1,0:T(8,128)(2,1)} %bitcast.21, bf16[64,256]{1,0:T(8,128)(2,1)} %bitcast.29, f32[256,1]{1,0:T(8,128)} %copy.42.bin_ref, ...), custom_call_target="tpu_custom_call", output_to_operand_aliasing={{}: (12, {})} | custom-call | flops 12650000384 | tf_op jit(solution)/shard_map/feed_forward/pallas_call | solution.py:449
  (37 shorter events, 9.0 us)
Async XLA Ops:
  7.4 100.4 %all-to-all-start = ((bf16[8,2,64,16,128]{4,3,2,1,0:T(8,128)(2,1)}), bf16[8,2,64,16,128]{4,3,2,1,0:T(8,128)(2,1)}, u32[]{:S(2)}, u32[]{:S(2)}) async-start(bf16[8,2,64,16,128]{4,3,2,1,0:T(8,128)(2,1)} %pack_columns.2.refs_4_), calls=%async_computation | async-start | bytes 8388608 | tf_op jit(solution)/shard_map/all_to_all | solution.py:479
  22.0 110.9 %collective-permute-start = (bf16[4,64,32,128]{3,2,1,0:T(8,128)(2,1)}, bf16[4,64,32,128]{3,2,1,0:T(8,128)(2,1)}, u32[]{:S(2)}, u32[]{:S(2)}) collective-permute-start(bf16[4,64,32,128]{3,2,1,0:T(8,128)(2,1)} %get-tuple-element.29), channel_id=1, source_target_pairs={{0,1},{1,0},{2,3},{3,2},{4,5},{5,4},{6,7},{7,6},{8,9},{9,8},{10,11... | collective-permute-start | bytes 6291464 | tf_op jit(solution)/shard_map/ppermute | solution.py:471
  23.5 109.4 %collective-permute-start.1 = (bf16[4,64,32,128]{3,2,1,0:T(8,128)(2,1)}, bf16[4,64,32,128]{3,2,1,0:T(8,128)(2,1)}, u32[]{:S(2)}, u32[]{:S(2)}) collective-permute-start(bf16[4,64,32,128]{3,2,1,0:T(8,128)(2,1)} %get-tuple-element.30), channel_id=1, source_target_pairs={{0,2},{1,3},{2,0},{3,1},{4,6},{5,7},{6,4},{7,5},{8,10},{9,11},{10,... | collective-permute-start | bytes 6291464 | tf_op jit(solution)/shard_map/ppermute | solution.py:471
  25.0 107.9 %collective-permute-start.2 = (bf16[4,64,32,128]{3,2,1,0:T(8,128)(2,1)}, bf16[4,64,32,128]{3,2,1,0:T(8,128)(2,1)}, u32[]{:S(2)}, u32[]{:S(2)}) collective-permute-start(bf16[4,64,32,128]{3,2,1,0:T(8,128)(2,1)} %get-tuple-element.31), channel_id=1, source_target_pairs={{0,3},{1,2},{2,1},{3,0},{4,7},{5,6},{6,5},{7,4},{8,11},{9,10},{10,... | collective-permute-start | bytes 6291464 | tf_op jit(solution)/shard_map/ppermute | solution.py:471
  107.8 98.6 %all-to-all-start.1 = ((bf16[8,2,64,16,128]{4,3,2,1,0:T(8,128)(2,1)}), bf16[8,2,64,16,128]{4,3,2,1,0:T(8,128)(2,1)}, u32[]{:S(2)}, u32[]{:S(2)}) async-start(bf16[8,2,64,16,128]{4,3,2,1,0:T(8,128)(2,1)} %pack_columns.3), calls=%async_computation.1 | async-start | bytes 8388608 | tf_op jit(solution)/shard_map/all_to_all | solution.py:479
  174.4 48.8 %collective-permute-start.3 = (bf16[4,32,64,128]{3,2,1,0:T(8,128)(2,1)}, bf16[4,32,64,128]{3,2,1,0:T(8,128)(2,1)}, u32[]{:S(2)}, u32[]{:S(2)}) collective-permute-start(bf16[4,32,64,128]{3,2,1,0:T(8,128)(2,1)} %get-tuple-element.37), channel_id=1, source_target_pairs={{0,1},{1,0},{2,3},{3,2},{4,5},{5,4},{6,7},{7,6},{8,9},{9,8},{10,11... | collective-permute-start | bytes 6291464 | tf_op jit(solution)/shard_map/ppermute | solution.py:471
  175.9 92.9 %collective-permute-start.4 = (bf16[4,32,64,128]{3,2,1,0:T(8,128)(2,1)}, bf16[4,32,64,128]{3,2,1,0:T(8,128)(2,1)}, u32[]{:S(2)}, u32[]{:S(2)}) collective-permute-start(bf16[4,32,64,128]{3,2,1,0:T(8,128)(2,1)} %get-tuple-element.38), channel_id=1, source_target_pairs={{0,2},{1,3},{2,0},{3,1},{4,6},{5,7},{6,4},{7,5},{8,10},{9,11},{10,... | collective-permute-start | bytes 6291464 | tf_op jit(solution)/shard_map/ppermute | solution.py:471
  177.4 91.3 %collective-permute-start.5 = (bf16[4,32,64,128]{3,2,1,0:T(8,128)(2,1)}, bf16[4,32,64,128]{3,2,1,0:T(8,128)(2,1)}, u32[]{:S(2)}, u32[]{:S(2)}) collective-permute-start(bf16[4,32,64,128]{3,2,1,0:T(8,128)(2,1)} %get-tuple-element.39), channel_id=1, source_target_pairs={{0,3},{1,2},{2,1},{3,0},{4,7},{5,6},{6,5},{7,4},{8,11},{9,10},{10,... | collective-permute-start | bytes 6291464 | tf_op jit(solution)/shard_map/ppermute | solution.py:471
  206.4 98.6 %all-to-all-start.4 = ((bf16[8,32,64,128]{3,2,1,0:T(8,128)(2,1)}), bf16[8,32,64,128]{3,2,1,0:T(8,128)(2,1)}, u32[]{:S(2)}, u32[]{:S(2)}) async-start(bf16[8,32,64,128]{3,2,1,0:T(8,128)(2,1)} %get-tuple-element.42), calls=%async_computation.4 | async-start | bytes 8388608 | tf_op jit(solution)/shard_map/all_to_all | solution.py:479
  304.9 4.8 %copy-start.2 = (f32[256]{0:T(256)S(1)}, f32[256]{0:T(256)}, u32[]{:S(2)}) copy-start(f32[256]{0:T(256)} %param.18) | copy-start | bytes 3076
  304.9 5.6 %copy-start.1 = (bf16[64,256]{1,0:T(8,128)(2,1)S(1)}, bf16[64,256]{1,0:T(8,128)(2,1)}, u32[]{:S(2)}) copy-start(bf16[64,256]{1,0:T(8,128)(2,1)} %param.16) | copy-start | bytes 98308
  305.0 6.3 %copy-start.3 = (f32[64]{0:T(128)S(1)}, f32[64]{0:T(128)}, u32[]{:S(2)}) copy-start(f32[64]{0:T(128)} %param.19) | copy-start | bytes 772
  305.0 76.1 %all-to-all-start.3 = ((bf16[8,24,64,128]{3,2,1,0:T(8,128)(2,1)}), bf16[8,24,64,128]{3,2,1,0:T(8,128)(2,1)}, u32[]{:S(2)}, u32[]{:S(2)}) async-start(bf16[8,24,64,128]{3,2,1,0:T(8,128)(2,1)} %get-tuple-element.41), calls=%async_computation.3 | async-start | bytes 6291456 | tf_op jit(solution)/shard_map/all_to_all | solution.py:479
  381.1 37.3 %all-to-all-start.2 = ((bf16[8,8,64,128]{3,2,1,0:T(8,128)(2,1)}), bf16[8,8,64,128]{3,2,1,0:T(8,128)(2,1)S(1)}, u32[]{:S(2)}, u32[]{:S(2)}) async-start(bf16[8,8,64,128]{3,2,1,0:T(8,128)(2,1)} %get-tuple-element.40.refs_6_), calls=%async_computation.2 | async-start | bytes 2097152 | tf_op jit(solution)/shard_map/all_to_all | solution.py:479
  418.4 1.0 copy-start

commit v7 on v6

--- a/solution.py
+++ b/solution.py
@@ -384,7 +384,7 @@
 def cell_kernel(col_ways, me_ref, x_ref, win_ref, wout_ref, bin_ref, bout_ref, *refs):
     first_ref, second, third_ref = refs[0], refs[1 : 1 + col_ways], refs[1 + col_ways]
     out_ref, now, wide = refs[-3:]
-    channels, _, ways, lanes = x_ref.shape
+    channels, rows, ways, lanes = x_ref.shape
 
     for step in range(col_ways):
 
@@ -392,51 +392,57 @@
         def _():
             now[...] = second[step][...]
 
-    for col in range(0, ways, 2):
-        summed = []
-        for at in range(2):
-            pair = first_ref[col + at].astype(jnp.float32) + now[col + at].astype(jnp.float32)
-            pair = pair.astype(jnp.bfloat16).astype(jnp.float32)
-            total = pair + third_ref[col + at].astype(jnp.float32)
-            summed.append(total.astype(jnp.bfloat16))
-        pre = mm(win_ref[...], jnp.concatenate(summed, axis=1)) + bin_ref[...]
-        hidden = (0.5 * pre * (1.0 + lax.erf(pre * HALF_ROOT))).astype(jnp.bfloat16)
-        result = mm(wout_ref[...], hidden) + bout_ref[...]
-        for at in range(2):
-            wide[pl.ds(col + at, channels, stride=ways), :] = result[
-                :, at * lanes : (at + 1) * lanes
-            ]
-    total = wide[...].reshape(channels, ways, lanes) + x_ref[:, 0].astype(jnp.float32)
-    out_ref[:, 0] = total.astype(jnp.bfloat16)
+    for row in range(rows):
+        for col in range(0, ways, 2):
+            summed = []
+            for place in (col, col + 1):
+                pair = first_ref[place, row].astype(jnp.float32)
+                pair = (pair + now[row, place].astype(jnp.float32)).astype(jnp.bfloat16)
+                total = pair.astype(jnp.float32) + third_ref[row, place].astype(jnp.float32)
+                summed.append(total.astype(jnp.bfloat16))
+            scaled = mm(win_ref[...], jnp.concatenate(summed, axis=1)) * HALF_ROOT + bin_ref[...]
+            hidden = (scaled + scaled * lax.erf(scaled)).astype(jnp.bfloat16)
+            result = mm(wout_ref[...], hidden) * HALF_ROOT + bout_ref[...]
+            for at in range(2):
+                wide[row, pl.ds(col + at, channels, stride=ways), :] = result[
+                    :, at * lanes : (at + 1) * lanes
+                ]
+        total = wide[row].reshape(channels, ways, lanes) + x_ref[:, row].astype(jnp.float32)
+        out_ref[:, row] = total.astype(jnp.bfloat16)
 
 
 def cells(kernel_name, field, first, base, second, third, ffn, chunk, begin, count, me, done, after):
     channels, rows, cols, lanes = field.shape
     ways, col_ways = first.shape[0], len(second)
     across = rows // col_ways
+    block = across // 2
+    first = first.reshape(ways, -1, col_ways, channels, lanes)
+    base, begin, steps = base // (col_ways * block), begin // block, count // block
 
     def row(step, at, me):
-        return (me[1] ^ step) * across + begin + at
+        return (me[1] ^ step) * (across // block) + begin + at
 
     def own_row(which):
         def index(step, at, me):
-            now = jnp.where(step == which, at, jnp.where(step < which, 0, count - 1))
+            now = jnp.where(step == which, at, jnp.where(step < which, 0, steps - 1))
             return begin + now, chunk, 0, 0
 
-        return pl.BlockSpec((None, ways, channels, lanes), index)
+        return pl.BlockSpec((block, ways, channels, lanes), index)
 
     whole = lambda shape: pl.BlockSpec(shape, lambda *_: (0,) * len(shape))
-    tile = pl.BlockSpec((channels, 1, ways, lanes), lambda s, a, me: (0, row(s, a, me), chunk, 0))
+    tile = pl.BlockSpec(
+        (channels, block, ways, lanes), lambda s, a, me: (0, row(s, a, me), chunk, 0)
+    )
     in_specs = [tile] + [whole(w.shape) for w in ffn]
     in_specs.append(
         pl.BlockSpec(
-            (ways, None, channels, lanes),
-            lambda s, a, me: (0, base + a * col_ways + (me[1] ^ s), 0, 0),
+            (ways, block, None, channels, lanes),
+            lambda s, a, me: (0, base + a, me[1] ^ s, 0, 0),
         )
     )
     in_specs += [own_row(step) for step in range(col_ways)]
     in_specs.append(
-        pl.BlockSpec((None, ways, channels, lanes), lambda s, a, me: (row(s, a, me), chunk, 0, 0))
+        pl.BlockSpec((block, ways, channels, lanes), lambda s, a, me: (row(s, a, me), chunk, 0, 0))
     )
     operands = [me, *in_hbm([field]), *ffn, *in_hbm([first, *second, third])]
     aliases = {}
@@ -450,12 +456,12 @@
         functools.partial(cell_kernel, col_ways),
         grid_spec=pltpu.PrefetchScalarGridSpec(
             num_scalar_prefetch=1,
-            grid=(col_ways, count),
+            grid=(col_ways, steps),
             in_specs=in_specs,
             out_specs=tile,
             scratch_shapes=[
-                pltpu.VMEM((ways, channels, lanes), jnp.bfloat16),
-                pltpu.VMEM((channels * ways, lanes), jnp.float32),
+                pltpu.VMEM((block, ways, channels, lanes), jnp.bfloat16),
+                pltpu.VMEM((block, channels * ways, lanes), jnp.float32),
             ],
         ),
         out_shape=hbm(*field.shape),
@@ -486,7 +492,7 @@
     me = jnp.stack([row_me, col_me]).astype(jnp.int32)
     chunks = cols // ways
     across = rows // col_ways
-    ffn = (ffn_in.T, ffn_out.T, bias_in[:, None], bias_out[:, None])
+    ffn = (ffn_in.T, ffn_out.T, bias_in[:, None] * HALF_ROOT, bias_out[:, None])
 
     early_count = max(1, chunks // 2)
     rest = chunks - early_count

time: 433 us -> 428 us (0.988)
  Pallas kernels: 247 us -> 238 us
  waiting for transfers between devices: 144 us -> 149 us
    pallas_call x5, Pallas kernels: 89.1 us -> 80.4 us  [cells(): pl.pallas_call(functools.partial(cell_kernel, col_ways), grid_spec=pltpu....]
  transfers between devices with their start and end apart: 11 -> 11, of which waited for: 6 -> 6; matrix products, arithmetic and copies ran while one was open for 2% -> 2% of each run, Pallas kernels for 53% -> 52%
where the time goes in v7:
time: 428 us; the launch traced here: 427 us
  Pallas kernels  238 us (56%)
  waiting for transfers between devices  149 us (35%)
  starting transfers between devices  30.8 us (7%)
  local copies, waits for them, and re-layouts  5.75 us (1%)
    all_to_all x5, waiting for transfers between devices, trade(): return lax.all_to_all(stack, 'row', split_axis=0, concat_axis=0)  90.8 us
    pallas_call x5, Pallas kernels, along_lines(): pl.pallas_call(lambda *refs: lines_kernel(ways, *refs[len(idle):last], *r...  86 us
    pallas_call x5, Pallas kernels, cells(): pl.pallas_call(functools.partial(cell_kernel, col_ways), grid_spec=pltpu....  80.4 us
    ppermute x6, waiting for transfers between devices, swap(): return lax.ppermute(piece, axis, [(at, at ^ step) for at in range(ways)])  57.8 us
    pallas_call x2, Pallas kernels, last_branch(): pl.pallas_call(lambda *refs: last_kernel(*refs[len(idle):len(idle) + 5],...  44.7 us
    all_to_all x5, starting transfers between devices, trade(): return lax.all_to_all(stack, 'row', split_axis=0, concat_axis=0)  23.8 us
    pallas_call x2, Pallas kernels, pack(): pl.pallas_call(pack_kernel, grid=(count, channels // depth), in_specs=[pl...  14.7 us
  transfers between devices with their start and end apart: 11, of which 6 were waited for; matrix products, arithmetic and copies ran while one was open for 2% of the time, Pallas kernels for 52%

profile of v7, /device:TPU:0, one launch (start us, length us, event | category | flops | bytes accessed | tf_op | source)
XLA Modules:
  0.0 426.9 jit_solution(2568621953196701644)
XLA Ops:
  0.0 7.4 %pack_columns.2.refs_4_ = bf16[8,2,64,16,128]{4,3,2,1,0:T(8,128)(2,1)} custom-call(bf16[64,16,32,128]{3,2,1,0:T(8,128)(2,1)} %x_ref.13), custom_call_target="tpu_custom_call" | custom-call | flops 9200000000 | tf_op jit(solution)/shard_map/pack_columns/pallas_call | solution.py:132
  7.4 6.3 %all-to-all-start = ((bf16[8,2,64,16,128]{4,3,2,1,0:T(8,128)(2,1)}), bf16[8,2,64,16,128]{4,3,2,1,0:T(8,128)(2,1)}, u32[]{:S(2)}, u32[]{:S(2)}) async-start(bf16[8,2,64,16,128]{4,3,2,1,0:T(8,128)(2,1)} %pack_columns.2.refs_4_), calls=%async_computation | async-start | bytes 8388608 | tf_op jit(solution)/shard_map/all_to_all | solution.py:485
  14.3 7.7 %rows_first.1 = (bf16[4,64,32,128]{3,2,1,0:T(8,128)(2,1)}, bf16[4,64,32,128]{3,2,1,0:T(8,128)(2,1)}, bf16[4,64,32,128]{3,2,1,0:T(8,128)(2,1)}, bf16[4,64,32,128]{3,2,1,0:T(8,128)(2,1)}) custom-call(s32[2]{0:T(128)} %pad_add_fusion.me_ref, bf16[64,16,32,128]{3,2,1,0:T(8,128)(2,1)} %x_ref.13, bf16[64,16,32,128]{3,2,1,0:T(8,128)(2,1)} %x_ref.13, ...), custom_call_target="tpu_custom_call" | custom-call | flops 8739999744 | tf_op jit(solution)/shard_map/rows_first/pallas_call | solution.py:160
  22.0 1.5 collective-permute-start
  23.5 1.5 collective-permute-start.1
  30.7 4.9 %mixing_matrices.1 = (bf16[32,128,128]{2,1,0:T(8,128)(2,1)}, bf16[32,128,128]{2,1,0:T(8,128)(2,1)}, bf16[32,128,128]{2,1,0:T(8,128)(2,1)}) custom-call(bf16[4,64,32,128]{3,2,1,0:T(8,128)(2,1)} %get-tuple-element.25._.refs_4_.refs_8_, bf16[2,32,64,64]{3,2,1,0:T(8,128)(2,1)} %refs_0_.3, bf16[2,32,64,64]{3,2,1,0:T(8,128)(2,1)} %refs_1_.3, ...), custom_call_target="tpu_custom_call" | custom-call | flops 5750000128 | tf_op jit(solution)/shard_map/mixing_matrices/pallas_call | solution.py:68
  35.6 22.3 %last_branch.2.refs_0_ = bf16[16,32,64,128]{3,2,1,0:T(8,128)(2,1)} custom-call(bf16[64,128]{1,0:T(8,128)(2,1)} %pad_maximum_fusion.1.refs_0_.refs_1_.refs_4_, bf16[64,128]{1,0:T(8,128)(2,1)} %get-tuple-element.44.refs_1_.refs_2_, bf16[32,128,128]{2,1,0:T(8,128)(2,1)} %get-tuple-element.26.refs_2_.refs_3_, bf16[64,16,32,128]{3,2,1,0:T(8,128)(2,1)} %x_ref.13), custom_call_target="tpu_custom_call" | custom-call | flops 25300000768 | tf_op jit(solution)/shard_map/last_branch/pallas_call | solution.py:355
  57.9 22.4 %last_branch.3.refs_0_.refs_5_ = bf16[16,32,64,128]{3,2,1,0:T(8,128)(2,1)} custom-call(bf16[16,32,64,128]{3,2,1,0:T(8,128)(2,1)} %last_branch.2.refs_0_, bf16[64,128]{1,0:T(8,128)(2,1)} %pad_maximum_fusion.1.refs_0_.refs_1_.refs_4_, bf16[64,128]{1,0:T(8,128)(2,1)} %get-tuple-element.44.refs_1_.refs_2_, ...), custom_call_target="tpu_custom_call", output_to_operand_aliasing={{}: (0, {})} | custom-call | flops 25300000768 | tf_op jit(solution)/shard_map/last_branch/pallas_call | solution.py:355
  80.3 7.4 %pack_columns.3 = bf16[8,2,64,16,128]{4,3,2,1,0:T(8,128)(2,1)} custom-call(bf16[64,16,32,128]{3,2,1,0:T(8,128)(2,1)} %x_ref.13, bf16[16,32,64,128]{3,2,1,0:T(8,128)(2,1)} %last_branch.3.refs_0_.refs_5_), custom_call_target="tpu_custom_call" | custom-call | flops 9200000000 | tf_op jit(solution)/shard_map/pack_columns/pallas_call | solution.py:132
  87.7 20.1 %all-to-all-done.refs_4_ = bf16[8,2,64,16,128]{4,3,2,1,0:T(8,128)(2,1)} async-done(((bf16[8,2,64,16,128]{4,3,2,1,0:T(8,128)(2,1)}), bf16[8,2,64,16,128]{4,3,2,1,0:T(8,128)(2,1)}, u32[]{:S(2)}, u32[]{:S(2)}) %all-to-all-start) | async-done | bytes 4194336 | tf_op jit(solution)/shard_map/all_to_all | solution.py:485
  107.8 4.6 %all-to-all-start.1 = ((bf16[8,2,64,16,128]{4,3,2,1,0:T(8,128)(2,1)}), bf16[8,2,64,16,128]{4,3,2,1,0:T(8,128)(2,1)}, u32[]{:S(2)}, u32[]{:S(2)}) async-start(bf16[8,2,64,16,128]{4,3,2,1,0:T(8,128)(2,1)} %pack_columns.3), calls=%async_computation.1 | async-start | bytes 8388608 | tf_op jit(solution)/shard_map/all_to_all | solution.py:485
  112.4 20.6 %line_branch.5.refs_0_.refs_4_ = bf16[8,32,64,128]{3,2,1,0:T(8,128)(2,1)} custom-call(bf16[16,32,64,128]{3,2,1,0:T(8,128)(2,1)} %last_branch.3.refs_0_.refs_5_, bf16[64,128]{1,0:T(8,128)(2,1)} %pad_maximum_fusion.1.refs_0_.refs_1_.refs_4_, bf16[128,64]{1,0:T(8,128)(2,1)} %bitcast.34, bf16[32,128,128]{2,1,0:T(8,128)(2,1)} %get-tuple-element.27.refs_3_.refs_6_, ...), custom_call_target="tpu_custom_call" | custom-call | flops 23000000512 | tf_op jit(solution)/shard_map/line_branch/pallas_call | solution.py:293
  132.9 20.7 %line_branch.6 = (bf16[4,32,64,128]{3,2,1,0:T(8,128)(2,1)}, bf16[4,32,64,128]{3,2,1,0:T(8,128)(2,1)}, bf16[4,32,64,128]{3,2,1,0:T(8,128)(2,1)}, bf16[4,32,64,128]{3,2,1,0:T(8,128)(2,1)}) custom-call(bf16[8,32,64,128]{3,2,1,0:T(8,128)(2,1)} %line_branch.5.refs_0_.refs_4_, bf16[64,128]{1,0:T(8,128)(2,1)} %copy.32.refs_1_.refs_5_, bf16[128,64]{1,0:T(8,128)(2,1)} %bitcast.37, ...), custom_call_target="tpu_custom_call" | custom-call | flops 23000000512 | tf_op jit(solution)/shard_map/line_branch/pallas_call | solution.py:293
  153.7 20.7 %line_branch.7 = (bf16[4,32,64,128]{3,2,1,0:T(8,128)(2,1)}, bf16[4,32,64,128]{3,2,1,0:T(8,128)(2,1)}, bf16[4,32,64,128]{3,2,1,0:T(8,128)(2,1)}, bf16[4,32,64,128]{3,2,1,0:T(8,128)(2,1)}, bf16[8,32,64,128]{3,2,1,0:T(8,128)(2,1)}) custom-call(bf16[4,32,64,128]{3,2,1,0:T(8,128)(2,1)} %get-tuple-elem, ...), custom_call_target="tpu_custom_call", output_to_operand_aliasing={{0}: (0, {}), {1}: (1, {}), {2}: (2, {}), {3}: (3, {}), {4}... | custom-call | flops 23000000512 | tf_op jit(solution)/shard_map/line_branch/pallas_call | solution.py:293
  174.4 1.5 collective-permute-start.3
  175.9 1.5 collective-permute-start.4
  177.9 28.5 %all-to-all-done.1.refs_7_.refs_4_ = bf16[8,2,64,16,128]{4,3,2,1,0:T(8,128)(2,1)} async-done(((bf16[8,2,64,16,128]{4,3,2,1,0:T(8,128)(2,1)}), bf16[8,2,64,16,128]{4,3,2,1,0:T(8,128)(2,1)}, u32[]{:S(2)}, u32[]{:S(2)}) %all-to-all-start.1) | async-done | bytes 4194336 | tf_op jit(solution)/shard_map/all_to_all | solution.py:485
  206.4 4.6 %all-to-all-start.4 = ((bf16[8,32,64,128]{3,2,1,0:T(8,128)(2,1)}), bf16[8,32,64,128]{3,2,1,0:T(8,128)(2,1)}, u32[]{:S(2)}, u32[]{:S(2)}) async-start(bf16[8,32,64,128]{3,2,1,0:T(8,128)(2,1)} %get-tuple-element.42), calls=%async_computation.4 | async-start | bytes 8388608 | tf_op jit(solution)/shard_map/all_to_all | solution.py:485
  210.9 12.2 %collective-permute-done.3.refs_1_.refs_2_ = bf16[4,32,64,128]{3,2,1,0:T(8,128)(2,1)} collective-permute-done((bf16[4,32,64,128]{3,2,1,0:T(8,128)(2,1)}, bf16[4,32,64,128]{3,2,1,0:T(8,128)(2,1)}, u32[]{:S(2)}, u32[]{:S(2)}) %collective-permute-start.3) | collective-permute-done | bytes 2097184 | tf_op jit(solution)/shard_map/ppermute | solution.py:477
  223.1 45.6 %collective-permute-done.4.refs_2_.refs_3_ = bf16[4,32,64,128]{3,2,1,0:T(8,128)(2,1)} collective-permute-done((bf16[4,32,64,128]{3,2,1,0:T(8,128)(2,1)}, bf16[4,32,64,128]{3,2,1,0:T(8,128)(2,1)}, u32[]{:S(2)}, u32[]{:S(2)}) %collective-permute-start.4) | collective-permute-done | bytes 2097184 | tf_op jit(solution)/shard_map/ppermute | solution.py:477
  268.7 12.0 %line_branch.8.refs_0_ = bf16[8,24,64,128]{3,2,1,0:T(8,128)(2,1)} custom-call(bf16[4,32,64,128]{3,2,1,0:T(8,128)(2,1)} %get-tuple-element.36.refs_0_.refs_1_, bf16[4,32,64,128]{3,2,1,0:T(8,128)(2,1)} %collective-permute-done.3.refs_1_.refs_2_, bf16[4,32,64,128]{3,2,1,0:T(8,128)(2,1)} %collective-permute-done.4.refs_2_.refs_3_, ...), custom_call_target="tpu_custom_call" | custom-call | flops 230000001024 | tf_op jit(solution)/shard_map/line_branch/pallas_call | solution.py:293
  280.7 12.1 %line_branch.9 = (bf16[8,24,64,128]{3,2,1,0:T(8,128)(2,1)}, bf16[8,8,64,128]{3,2,1,0:T(8,128)(2,1)}) custom-call(bf16[8,24,64,128]{3,2,1,0:T(8,128)(2,1)} %line_branch.8.refs_0_, bf16[64,128]{1,0:T(8,128)(2,1)} %pad_maximum_fusion.1.refs_0_.refs_1_.refs_4_, bf16[128,64]{1,0:T(8,128)(2,1)} %bitcast.36, ...), custom_call_target="tpu_custom_call", output_to_operand_aliasing={{0}: (0, {})} | custom-call | flops 11500000256 | tf_op jit(solution)/shard_map/line_branch/pallas_call | solution.py:293
  292.8 12.2 %all-to-all-done.4 = bf16[8,32,64,128]{3,2,1,0:T(8,128)(2,1)} async-done(((bf16[8,32,64,128]{3,2,1,0:T(8,128)(2,1)}), bf16[8,32,64,128]{3,2,1,0:T(8,128)(2,1)}, u32[]{:S(2)}, u32[]{:S(2)}) %all-to-all-start.4) | async-done | bytes 4194336 | tf_op jit(solution)/shard_map/all_to_all | solution.py:485
  305.0 4.8 %all-to-all-start.3 = ((bf16[8,24,64,128]{3,2,1,0:T(8,128)(2,1)}), bf16[8,24,64,128]{3,2,1,0:T(8,128)(2,1)}, u32[]{:S(2)}, u32[]{:S(2)}) async-start(bf16[8,24,64,128]{3,2,1,0:T(8,128)(2,1)} %get-tuple-element.41), calls=%async_computation.3 | async-start | bytes 6291456 | tf_op jit(solution)/shard_map/all_to_all | solution.py:485
  312.0 19.5 %feed_forward.5.refs_6_ = bf16[64,16,32,128]{3,2,1,0:T(8,128)(2,1)} custom-call(s32[2]{0:T(128)} %pad_add_fusion.me_ref, bf16[64,16,32,128]{3,2,1,0:T(8,128)(2,1)} %x_ref.13, bf16[256,64]{1,0:T(8,128)(2,1)} %bitcast.21, bf16[64,256]{1,0:T(8,128)(2,1)} %bitcast.29, f32[256,1]{1,0:T(8,128)} %copy.42.bin_ref, f32[64,1]{1,0:T(8,128)} %copy.43.bout_ref, ...), custom_call_target="tpu_custom_call" | custom-call | flops 2300000000 | tf_op jit(solution)/shard_map/feed_forward/pallas_call | solution.py:455
  331.5 19.5 %feed_forward.6.refs_6_ = bf16[64,16,32,128]{3,2,1,0:T(8,128)(2,1)} custom-call(s32[2]{0:T(128)} %pad_add_fusion.me_ref, bf16[64,16,32,128]{3,2,1,0:T(8,128)(2,1)} %x_ref.13, bf16[256,64]{1,0:T(8,128)(2,1)} %bitcast.22, bf16[64,256]{1,0:T(8,128)(2,1)} %bitcast.30, f32[256,1]{1,0:T(8,128)} %copy.42.bin_ref, ...), custom_call_target="tpu_custom_call", output_to_operand_aliasing={{}: (12, {})} | custom-call | flops 2300000000 | tf_op jit(solution)/shard_map/feed_forward/pallas_call | solution.py:455
  351.0 30.0 %all-to-all-done.3 = bf16[8,24,64,128]{3,2,1,0:T(8,128)(2,1)} async-done(((bf16[8,24,64,128]{3,2,1,0:T(8,128)(2,1)}), bf16[8,24,64,128]{3,2,1,0:T(8,128)(2,1)}, u32[]{:S(2)}, u32[]{:S(2)}) %all-to-all-start.3) | async-done | bytes 3145760 | tf_op jit(solution)/shard_map/all_to_all | solution.py:485
  381.1 3.6 all-to-all-start.2
  384.6 19.6 %feed_forward.7.refs_6_ = bf16[64,16,32,128]{3,2,1,0:T(8,128)(2,1)} custom-call(s32[2]{0:T(128)} %pad_add_fusion.me_ref, bf16[64,16,32,128]{3,2,1,0:T(8,128)(2,1)} %x_ref.13, bf16[256,64]{1,0:T(8,128)(2,1)} %bitcast.23, bf16[64,256]{1,0:T(8,128)(2,1)} %bitcast.31, f32[256,1]{1,0:T(8,128)} %copy.42.bin_ref, ...), custom_call_target="tpu_custom_call", output_to_operand_aliasing={{}: (12, {})} | custom-call | flops 69000003584 | tf_op jit(solution)/shard_map/feed_forward/pallas_call | solution.py:455
  404.2 10.9 %feed_forward.8.refs_6_ = bf16[64,16,32,128]{3,2,1,0:T(8,128)(2,1)} custom-call(s32[2]{0:T(128)} %pad_add_fusion.me_ref, bf16[64,16,32,128]{3,2,1,0:T(8,128)(2,1)} %x_ref.13, bf16[256,64]{1,0:T(8,128)(2,1)} %bitcast.24, bf16[64,256]{1,0:T(8,128)(2,1)} %bitcast.32, f32[256,1]{1,0:T(8,128)} %copy.42.bin_ref, ...), custom_call_target="tpu_custom_call", output_to_operand_aliasing={{}: (12, {})} | custom-call | flops 69000003584 | tf_op jit(solution)/shard_map/feed_forward/pallas_call | solution.py:455
  415.1 1.0 copy-done
  416.0 10.9 %feed_forward.9 = bf16[64,16,32,128]{3,2,1,0:T(8,128)(2,1)} custom-call(s32[2]{0:T(128)} %pad_add_fusion.me_ref, bf16[64,16,32,128]{3,2,1,0:T(8,128)(2,1)} %x_ref.13, bf16[256,64]{1,0:T(8,128)(2,1)} %bitcast.25, bf16[64,256]{1,0:T(8,128)(2,1)} %bitcast.33, f32[256,1]{1,0:T(8,128)} %copy.42.bin_ref, ...), custom_call_target="tpu_custom_call", output_to_operand_aliasing={{}: (12, {})} | custom-call | flops 12650000384 | tf_op jit(solution)/shard_map/feed_forward/pallas_call | solution.py:455
  (38 shorter events, 9.0 us)
Async XLA Ops:
  7.4 100.4 %all-to-all-start = ((bf16[8,2,64,16,128]{4,3,2,1,0:T(8,128)(2,1)}), bf16[8,2,64,16,128]{4,3,2,1,0:T(8,128)(2,1)}, u32[]{:S(2)}, u32[]{:S(2)}) async-start(bf16[8,2,64,16,128]{4,3,2,1,0:T(8,128)(2,1)} %pack_columns.2.refs_4_), calls=%async_computation | async-start | bytes 8388608 | tf_op jit(solution)/shard_map/all_to_all | solution.py:485
  22.0 110.9 %collective-permute-start = (bf16[4,64,32,128]{3,2,1,0:T(8,128)(2,1)}, bf16[4,64,32,128]{3,2,1,0:T(8,128)(2,1)}, u32[]{:S(2)}, u32[]{:S(2)}) collective-permute-start(bf16[4,64,32,128]{3,2,1,0:T(8,128)(2,1)} %get-tuple-element.29), channel_id=1, source_target_pairs={{0,1},{1,0},{2,3},{3,2},{4,5},{5,4},{6,7},{7,6},{8,9},{9,8},{10,11... | collective-permute-start | bytes 6291464 | tf_op jit(solution)/shard_map/ppermute | solution.py:477
  23.5 109.4 %collective-permute-start.1 = (bf16[4,64,32,128]{3,2,1,0:T(8,128)(2,1)}, bf16[4,64,32,128]{3,2,1,0:T(8,128)(2,1)}, u32[]{:S(2)}, u32[]{:S(2)}) collective-permute-start(bf16[4,64,32,128]{3,2,1,0:T(8,128)(2,1)} %get-tuple-element.30), channel_id=1, source_target_pairs={{0,2},{1,3},{2,0},{3,1},{4,6},{5,7},{6,4},{7,5},{8,10},{9,11},{10,... | collective-permute-start | bytes 6291464 | tf_op jit(solution)/shard_map/ppermute | solution.py:477
  25.0 107.9 %collective-permute-start.2 = (bf16[4,64,32,128]{3,2,1,0:T(8,128)(2,1)}, bf16[4,64,32,128]{3,2,1,0:T(8,128)(2,1)}, u32[]{:S(2)}, u32[]{:S(2)}) collective-permute-start(bf16[4,64,32,128]{3,2,1,0:T(8,128)(2,1)} %get-tuple-element.31), channel_id=1, source_target_pairs={{0,3},{1,2},{2,1},{3,0},{4,7},{5,6},{6,5},{7,4},{8,11},{9,10},{10,... | collective-permute-start | bytes 6291464 | tf_op jit(solution)/shard_map/ppermute | solution.py:477
  107.8 98.6 %all-to-all-start.1 = ((bf16[8,2,64,16,128]{4,3,2,1,0:T(8,128)(2,1)}), bf16[8,2,64,16,128]{4,3,2,1,0:T(8,128)(2,1)}, u32[]{:S(2)}, u32[]{:S(2)}) async-start(bf16[8,2,64,16,128]{4,3,2,1,0:T(8,128)(2,1)} %pack_columns.3), calls=%async_computation.1 | async-start | bytes 8388608 | tf_op jit(solution)/shard_map/all_to_all | solution.py:485
  174.4 48.8 %collective-permute-start.3 = (bf16[4,32,64,128]{3,2,1,0:T(8,128)(2,1)}, bf16[4,32,64,128]{3,2,1,0:T(8,128)(2,1)}, u32[]{:S(2)}, u32[]{:S(2)}) collective-permute-start(bf16[4,32,64,128]{3,2,1,0:T(8,128)(2,1)} %get-tuple-element.37), channel_id=1, source_target_pairs={{0,1},{1,0},{2,3},{3,2},{4,5},{5,4},{6,7},{7,6},{8,9},{9,8},{10,11... | collective-permute-start | bytes 6291464 | tf_op jit(solution)/shard_map/ppermute | solution.py:477
  175.9 92.9 %collective-permute-start.4 = (bf16[4,32,64,128]{3,2,1,0:T(8,128)(2,1)}, bf16[4,32,64,128]{3,2,1,0:T(8,128)(2,1)}, u32[]{:S(2)}, u32[]{:S(2)}) collective-permute-start(bf16[4,32,64,128]{3,2,1,0:T(8,128)(2,1)} %get-tuple-element.38), channel_id=1, source_target_pairs={{0,2},{1,3},{2,0},{3,1},{4,6},{5,7},{6,4},{7,5},{8,10},{9,11},{10,... | collective-permute-start | bytes 6291464 | tf_op jit(solution)/shard_map/ppermute | solution.py:477
  177.4 91.3 %collective-permute-start.5 = (bf16[4,32,64,128]{3,2,1,0:T(8,128)(2,1)}, bf16[4,32,64,128]{3,2,1,0:T(8,128)(2,1)}, u32[]{:S(2)}, u32[]{:S(2)}) collective-permute-start(bf16[4,32,64,128]{3,2,1,0:T(8,128)(2,1)} %get-tuple-element.39), channel_id=1, source_target_pairs={{0,3},{1,2},{2,1},{3,0},{4,7},{5,6},{6,5},{7,4},{8,11},{9,10},{10,... | collective-permute-start | bytes 6291464 | tf_op jit(solution)/shard_map/ppermute | solution.py:477
  206.4 98.6 %all-to-all-start.4 = ((bf16[8,32,64,128]{3,2,1,0:T(8,128)(2,1)}), bf16[8,32,64,128]{3,2,1,0:T(8,128)(2,1)}, u32[]{:S(2)}, u32[]{:S(2)}) async-start(bf16[8,32,64,128]{3,2,1,0:T(8,128)(2,1)} %get-tuple-element.42), calls=%async_computation.4 | async-start | bytes 8388608 | tf_op jit(solution)/shard_map/all_to_all | solution.py:485
  304.9 4.8 %copy-start.2 = (f32[256]{0:T(256)S(1)}, f32[256]{0:T(256)}, u32[]{:S(2)}) copy-start(f32[256]{0:T(256)} %param.18) | copy-start | bytes 3076
  304.9 5.6 %copy-start.1 = (bf16[64,256]{1,0:T(8,128)(2,1)S(1)}, bf16[64,256]{1,0:T(8,128)(2,1)}, u32[]{:S(2)}) copy-start(bf16[64,256]{1,0:T(8,128)(2,1)} %param.16) | copy-start | bytes 98308
  305.0 6.3 %copy-start.3 = (f32[64]{0:T(128)S(1)}, f32[64]{0:T(128)}, u32[]{:S(2)}) copy-start(f32[64]{0:T(128)} %param.19) | copy-start | bytes 772
  305.0 76.1 %all-to-all-start.3 = ((bf16[8,24,64,128]{3,2,1,0:T(8,128)(2,1)}), bf16[8,24,64,128]{3,2,1,0:T(8,128)(2,1)}, u32[]{:S(2)}, u32[]{:S(2)}) async-start(bf16[8,24,64,128]{3,2,1,0:T(8,128)(2,1)} %get-tuple-element.41), calls=%async_computation.3 | async-start | bytes 6291456 | tf_op jit(solution)/shard_map/all_to_all | solution.py:485
  381.1 34.0 %all-to-all-start.2 = ((bf16[8,8,64,128]{3,2,1,0:T(8,128)(2,1)}), bf16[8,8,64,128]{3,2,1,0:T(8,128)(2,1)S(1)}, u32[]{:S(2)}, u32[]{:S(2)}) async-start(bf16[8,8,64,128]{3,2,1,0:T(8,128)(2,1)} %get-tuple-element.40.refs_6_), calls=%async_computation.2 | async-start | bytes 2097152 | tf_op jit(solution)/shard_map/all_to_all | solution.py:485
  415.1 1.0 copy-start

commit v8 on v7

--- a/solution.py
+++ b/solution.py
@@ -415,7 +415,7 @@
     channels, rows, cols, lanes = field.shape
     ways, col_ways = first.shape[0], len(second)
     across = rows // col_ways
-    block = across // 2
+    block = 2 if begin % 2 == 0 and count % 2 == 0 else 1
     first = first.reshape(ways, -1, col_ways, channels, lanes)
     base, begin, steps = base // (col_ways * block), begin // block, count // block
 
@@ -521,17 +521,31 @@
     )
     second_in = exchange(second, "col")
     after = [second[0], *second_in[1:]]
+    small = max(1, across // 4)
     if rest == 2:
-        half = rows // 2
-        outs = [(rows + half, rows, 0)]
         (middle,) = along_lines(
-            "late0", late_in, first_mix, 0, 1, after, groups=col_ways, outs=outs
-        )
-        outs = [(rows + half, half, rows // half), (half, half, 0)]
-        middle, end = along_lines(
-            "late1", late_in, first_mix, 1, 1, [], groups=col_ways, outs=outs, done=[middle]
-        )
-        back = [parts, middle, end]
+            "late0",
+            late_in,
+            first_mix,
+            0,
+            1,
+            after,
+            groups=col_ways,
+            outs=[(rows, rows, 0)],
+        )
+        sizes = [col_ways * (across - small), col_ways * small]
+        most, end, middle = along_lines(
+            "late1",
+            late_in,
+            first_mix,
+            1,
+            1,
+            [],
+            groups=col_ways,
+            outs=[(size, size, 0) for size in sizes],
+            held=[middle],
+        )
+        back = [parts, middle, most, end]
     else:
         (late,) = along_lines(
             "late0", late_in, first_mix, 0, rest, after, groups=col_ways, outs=[(rest * rows, rows, 0)]
@@ -542,8 +556,8 @@
     calls = [(0, chunk * rows, chunk, 0, across) for chunk in range(early_count)]
     if rest == 2:
         calls.append((1, 0, early_count, 0, across))
-        calls.append((1, rows, early_count + 1, 0, cut))
-        calls.append((2, 0, early_count + 1, cut, across - cut))
+        calls.append((2, 0, early_count + 1, 0, across - small))
+        calls.append((3, 0, early_count + 1, across - small, small))
     else:
         calls += [(1, at * rows, early_count + at, 0, across) for at in range(rest)]
     result, token = None, late_in if rest != 2 else end

time: 428 us -> 429 us (level)
    all_to_all x5 -> x6, waiting for transfers between devices: 90.8 us -> 86.7 us  [trade(): return lax.all_to_all(stack, 'row', split_axis=0, concat_axis=0)]
    all_to_all x5 -> x6, starting transfers between devices: 23.8 us -> 27.8 us  [trade(): return lax.all_to_all(stack, 'row', split_axis=0, concat_axis=0)]
  transfers between devices with their start and end apart: 11 -> 12, of which waited for: 6 -> 7; matrix products, arithmetic and copies ran while one was open for 2% -> 2% of each run, Pallas kernels for 52% -> 53%
where the time goes in v8:
time: 429 us; the launch traced here: 428 us
  Pallas kernels  241 us (56%)
  waiting for transfers between devices  145 us (34%)
  starting transfers between devices  34.8 us (8%)
  local copies, waits for them, and re-layouts  4.8 us (1%)
    all_to_all x6, waiting for transfers between devices, trade(): return lax.all_to_all(stack, 'row', split_axis=0, concat_axis=0)  86.7 us
    pallas_call x5, Pallas kernels, along_lines(): pl.pallas_call(lambda *refs: lines_kernel(ways, *refs[len(idle):last], *r...  85.8 us
    pallas_call x5, Pallas kernels, cells(): pl.pallas_call(functools.partial(cell_kernel, col_ways), grid_spec=pltpu....  82.6 us
    ppermute x6, waiting for transfers between devices, swap(): return lax.ppermute(piece, axis, [(at, at ^ step) for at in range(ways)])  57.8 us
    pallas_call x2, Pallas kernels, last_branch(): pl.pallas_call(lambda *refs: last_kernel(*refs[len(idle):len(idle) + 5],...  44.7 us
    all_to_all x6, starting transfers between devices, trade(): return lax.all_to_all(stack, 'row', split_axis=0, concat_axis=0)  27.8 us
    pallas_call x2, Pallas kernels, pack(): pl.pallas_call(pack_kernel, grid=(count, channels // depth), in_specs=[pl...  14.7 us
  transfers between devices with their start and end apart: 12, of which 7 were waited for; matrix products, arithmetic and copies ran while one was open for 2% of the time, Pallas kernels for 53%

profile of v8, /device:TPU:0, one launch (start us, length us, event | category | flops | bytes accessed | tf_op | source)
XLA Modules:
  0.0 428.0 jit_solution(17851605999288494720)
XLA Ops:
  0.0 7.4 %pack_columns.2.refs_4_ = bf16[8,2,64,16,128]{4,3,2,1,0:T(8,128)(2,1)} custom-call(bf16[64,16,32,128]{3,2,1,0:T(8,128)(2,1)} %x_ref.13), custom_call_target="tpu_custom_call" | custom-call | flops 9200000000 | tf_op jit(solution)/shard_map/pack_columns/pallas_call | solution.py:132
  7.4 6.3 %all-to-all-start = ((bf16[8,2,64,16,128]{4,3,2,1,0:T(8,128)(2,1)}), bf16[8,2,64,16,128]{4,3,2,1,0:T(8,128)(2,1)}, u32[]{:S(2)}, u32[]{:S(2)}) async-start(bf16[8,2,64,16,128]{4,3,2,1,0:T(8,128)(2,1)} %pack_columns.2.refs_4_), calls=%async_computation | async-start | bytes 8388608 | tf_op jit(solution)/shard_map/all_to_all | solution.py:485
  14.3 7.7 %rows_first.1 = (bf16[4,64,32,128]{3,2,1,0:T(8,128)(2,1)}, bf16[4,64,32,128]{3,2,1,0:T(8,128)(2,1)}, bf16[4,64,32,128]{3,2,1,0:T(8,128)(2,1)}, bf16[4,64,32,128]{3,2,1,0:T(8,128)(2,1)}) custom-call(s32[2]{0:T(128)} %pad_add_fusion.me_ref, bf16[64,16,32,128]{3,2,1,0:T(8,128)(2,1)} %x_ref.13, bf16[64,16,32,128]{3,2,1,0:T(8,128)(2,1)} %x_ref.13, ...), custom_call_target="tpu_custom_call" | custom-call | flops 8739999744 | tf_op jit(solution)/shard_map/rows_first/pallas_call | solution.py:160
  23.5 1.5 collective-permute-start.1
  30.7 5.0 %mixing_matrices.1 = (bf16[32,128,128]{2,1,0:T(8,128)(2,1)}, bf16[32,128,128]{2,1,0:T(8,128)(2,1)}, bf16[32,128,128]{2,1,0:T(8,128)(2,1)}) custom-call(bf16[4,64,32,128]{3,2,1,0:T(8,128)(2,1)} %get-tuple-element.26._.refs_4_.refs_8_, bf16[2,32,64,64]{3,2,1,0:T(8,128)(2,1)} %refs_0_.3, bf16[2,32,64,64]{3,2,1,0:T(8,128)(2,1)} %refs_1_.3, ...), custom_call_target="tpu_custom_call" | custom-call | flops 5750000128 | tf_op jit(solution)/shard_map/mixing_matrices/pallas_call | solution.py:68
  35.6 22.3 %last_branch.2.refs_0_ = bf16[16,32,64,128]{3,2,1,0:T(8,128)(2,1)} custom-call(bf16[64,128]{1,0:T(8,128)(2,1)} %pad_maximum_fusion.1.refs_0_.refs_1_.refs_4_, bf16[64,128]{1,0:T(8,128)(2,1)} %get-tuple-element.46.refs_1_.refs_2_, bf16[32,128,128]{2,1,0:T(8,128)(2,1)} %get-tuple-element.27.refs_2_.refs_3_, bf16[64,16,32,128]{3,2,1,0:T(8,128)(2,1)} %x_ref.13), custom_call_target="tpu_custom_call" | custom-call | flops 25300000768 | tf_op jit(solution)/shard_map/last_branch/pallas_call | solution.py:355
  57.9 22.4 %last_branch.3.refs_0_.refs_5_ = bf16[16,32,64,128]{3,2,1,0:T(8,128)(2,1)} custom-call(bf16[16,32,64,128]{3,2,1,0:T(8,128)(2,1)} %last_branch.2.refs_0_, bf16[64,128]{1,0:T(8,128)(2,1)} %pad_maximum_fusion.1.refs_0_.refs_1_.refs_4_, bf16[64,128]{1,0:T(8,128)(2,1)} %get-tuple-element.46.refs_1_.refs_2_, ...), custom_call_target="tpu_custom_call", output_to_operand_aliasing={{}: (0, {})} | custom-call | flops 25300000768 | tf_op jit(solution)/shard_map/last_branch/pallas_call | solution.py:355
  80.3 7.4 %pack_columns.3 = bf16[8,2,64,16,128]{4,3,2,1,0:T(8,128)(2,1)} custom-call(bf16[64,16,32,128]{3,2,1,0:T(8,128)(2,1)} %x_ref.13, bf16[16,32,64,128]{3,2,1,0:T(8,128)(2,1)} %last_branch.3.refs_0_.refs_5_), custom_call_target="tpu_custom_call" | custom-call | flops 9200000000 | tf_op jit(solution)/shard_map/pack_columns/pallas_call | solution.py:132
  87.7 20.1 %all-to-all-done.refs_4_ = bf16[8,2,64,16,128]{4,3,2,1,0:T(8,128)(2,1)} async-done(((bf16[8,2,64,16,128]{4,3,2,1,0:T(8,128)(2,1)}), bf16[8,2,64,16,128]{4,3,2,1,0:T(8,128)(2,1)}, u32[]{:S(2)}, u32[]{:S(2)}) %all-to-all-start) | async-done | bytes 4194336 | tf_op jit(solution)/shard_map/all_to_all | solution.py:485
  107.8 4.6 %all-to-all-start.1 = ((bf16[8,2,64,16,128]{4,3,2,1,0:T(8,128)(2,1)}), bf16[8,2,64,16,128]{4,3,2,1,0:T(8,128)(2,1)}, u32[]{:S(2)}, u32[]{:S(2)}) async-start(bf16[8,2,64,16,128]{4,3,2,1,0:T(8,128)(2,1)} %pack_columns.3), calls=%async_computation.1 | async-start | bytes 8388608 | tf_op jit(solution)/shard_map/all_to_all | solution.py:485
  112.4 20.6 %line_branch.5.refs_0_.refs_4_ = bf16[8,32,64,128]{3,2,1,0:T(8,128)(2,1)} custom-call(bf16[16,32,64,128]{3,2,1,0:T(8,128)(2,1)} %last_branch.3.refs_0_.refs_5_, bf16[64,128]{1,0:T(8,128)(2,1)} %pad_maximum_fusion.1.refs_0_.refs_1_.refs_4_, bf16[128,64]{1,0:T(8,128)(2,1)} %bitcast.35, bf16[32,128,128]{2,1,0:T(8,128)(2,1)} %get-tuple-element.28.refs_3_.refs_6_, ...), custom_call_target="tpu_custom_call" | custom-call | flops 23000000512 | tf_op jit(solution)/shard_map/line_branch/pallas_call | solution.py:293
  132.9 20.7 %line_branch.6 = (bf16[4,32,64,128]{3,2,1,0:T(8,128)(2,1)}, bf16[4,32,64,128]{3,2,1,0:T(8,128)(2,1)}, bf16[4,32,64,128]{3,2,1,0:T(8,128)(2,1)}, bf16[4,32,64,128]{3,2,1,0:T(8,128)(2,1)}) custom-call(bf16[8,32,64,128]{3,2,1,0:T(8,128)(2,1)} %line_branch.5.refs_0_.refs_4_, bf16[64,128]{1,0:T(8,128)(2,1)} %copy.32.refs_1_.refs_5_, bf16[128,64]{1,0:T(8,128)(2,1)} %bitcast.38, ...), custom_call_target="tpu_custom_call" | custom-call | flops 23000000512 | tf_op jit(solution)/shard_map/line_branch/pallas_call | solution.py:293
  153.6 20.7 %line_branch.7 = (bf16[4,32,64,128]{3,2,1,0:T(8,128)(2,1)}, bf16[4,32,64,128]{3,2,1,0:T(8,128)(2,1)}, bf16[4,32,64,128]{3,2,1,0:T(8,128)(2,1)}, bf16[4,32,64,128]{3,2,1,0:T(8,128)(2,1)}, bf16[8,32,64,128]{3,2,1,0:T(8,128)(2,1)}) custom-call(bf16[4,32,64,128]{3,2,1,0:T(8,128)(2,1)} %get-tuple-elem, ...), custom_call_target="tpu_custom_call", output_to_operand_aliasing={{0}: (0, {}), {1}: (1, {}), {2}: (2, {}), {3}: (3, {}), {4}... | custom-call | flops 23000000512 | tf_op jit(solution)/shard_map/line_branch/pallas_call | solution.py:293
  174.3 1.5 collective-permute-start.3
  175.8 1.5 collective-permute-start.4
  177.8 28.5 %all-to-all-done.1.refs_7_.refs_4_ = bf16[8,2,64,16,128]{4,3,2,1,0:T(8,128)(2,1)} async-done(((bf16[8,2,64,16,128]{4,3,2,1,0:T(8,128)(2,1)}), bf16[8,2,64,16,128]{4,3,2,1,0:T(8,128)(2,1)}, u32[]{:S(2)}, u32[]{:S(2)}) %all-to-all-start.1) | async-done | bytes 4194336 | tf_op jit(solution)/shard_map/all_to_all | solution.py:485
  206.4 4.5 %all-to-all-start.5 = ((bf16[8,32,64,128]{3,2,1,0:T(8,128)(2,1)}), bf16[8,32,64,128]{3,2,1,0:T(8,128)(2,1)}, u32[]{:S(2)}, u32[]{:S(2)}) async-start(bf16[8,32,64,128]{3,2,1,0:T(8,128)(2,1)} %get-tuple-element.44), calls=%async_computation.5 | async-start | bytes 8388608 | tf_op jit(solution)/shard_map/all_to_all | solution.py:485
  210.9 12.2 %collective-permute-done.3.refs_1_.refs_2_ = bf16[4,32,64,128]{3,2,1,0:T(8,128)(2,1)} collective-permute-done((bf16[4,32,64,128]{3,2,1,0:T(8,128)(2,1)}, bf16[4,32,64,128]{3,2,1,0:T(8,128)(2,1)}, u32[]{:S(2)}, u32[]{:S(2)}) %collective-permute-start.3) | collective-permute-done | bytes 2097184 | tf_op jit(solution)/shard_map/ppermute | solution.py:477
  223.1 45.6 %collective-permute-done.4.refs_2_.refs_3_ = bf16[4,32,64,128]{3,2,1,0:T(8,128)(2,1)} collective-permute-done((bf16[4,32,64,128]{3,2,1,0:T(8,128)(2,1)}, bf16[4,32,64,128]{3,2,1,0:T(8,128)(2,1)}, u32[]{:S(2)}, u32[]{:S(2)}) %collective-permute-start.4) | collective-permute-done | bytes 2097184 | tf_op jit(solution)/shard_map/ppermute | solution.py:477
  268.7 11.9 %line_branch.8.refs_0_ = bf16[8,16,64,128]{3,2,1,0:T(8,128)(2,1)} custom-call(bf16[4,32,64,128]{3,2,1,0:T(8,128)(2,1)} %get-tuple-element.37.refs_0_.refs_1_, bf16[4,32,64,128]{3,2,1,0:T(8,128)(2,1)} %collective-permute-done.3.refs_1_.refs_2_, bf16[4,32,64,128]{3,2,1,0:T(8,128)(2,1)} %collective-permute-done.4.refs_2_.refs_3_, ...), custom_call_target="tpu_custom_call" | custom-call | flops 230000001024 | tf_op jit(solution)/shard_map/line_branch/pallas_call | solution.py:293
  280.6 12.0 %line_branch.9 = (bf16[8,12,64,128]{3,2,1,0:T(8,128)(2,1)}, bf16[8,4,64,128]{3,2,1,0:T(8,128)(2,1)}, bf16[8,16,64,128]{3,2,1,0:T(8,128)(2,1)}) custom-call(bf16[8,16,64,128]{3,2,1,0:T(8,128)(2,1)} %line_branch.8.refs_0_, bf16[64,128]{1,0:T(8,128)(2,1)} %pad_maximum_fusion.1.refs_0_.refs_1_.refs_4_, ...), custom_call_target="tpu_custom_call", output_to_operand_aliasing={{2}: (0, {})} | custom-call | flops 11500000256 | tf_op jit(solution)/shard_map/line_branch/pallas_call | solution.py:293
  292.6 12.3 %all-to-all-done.5 = bf16[8,32,64,128]{3,2,1,0:T(8,128)(2,1)} async-done(((bf16[8,32,64,128]{3,2,1,0:T(8,128)(2,1)}), bf16[8,32,64,128]{3,2,1,0:T(8,128)(2,1)}, u32[]{:S(2)}, u32[]{:S(2)}) %all-to-all-start.5) | async-done | bytes 4194336 | tf_op jit(solution)/shard_map/all_to_all | solution.py:485
  304.9 4.7 %all-to-all-start.4 = ((bf16[8,16,64,128]{3,2,1,0:T(8,128)(2,1)}), bf16[8,16,64,128]{3,2,1,0:T(8,128)(2,1)}, u32[]{:S(2)}, u32[]{:S(2)}) async-start(bf16[8,16,64,128]{3,2,1,0:T(8,128)(2,1)} %get-tuple-element.43), calls=%async_computation.4 | async-start | bytes 4194304 | tf_op jit(solution)/shard_map/all_to_all | solution.py:485
  311.9 19.5 %feed_forward.5.refs_6_ = bf16[64,16,32,128]{3,2,1,0:T(8,128)(2,1)} custom-call(s32[2]{0:T(128)} %pad_add_fusion.me_ref, bf16[64,16,32,128]{3,2,1,0:T(8,128)(2,1)} %x_ref.13, bf16[256,64]{1,0:T(8,128)(2,1)} %bitcast.22, bf16[64,256]{1,0:T(8,128)(2,1)} %bitcast.29, f32[256,1]{1,0:T(8,128)} %copy.42.bin_ref, f32[64,1]{1,0:T(8,128)} %copy.43.bout_ref, ...), custom_call_target="tpu_custom_call" | custom-call | flops 2300000000 | tf_op jit(solution)/shard_map/feed_forward/pallas_call | solution.py:455
  331.4 19.5 %feed_forward.6.refs_6_ = bf16[64,16,32,128]{3,2,1,0:T(8,128)(2,1)} custom-call(s32[2]{0:T(128)} %pad_add_fusion.me_ref, bf16[64,16,32,128]{3,2,1,0:T(8,128)(2,1)} %x_ref.13, bf16[256,64]{1,0:T(8,128)(2,1)} %bitcast.23, bf16[64,256]{1,0:T(8,128)(2,1)} %bitcast.30, f32[256,1]{1,0:T(8,128)} %copy.42.bin_ref, ...), custom_call_target="tpu_custom_call", output_to_operand_aliasing={{}: (12, {})} | custom-call | flops 2300000000 | tf_op jit(solution)/shard_map/feed_forward/pallas_call | solution.py:455
  350.9 7.5 %all-to-all-done.4 = bf16[8,16,64,128]{3,2,1,0:T(8,128)(2,1)} async-done(((bf16[8,16,64,128]{3,2,1,0:T(8,128)(2,1)}), bf16[8,16,64,128]{3,2,1,0:T(8,128)(2,1)}, u32[]{:S(2)}, u32[]{:S(2)}) %all-to-all-start.4) | async-done | bytes 2097184 | tf_op jit(solution)/shard_map/all_to_all | solution.py:485
  358.5 3.6 all-to-all-start.3
  362.1 19.5 %feed_forward.7.refs_6_ = bf16[64,16,32,128]{3,2,1,0:T(8,128)(2,1)} custom-call(s32[2]{0:T(128)} %pad_add_fusion.me_ref, bf16[64,16,32,128]{3,2,1,0:T(8,128)(2,1)} %x_ref.13, bf16[256,64]{1,0:T(8,128)(2,1)} %bitcast.24, bf16[64,256]{1,0:T(8,128)(2,1)} %bitcast.31, f32[256,1]{1,0:T(8,128)} %copy.42.bin_ref, ...), custom_call_target="tpu_custom_call", output_to_operand_aliasing={{}: (12, {})} | custom-call | flops 69000003584 | tf_op jit(solution)/shard_map/feed_forward/pallas_call | solution.py:455
  381.6 18.2 %all-to-all-done.3 = bf16[8,12,64,128]{3,2,1,0:T(8,128)(2,1)S(1)} async-done(((bf16[8,12,64,128]{3,2,1,0:T(8,128)(2,1)}), bf16[8,12,64,128]{3,2,1,0:T(8,128)(2,1)S(1)}, u32[]{:S(2)}, u32[]{:S(2)}) %all-to-all-start.3) | async-done | bytes 1572896 | tf_op jit(solution)/shard_map/all_to_all | solution.py:485
  399.8 4.1 all-to-all-start.2
  404.0 16.9 %feed_forward.8.refs_6_ = bf16[64,16,32,128]{3,2,1,0:T(8,128)(2,1)} custom-call(s32[2]{0:T(128)} %pad_add_fusion.me_ref, bf16[64,16,32,128]{3,2,1,0:T(8,128)(2,1)} %x_ref.13, bf16[256,64]{1,0:T(8,128)(2,1)} %bitcast.25, bf16[64,256]{1,0:T(8,128)(2,1)} %bitcast.32, f32[256,1]{1,0:T(8,128)} %copy.42.bin_ref, ...), custom_call_target="tpu_custom_call", output_to_operand_aliasing={{}: (12, {})} | custom-call | flops 69000003584 | tf_op jit(solution)/shard_map/feed_forward/pallas_call | solution.py:455
  420.9 7.1 %feed_forward.9 = bf16[64,16,32,128]{3,2,1,0:T(8,128)(2,1)} custom-call(s32[2]{0:T(128)} %pad_add_fusion.me_ref, bf16[64,16,32,128]{3,2,1,0:T(8,128)(2,1)} %x_ref.13, bf16[256,64]{1,0:T(8,128)(2,1)} %bitcast.26, bf16[64,256]{1,0:T(8,128)(2,1)} %bitcast.33, f32[256,1]{1,0:T(8,128)} %copy.42.bin_ref, ...), custom_call_target="tpu_custom_call", output_to_operand_aliasing={{}: (12, {})} | custom-call | flops 12650000384 | tf_op jit(solution)/shard_map/feed_forward/pallas_call | solution.py:455
  (40 shorter events, 10.5 us)
Async XLA Ops:
  7.4 100.4 %all-to-all-start = ((bf16[8,2,64,16,128]{4,3,2,1,0:T(8,128)(2,1)}), bf16[8,2,64,16,128]{4,3,2,1,0:T(8,128)(2,1)}, u32[]{:S(2)}, u32[]{:S(2)}) async-start(bf16[8,2,64,16,128]{4,3,2,1,0:T(8,128)(2,1)} %pack_columns.2.refs_4_), calls=%async_computation | async-start | bytes 8388608 | tf_op jit(solution)/shard_map/all_to_all | solution.py:485
  22.0 110.9 %collective-permute-start = (bf16[4,64,32,128]{3,2,1,0:T(8,128)(2,1)}, bf16[4,64,32,128]{3,2,1,0:T(8,128)(2,1)}, u32[]{:S(2)}, u32[]{:S(2)}) collective-permute-start(bf16[4,64,32,128]{3,2,1,0:T(8,128)(2,1)} %get-tuple-element.30), channel_id=1, source_target_pairs={{0,1},{1,0},{2,3},{3,2},{4,5},{5,4},{6,7},{7,6},{8,9},{9,8},{10,11... | collective-permute-start | bytes 6291464 | tf_op jit(solution)/shard_map/ppermute | solution.py:477
  23.5 109.4 %collective-permute-start.1 = (bf16[4,64,32,128]{3,2,1,0:T(8,128)(2,1)}, bf16[4,64,32,128]{3,2,1,0:T(8,128)(2,1)}, u32[]{:S(2)}, u32[]{:S(2)}) collective-permute-start(bf16[4,64,32,128]{3,2,1,0:T(8,128)(2,1)} %get-tuple-element.31), channel_id=1, source_target_pairs={{0,2},{1,3},{2,0},{3,1},{4,6},{5,7},{6,4},{7,5},{8,10},{9,11},{10,... | collective-permute-start | bytes 6291464 | tf_op jit(solution)/shard_map/ppermute | solution.py:477
  25.0 107.9 %collective-permute-start.2 = (bf16[4,64,32,128]{3,2,1,0:T(8,128)(2,1)}, bf16[4,64,32,128]{3,2,1,0:T(8,128)(2,1)}, u32[]{:S(2)}, u32[]{:S(2)}) collective-permute-start(bf16[4,64,32,128]{3,2,1,0:T(8,128)(2,1)} %get-tuple-element.32), channel_id=1, source_target_pairs={{0,3},{1,2},{2,1},{3,0},{4,7},{5,6},{6,5},{7,4},{8,11},{9,10},{10,... | collective-permute-start | bytes 6291464 | tf_op jit(solution)/shard_map/ppermute | solution.py:477
  107.8 98.6 %all-to-all-start.1 = ((bf16[8,2,64,16,128]{4,3,2,1,0:T(8,128)(2,1)}), bf16[8,2,64,16,128]{4,3,2,1,0:T(8,128)(2,1)}, u32[]{:S(2)}, u32[]{:S(2)}) async-start(bf16[8,2,64,16,128]{4,3,2,1,0:T(8,128)(2,1)} %pack_columns.3), calls=%async_computation.1 | async-start | bytes 8388608 | tf_op jit(solution)/shard_map/all_to_all | solution.py:485
  174.3 48.8 %collective-permute-start.3 = (bf16[4,32,64,128]{3,2,1,0:T(8,128)(2,1)}, bf16[4,32,64,128]{3,2,1,0:T(8,128)(2,1)}, u32[]{:S(2)}, u32[]{:S(2)}) collective-permute-start(bf16[4,32,64,128]{3,2,1,0:T(8,128)(2,1)} %get-tuple-element.38), channel_id=1, source_target_pairs={{0,1},{1,0},{2,3},{3,2},{4,5},{5,4},{6,7},{7,6},{8,9},{9,8},{10,11... | collective-permute-start | bytes 6291464 | tf_op jit(solution)/shard_map/ppermute | solution.py:477
  175.8 92.9 %collective-permute-start.4 = (bf16[4,32,64,128]{3,2,1,0:T(8,128)(2,1)}, bf16[4,32,64,128]{3,2,1,0:T(8,128)(2,1)}, u32[]{:S(2)}, u32[]{:S(2)}) collective-permute-start(bf16[4,32,64,128]{3,2,1,0:T(8,128)(2,1)} %get-tuple-element.39), channel_id=1, source_target_pairs={{0,2},{1,3},{2,0},{3,1},{4,6},{5,7},{6,4},{7,5},{8,10},{9,11},{10,... | collective-permute-start | bytes 6291464 | tf_op jit(solution)/shard_map/ppermute | solution.py:477
  177.3 91.3 %collective-permute-start.5 = (bf16[4,32,64,128]{3,2,1,0:T(8,128)(2,1)}, bf16[4,32,64,128]{3,2,1,0:T(8,128)(2,1)}, u32[]{:S(2)}, u32[]{:S(2)}) collective-permute-start(bf16[4,32,64,128]{3,2,1,0:T(8,128)(2,1)} %get-tuple-element.40), channel_id=1, source_target_pairs={{0,3},{1,2},{2,1},{3,0},{4,7},{5,6},{6,5},{7,4},{8,11},{9,10},{10,... | collective-permute-start | bytes 6291464 | tf_op jit(solution)/shard_map/ppermute | solution.py:477
  206.4 98.6 %all-to-all-start.5 = ((bf16[8,32,64,128]{3,2,1,0:T(8,128)(2,1)}), bf16[8,32,64,128]{3,2,1,0:T(8,128)(2,1)}, u32[]{:S(2)}, u32[]{:S(2)}) async-start(bf16[8,32,64,128]{3,2,1,0:T(8,128)(2,1)} %get-tuple-element.44), calls=%async_computation.5 | async-start | bytes 8388608 | tf_op jit(solution)/shard_map/all_to_all | solution.py:485
  304.9 4.7 %copy-start.2 = (f32[256]{0:T(256)S(1)}, f32[256]{0:T(256)}, u32[]{:S(2)}) copy-start(f32[256]{0:T(256)} %param.18) | copy-start | bytes 3076
  304.9 5.5 %copy-start.1 = (bf16[64,256]{1,0:T(8,128)(2,1)S(1)}, bf16[64,256]{1,0:T(8,128)(2,1)}, u32[]{:S(2)}) copy-start(bf16[64,256]{1,0:T(8,128)(2,1)} %param.16) | copy-start | bytes 98308
  304.9 6.2 %copy-start.3 = (f32[64]{0:T(128)S(1)}, f32[64]{0:T(128)}, u32[]{:S(2)}) copy-start(f32[64]{0:T(128)} %param.19) | copy-start | bytes 772
  304.9 53.6 %all-to-all-start.4 = ((bf16[8,16,64,128]{3,2,1,0:T(8,128)(2,1)}), bf16[8,16,64,128]{3,2,1,0:T(8,128)(2,1)}, u32[]{:S(2)}, u32[]{:S(2)}) async-start(bf16[8,16,64,128]{3,2,1,0:T(8,128)(2,1)} %get-tuple-element.43), calls=%async_computation.4 | async-start | bytes 4194304 | tf_op jit(solution)/shard_map/all_to_all | solution.py:485
  358.5 41.3 %all-to-all-start.3 = ((bf16[8,12,64,128]{3,2,1,0:T(8,128)(2,1)}), bf16[8,12,64,128]{3,2,1,0:T(8,128)(2,1)S(1)}, u32[]{:S(2)}, u32[]{:S(2)}) async-start(bf16[8,12,64,128]{3,2,1,0:T(8,128)(2,1)} %get-tuple-element.42), calls=%async_computation.3 | async-start | bytes 3145728 | tf_op jit(solution)/shard_map/all_to_all | solution.py:485
  399.8 4.2 copy-start
  399.8 21.1 %all-to-all-start.2 = ((bf16[8,4,64,128]{3,2,1,0:T(8,128)(2,1)}), bf16[8,4,64,128]{3,2,1,0:T(8,128)(2,1)}, u32[]{:S(2)}, u32[]{:S(2)}) async-start(bf16[8,4,64,128]{3,2,1,0:T(8,128)(2,1)} %get-tuple-element.41.refs_6_), calls=%async_computation.2 | async-start | bytes 1048576 | tf_op jit(solution)/shard_map/all_to_all | solution.py:485
